TPU v7x, 32 devices: a whole 2x2x4 slice. The times are simulated.
32 devices in a mesh: dp: 16 (over z, y, x), seq: 2 (over core).
Axes of the slice: x: 2, y: 2, z: 4, core: 2. Of those that a mesh axis runs over, the one named last changes fastest.
Arguments:
- block_input: bfloat16 [16, 2048, 512], P('dp', 'seq'), may hold values from -6 to 6
- mixer_gain: bfloat16 [512], P(('dp', 'seq')), may hold values from 0.099609375 to 1.8984375
- mixer_bias: bfloat16 [512], P(('dp', 'seq')), may hold values from -3 to 3
- in_proj: bfloat16 [512, 512], P(('dp', 'seq')), may hold values from -0.25 to 0.25
- kernel_param: bfloat16 [512, 192], P(('dp', 'seq')), may hold values from -6 to 6
- skip_gain: bfloat16 [512], P(('dp', 'seq')), may hold values from -4 to 4
- out_proj: bfloat16 [512, 512], P(('dp', 'seq')), may hold values from -0.25 to 0.25
- mlp_gain: bfloat16 [512], P(('dp', 'seq')), may hold values from 0.099609375 to 1.8984375
- mlp_bias: bfloat16 [512], P(('dp', 'seq')), may hold values from -3 to 3
- up_proj: bfloat16 [512, 2048], P(('dp', 'seq')), may hold values from -0.25 to 0.25
- down_proj: bfloat16 [512, 2048], P(('dp', 'seq')), may hold values from -0.125 to 0.125
- out_cotangent: bfloat16 [16, 2048, 512], P('dp', 'seq'), may hold values from -6 to 6
Outputs:
- block_output: bfloat16 [16, 2048, 512], P('dp', 'seq')
- input_grad: float32 [16, 2048, 512], P('dp', 'seq')
- mixer_gain_grad: float32 [512], P(('dp', 'seq'))
- mixer_bias_grad: float32 [512], P(('dp', 'seq'))
- in_proj_grad: float32 [512, 512], P(('dp', 'seq'))
- kernel_param_grad: float32 [512, 192], P(('dp', 'seq'))
- skip_gain_grad: float32 [512], P(('dp', 'seq'))
- out_proj_grad: float32 [512, 512], P(('dp', 'seq'))
- mlp_gain_grad: float32 [512], P(('dp', 'seq'))
- mlp_bias_grad: float32 [512], P(('dp', 'seq'))
- up_proj_grad: float32 [512, 2048], P(('dp', 'seq'))
- down_proj_grad: float32 [512, 2048], P(('dp', 'seq'))
All inputs are finite; a program needn't handle non-finite values.
Results may differ from a plain program's by a relative error of at most 0.014.
Values may be sent and summed in bfloat16 or wider, within the bound.
No kernel may reach another device: no remote copies, remote signals or barrier semaphores. Data moves between devices by JAX's collectives and lax.ppermute only.
A program may use at most 128 MiB of HBM per device.

v0:
```python
import math

import jax
import jax.numpy as jnp
import numpy as np
from jax import lax
from jax.experimental import pallas as pl
from jax.experimental.pallas import tpu as pltpu
from jax.sharding import PartitionSpec as P

TAPS = 32
SCALES = 6
FINE = 3
FREQ = 256
HALF = FREQ // 2
BLOCK = 256
POOL = 8
OFFSET = 28
TILE = 512
WIDE = 512
PACK = 768
F32 = jnp.float32
BF16 = jnp.bfloat16
NT = ((1,), (1,))
TN = ((0,), (0,))


def odd_basis(positions):
    order = np.concatenate([np.arange(0, FREQ, 2), np.arange(1, FREQ, 2)])
    angle = np.pi * np.outer(order + 0.5, positions) / FREQ
    return np.concatenate([np.cos(angle), -np.sin(angle)], axis=0)


def tap_basis(start, first):
    columns = np.zeros((2 * FREQ, 256))
    for scale_at in range(FINE):
        wide = 2**scale_at
        lag = start + TAPS * (wide - 1)
        for tap in range(TAPS):
            at = first + scale_at * TAPS + tap
            columns[:, at] = odd_basis(lag + tap * wide + np.arange(wide)).sum(axis=1)
    return columns


def bf16_const(array):
    return jnp.asarray(np.asarray(array, np.float32).astype(jnp.bfloat16))


def dot(a, b, contract=((1,), (0,))):
    return lax.dot_general(a, b, (contract, ((), ())), preferred_element_type=F32)


def normal_parts(values):
    cdf = 0.5 + 0.5 * lax.erf(values * np.float32(math.sqrt(0.5)))
    pdf = jnp.exp(-0.5 * values * values) * np.float32(1 / math.sqrt(2 * math.pi))
    return cdf, pdf


def split_dp(count):
    edge = round((count / 2) ** (1 / 3))
    return (2 * edge, edge * edge) if 2 * edge**3 == count else (1, count)


def swap_route(count, mask):
    return [(i, i ^ mask) for i in range(count)]


SWAP = [(0, 1), (1, 0)]


def tie(value, *others):
    return lax.optimization_barrier((value, *others))[0]


def far_steps():
    nz, _ = split_dp(lax.axis_size("dp"))
    return [1 << bit for bit in reversed(range(nz.bit_length() - 1))]


def from_line(held, step):
    dp_count = lax.axis_size("dp")
    _, nxy = split_dp(dp_count)
    return lax.ppermute(held, "dp", swap_route(dp_count, step * nxy))


def paired(held, got):
    return jnp.stack([held, got], axis=1).reshape((-1,) + held.shape[1:])


def gather_line(held, step):
    return paired(held, from_line(held, step))


def gather_far(shard):
    held = shard[None]
    for step in far_steps():
        held = gather_line(held, step)
    return held


def gather_near(held):
    dp_count = lax.axis_size("dp")
    _, nxy = split_dp(dp_count)
    return [held] + [lax.ppermute(held, "dp", swap_route(dp_count, k)) for k in range(1, nxy)]


def gather_core(pieces):
    held = jnp.concatenate(pieces)
    return [held, lax.ppermute(held, "seq", SWAP)]


def gather_plane(held):
    dp_count = lax.axis_size("dp")
    _, nxy = split_dp(dp_count)
    if nxy != 4:
        return gather_near(held)
    by_x = lax.ppermute(held, "dp", swap_route(dp_count, 1))
    by_y = lax.ppermute(held, "dp", swap_route(dp_count, 2))
    if held.shape[0] == 1:
        return [held, by_x, by_y, lax.ppermute(by_y, "dp", swap_route(dp_count, 1))]
    cut = held.shape[0] // 2
    return [
        held, by_x, by_y, lax.ppermute(by_y[:cut], "dp", swap_route(dp_count, 1)),
        lax.ppermute(by_x[cut:], "dp", swap_route(dp_count, 2)),
    ]


def row_place(at, count, plane_first, core_ref):
    nz, nxy = split_dp(count)
    other, at = divmod(at, count)
    if plane_first:
        z, xy = divmod(at, nxy)
    else:
        xy, z = divmod(at, nz)
    return ((z * nxy + xy) ^ core_ref[1]) * 2 + (other ^ core_ref[0])


def in_order(pieces, plane_first):
    if pieces[0].shape[1] % 16 == 0:
        return pieces
    dp_count = lax.axis_size("dp")
    nz, nxy = split_dp(dp_count)
    me, core = lax.axis_index("dp"), lax.axis_index("seq")
    by_dp = jnp.arange(dp_count).reshape(nz, nxy) ^ me
    by_dp = by_dp if plane_first else by_dp.T
    where = by_dp[None] * 2 + (jnp.arange(2)[:, None, None] ^ core)
    flat = jnp.concatenate(pieces)
    return [jnp.take(flat, jnp.argsort(where.reshape(-1)), axis=0).reshape(1, -1, flat.shape[2])]


def reduce_core(grads, *before):
    dp_count = lax.axis_size("dp")
    nz, nxy = split_dp(dp_count)
    if len(grads) == 1:
        core, me = lax.axis_index("seq"), lax.axis_index("dp")
        shaped = grads[0].reshape(dp_count, 2, -1, grads[0].shape[1])
        order = (jnp.arange(nz)[None, :] * nxy + jnp.arange(nxy)[:, None]) ^ me
        shaped = jnp.take(shaped, order.reshape(-1), axis=0)
        grads = [
            lax.dynamic_index_in_dim(shaped, 1 - core, 1, False),
            lax.dynamic_index_in_dim(shaped, core, 1, False),
        ]
    send, keep = grads
    got = lax.ppermute(send, "seq", SWAP)
    got = tie(got, *before)
    total = (keep.astype(F32) + got.astype(F32)).astype(BF16)
    return [total[k * nz : (k + 1) * nz] for k in range(nxy)]


def spread_near(pieces):
    dp_count = lax.axis_size("dp")
    return [pieces[0]] + [
        lax.ppermute(pieces[k], "dp", swap_route(dp_count, k)) for k in range(1, len(pieces))
    ]


def spread_far(part):
    dp_count = lax.axis_size("dp")
    nz, nxy = split_dp(dp_count)
    return [part[0]] + [
        lax.ppermute(part[k], "dp", swap_route(dp_count, k * nxy)) for k in range(1, nz)
    ]


def add_up(pieces, dtype=F32):
    total = pieces[0].astype(F32)
    for piece in pieces[1:]:
        total = total + piece.astype(F32)
    return total.astype(dtype)


def load_rows(core_ref, pieces, target, plane_first):
    if len(pieces) == 1:
        target[...] = pieces[0][0]
        return
    count = target.shape[0] // (2 * pieces[0].shape[1])
    at = 0
    for piece in pieces:
        held, rows, _ = piece.shape
        for i in range(held):
            start = row_place(at, count, plane_first, core_ref) * rows
            target[pl.ds(pl.multiple_of(start, 16), rows), :] = piece[i]
            at += 1


def span(at, size=BLOCK):
    return pl.ds(at * size, size)


def norm_stats(features):
    centre = features - jnp.mean(features, axis=-1, keepdims=True)
    inverse = lax.rsqrt(jnp.mean(centre * centre, axis=-1, keepdims=True) + 1e-05)
    return centre * inverse, inverse


def norm_back(xhat, inverse, scaled):
    return inverse * (
        scaled
        - jnp.mean(scaled, axis=-1, keepdims=True)
        - xhat * jnp.mean(scaled * xhat, axis=-1, keepdims=True)
    )


def quarters(spectrum):
    return [spectrum[i * HALF : (i + 1) * HALF].astype(F32) for i in range(4)]


def add_before(now, past):
    (re, ro, ie, io), (pre, pro, pie, pio) = now, past
    return re - pie, ro + pio, ie + pre, io - pro


def add_after(now, later):
    (re, ro, ie, io), (nre, nro, nie, nio) = now, later
    return re + nie, ro - nio, ie - nre, io + nro


def product(a, b):
    (are, aro, aie, aio), (bre, bro, bie, bio) = a, b
    return (
        are * bre - aie * bie,
        aro * bro - aio * bio,
        are * bie + aie * bre,
        aro * bio + aio * bro,
    )


def conj_product(a, b):
    (are, aro, aie, aio), (bre, bro, bie, bio) = a, b
    return (
        are * bre + aie * bie,
        aro * bro + aio * bio,
        are * bie - aie * bre,
        aro * bio - aio * bro,
    )


def stacked(parts):
    return jnp.concatenate([part.astype(BF16) for part in parts], axis=0)


def put_quarters(ref, at, parts):
    for i, part in enumerate(parts):
        ref[at, i * HALF : (i + 1) * HALF, :] = part.astype(ref.dtype)


def pack_kernel(core_ref, in_ref, param_ref, out_ref, up_ref, down_ref, *rest):
    vectors, (a_ref, b_ref, param, small, sem) = rest[:5], rest[5:]
    rows, feats = in_ref.shape
    half = up_ref.shape[1] // 2
    copies = [
        pltpu.make_async_copy(in_ref, a_ref.at[:, pl.ds(0, feats)], sem),
        pltpu.make_async_copy(param_ref, param, sem),
    ]
    for i, vector in enumerate(vectors):
        copies.append(pltpu.make_async_copy(vector, small.at[i], sem))
    for source, start, size, target, at in (
        (out_ref, 0, feats, a_ref, PACK), (up_ref, 0, half, a_ref, PACK + feats),
        (down_ref, 0, half, a_ref, PACK + feats + half), (up_ref, half, half, b_ref, 0),
        (down_ref, half, half, b_ref, half),
    ):
        copies.append(
            pltpu.make_async_copy(
                source.at[:, pl.ds(start, size)], target.at[:, pl.ds(at, size)], sem
            )
        )
    for copy in copies:
        copy.start()
    for copy in copies:
        copy.wait()
    spare = PACK - feats - param.shape[1]
    row = lax.broadcasted_iota(jnp.int32, (rows, rows), 0)
    lane = lax.broadcasted_iota(jnp.int32, (rows, rows), 1)
    slot = lax.broadcasted_iota(jnp.int32, (rows, spare), 1)
    block = jnp.zeros((rows, spare), F32)
    for i in range(len(vectors)):
        value = small[i].astype(F32)
        column = jnp.sum(jnp.where(row == lane, value, 0.0), axis=1, keepdims=True)
        block = jnp.where(slot == i, column, block)
    tail = jnp.concatenate([param[...].astype(F32), block], axis=1)
    a_ref[:, feats:PACK] = tail.astype(BF16)


def prepare_kernel(x_ref, cot_ref, xhat_ref, inv_ref, cot_t_ref, cot_copy, x_copy, sem):
    blocks = x_ref.shape[0] // BLOCK
    copies = []
    for source, target, which in ((x_ref, x_copy, 0), (cot_ref, cot_copy, 1)):
        for at in range(blocks):
            copies.append(
                pltpu.make_async_copy(source.at[span(at), :], target.at[span(at), :], sem.at[which, at])
            )
    for copy in copies:
        copy.start()
    for at in range(blocks):
        copies[at].wait()
        xhat, inverse = norm_stats(x_copy[span(at), :].astype(F32))
        xhat_ref[span(at), :] = xhat.astype(BF16)
        inv_ref[span(at), :] = jnp.broadcast_to(inverse, (BLOCK, 128))
    for at in range(blocks):
        copies[blocks + at].wait()
        cot_t_ref[:, span(at)] = cot_copy[span(at), :].T


def prior_kernel(x_ref, xhat_ref):
    for at in range(x_ref.shape[0] // BLOCK):
        xhat_ref[span(at), :] = norm_stats(x_ref[span(at), :].astype(F32))[0].astype(BF16)


def forward_kernel(
    n_pieces, core_ref, xhat_ref, prior_ref, basis, basis_t, basis_pool, back_pool,
    fine_basis, coarse_basis, pool_rows, scale_ref, wide_ref, *rest,
):
    pieces, rest = rest[:n_pieces], rest[n_pieces:]
    weights, vec_ref, fine_h_ref, coarse_h_ref, win_ref, pool_win_ref, act_ref, slope_ref = rest[:8]
    mixed_ref, pooled_ref = rest[8:]
    load_rows(core_ref, pieces, weights, False)
    feats = xhat_ref.shape[1]
    blocks = xhat_ref.shape[0] // BLOCK
    tail = weights[:, feats : feats + 256].astype(F32)
    raw = tail * scale_ref[...]
    inverse = lax.rsqrt(jnp.sum(raw * raw * wide_ref[...], axis=1, keepdims=True) + 1e-05)
    taps = (raw * inverse).astype(BF16)
    vec = tail[:, 128:256].T[64:72]
    vec_ref[...] = vec
    gain, bias, skip = vec[0:1], vec[1:2], vec[2:3]
    fine_h = dot(fine_basis[...], taps, NT)
    coarse_h = dot(coarse_basis[...], taps, NT)
    fine_h_ref[...] = fine_h.astype(BF16)
    coarse_h_ref[...] = coarse_h.astype(BF16)
    proj = weights[:, :feats]
    has_prior = core_ref[0].astype(F32)
    per = BLOCK // POOL
    past = None
    for at in range(blocks):
        normed = (prior_ref[span(at), :].astype(F32) * gain + bias).astype(BF16)
        mixed = (dot(normed, proj) * has_prior).astype(BF16)
        pooled_ref[span(at, per), :] = dot(pool_rows[...], mixed).astype(BF16)
        if at == blocks - 1:
            past = quarters(dot(basis[...], mixed))
    for at in range(blocks):
        normed = (xhat_ref[span(at), :].astype(F32) * gain + bias).astype(BF16)
        mixed = dot(normed, proj).astype(BF16)
        mixed_ref[span(at), :] = mixed
        pooled_ref[span(blocks + at, per), :] = dot(pool_rows[...], mixed).astype(BF16)
    pool_win = dot(basis_pool[...], pooled_ref[...])
    pool_win_ref[...] = pool_win.astype(BF16)
    coarse_y = stacked(product(quarters(coarse_h), quarters(pool_win)))
    fine_q = quarters(fine_h)
    for at in range(blocks):
        mixed = mixed_ref[span(at), :]
        now = quarters(dot(basis[...], mixed))
        window = add_before(now, past)
        past = now
        put_quarters(win_ref, at, window)
        total = dot(basis_t[...], stacked(product(fine_q, window)))
        total = total + dot(back_pool[span(at), :], coarse_y)
        pre_act = total * np.float32(1 / FREQ) + skip * mixed.astype(F32)
        cdf, pdf = normal_parts(pre_act)
        act_ref[span(at), :] = (pre_act * cdf).astype(BF16)
        slope_ref[span(at), :] = (cdf + pre_act * pdf).astype(BF16)


def place_of(core_ref, grad_refs):
    nz, nxy = split_dp(grad_refs[0].shape[0])
    return core_ref[0], core_ref[1] // nxy, core_ref[1] % nxy, nz, nxy


def put_rows(refs, columns, value, place):
    value = value.astype(BF16)
    if len(refs) == 1:
        refs[0][:, columns] = value
        return
    send_ref, keep_ref = refs
    count, rows, _ = send_ref.shape
    core, me_z, me_xy, nz, nxy = place
    for at in range(count):
        slot = ((at % nxy) ^ me_xy) * nz + ((at // nxy) ^ me_z)
        first = value[2 * at * rows : (2 * at + 1) * rows]
        second = value[(2 * at + 1) * rows : (2 * at + 2) * rows]
        send_ref[slot, :, columns] = jnp.where(core == 0, second, first)
        keep_ref[slot, :, columns] = jnp.where(core == 0, first, second)


def hidden_part(place, normed_ref, normed_t_ref, cot_ref, cot_t_ref, up_at, down_at, weights, hidden_ref, grad_up_ref, grad_refs):
    length = normed_ref.shape[0]
    count = hidden_ref.shape[1]
    for at in range(0, count, WIDE):
        columns = slice(at, at + WIDE)
        up = weights[:, up_at + at : up_at + at + WIDE]
        down = weights[:, down_at + at : down_at + at + WIDE]
        for row in range(0, length, TILE):
            rows = slice(row, row + TILE)
            up_val = dot(normed_ref[rows, :], up)
            grad_hidden = dot(cot_ref[rows, :], down)
            cdf, pdf = normal_parts(up_val)
            hidden_ref[rows, columns] = (up_val * cdf).astype(BF16)
            grad_up_ref[rows, columns] = (grad_hidden * (cdf + up_val * pdf)).astype(BF16)
        put_rows(grad_refs, slice(at, at + WIDE), dot(normed_t_ref[...], grad_up_ref[:, columns]), place)
        put_rows(grad_refs, slice(count + at, count + at + WIDE), dot(cot_t_ref[...], hidden_ref[:, columns]), place)


def middle_first_kernel(
    n_pieces, core_ref, act_ref, x_ref, cot_ref, cot_t_ref, vec_ref, *rest
):
    pieces, rest = rest[:n_pieces], rest[n_pieces:]
    (proj_ref, mid_ref, xhat_ref, inv_ref, normed_ref, normed_t_ref, hidden_ref, grad_up_ref), rest = rest[:8], rest[8:]
    weights, *grad_refs = rest
    load_rows(core_ref, pieces, weights, False)
    length, feats = x_ref.shape
    count = hidden_ref.shape[1]
    gain, bias = vec_ref[3:4, :], vec_ref[4:5, :]
    proj_ref[...] = weights[:, :feats]
    for at in range(length // BLOCK):
        mid = x_ref[span(at), :].astype(F32) + dot(act_ref[span(at), :], proj_ref[...])
        xhat, inverse = norm_stats(mid)
        normed = (xhat * gain + bias).astype(BF16)
        mid_ref[span(at), :] = mid
        xhat_ref[span(at), :] = xhat
        inv_ref[span(at), :] = jnp.broadcast_to(inverse, (BLOCK, 128))
        normed_ref[span(at), :] = normed
        normed_t_ref[:, span(at)] = normed.T
    hidden_part(
        place_of(core_ref, grad_refs), normed_ref, normed_t_ref, cot_ref, cot_t_ref, feats, feats + count,
        weights, hidden_ref, grad_up_ref, grad_refs,
    )


def middle_second_kernel(
    n_pieces, core_ref, cot_ref, cot_t_ref, normed_ref, normed_t_ref, *rest
):
    pieces, rest = rest[:n_pieces], rest[n_pieces:]
    hidden_ref, grad_up_ref, weights, *grad_refs = rest
    load_rows(core_ref, pieces, weights, True)
    hidden_part(
        place_of(core_ref, grad_refs), normed_ref, normed_t_ref, cot_ref, cot_t_ref, 0,
        hidden_ref.shape[1], weights, hidden_ref, grad_up_ref, grad_refs,
    )


def middle_third_kernel(
    slope_ref, cot_ref, vec_ref, pool_rows, proj_ref, xhat_ref, inv_ref, up_a_ref, up_b_ref, weights_a,
    weights_b, mid_grad_ref, vec_grad_ref, pre_grad_ref, halo_ref,
):
    length, feats = xhat_ref.shape
    count = up_a_ref.shape[1]
    gain = vec_ref[3:4, :]
    gain_grad = jnp.zeros((8, feats), F32)
    bias_grad = jnp.zeros((8, feats), F32)
    per = BLOCK // POOL
    for at in range(length // BLOCK):
        grad_normed = dot(up_a_ref[span(at), :], weights_a[:, feats : feats + count], NT)
        grad_normed = grad_normed + dot(up_b_ref[span(at), :], weights_b[:, :count], NT)
        xhat = xhat_ref[span(at), :]
        bias_grad = bias_grad + jnp.sum(grad_normed.reshape(BLOCK // 8, 8, feats), axis=0)
        gain_grad = gain_grad + jnp.sum((grad_normed * xhat).reshape(BLOCK // 8, 8, feats), axis=0)
        grad_mid = cot_ref[span(at), :].astype(F32) + norm_back(
            xhat, inv_ref[span(at), 0:1], grad_normed * gain
        )
        mid_grad_ref[span(at), :] = grad_mid
        grad_act = dot(grad_mid.astype(BF16), proj_ref[...], NT)
        grad_pre = (grad_act * slope_ref[span(at), :].astype(F32)).astype(BF16)
        pre_grad_ref[span(at), :] = grad_pre
        if at == 0:
            halo_ref[0:BLOCK, :] = grad_pre
        halo_ref[pl.ds(BLOCK + at * per, per), :] = (
            dot(pool_rows[...], grad_pre) * np.float32(POOL)
        ).astype(BF16)
    vec_grad_ref[0:1, :] = jnp.sum(gain_grad, axis=0, keepdims=True)
    vec_grad_ref[1:2, :] = jnp.sum(bias_grad, axis=0, keepdims=True)
    vec_grad_ref[2:8, :] = jnp.zeros((6, feats), F32)


def output_kernel(mid_ref, hidden_a_ref, hidden_b_ref, weights_a, weights_b, out_ref):
    length, feats = mid_ref.shape
    count = hidden_a_ref.shape[1]
    for at in range(length // BLOCK):
        total = mid_ref[span(at), :] + dot(hidden_a_ref[span(at), :], weights_a[:, feats + count :], NT)
        total = total + dot(hidden_b_ref[span(at), :], weights_b[:, count:], NT)
        out_ref[span(at), :] = total.astype(BF16)


def taps_kernel(
    act_ref, mid_grad_ref, pre_grad_ref, halo_ref, win_ref, pool_win_ref, basis, fine_basis,
    coarse_basis, out_grad_ref, tap_grad_ref, z_ref, mid_bf_ref,
):
    length, feats = act_ref.shape
    blocks = length // BLOCK
    total = None
    for at in range(blocks):
        mid_bf_ref[span(at), :] = mid_grad_ref[span(at), :].astype(BF16)
        z = dot(basis[...], pre_grad_ref[span(at), :])
        z_ref[at] = z.astype(BF16)
        term = conj_product(quarters(win_ref[at]), quarters(z))
        total = term if total is None else [a + b for a, b in zip(total, term)]
    out_grad_ref[...] = dot(act_ref[...], mid_bf_ref[...], TN).astype(BF16)
    pooled = length // POOL
    z_pool = dot(basis[:, 0:pooled], halo_ref[BLOCK : BLOCK + pooled, :])
    pool_term = conj_product(quarters(pool_win_ref[...]), quarters(z_pool))
    tap_grad_ref[...] = (
        (dot(stacked(total), fine_basis[...], TN) + dot(stacked(pool_term), coarse_basis[...], TN))
        * np.float32(1 / FREQ)
    ).astype(BF16)


def backward_kernel(
    core_ref, z_ref, halo_ref, next_ref, pre_grad_ref, fine_h_ref, coarse_h_ref, basis, basis_t, back_pool,
    weights, vec_ref, vec_grad_ref, xhat_ref, out_grad_ref, tap_grad_ref, mixed_grad_ref, *rest
):
    *grad_refs, pool_ref = rest
    place = place_of(core_ref, grad_refs)
    length, feats = xhat_ref.shape
    blocks = length // BLOCK
    pooled = length // POOL
    gain, bias, skip = vec_ref[0:1, :], vec_ref[1:2, :], vec_ref[2:3, :]
    fine_q = quarters(fine_h_ref[...])
    pool_ref[0:pooled, :] = halo_ref[BLOCK : BLOCK + pooled, :]
    pool_ref[pooled : 2 * pooled, :] = next_ref[BLOCK : BLOCK + pooled, :]
    z_pool = quarters(dot(basis[...], pool_ref[...]))
    coarse_y = stacked([v * np.float32(1 / POOL) for v in conj_product(quarters(coarse_h_ref[...]), z_pool)])
    later = quarters(dot(basis[...], next_ref[0:BLOCK, :]))
    sums = jnp.zeros((8, feats), F32)
    for at in reversed(range(blocks)):
        now = quarters(z_ref[at])
        y = stacked(conj_product(fine_q, add_after(now, later)))
        later = now
        total = dot(basis_t[...], y) + dot(back_pool[span(at), :], coarse_y)
        grad_mixed = (
            total * np.float32(1 / FREQ) + skip * pre_grad_ref[span(at), :].astype(F32)
        ).astype(BF16)
        mixed_grad_ref[span(at), :] = grad_mixed
        sums = sums + jnp.sum(grad_mixed.astype(F32).reshape(BLOCK // 8, 8, feats), axis=0)
    back = dot(xhat_ref[...], mixed_grad_ref[...], TN)
    mixed_sum = jnp.sum(sums, axis=0, keepdims=True)
    padded = jnp.concatenate([vec_ref[...], vec_grad_ref[...], jnp.zeros((112, feats), F32)], axis=0)
    columns = padded.T
    put_rows(grad_refs, slice(0, feats), columns[:, 0:1] * back + columns[:, 1:2] * mixed_sum, place)
    put_rows(grad_refs, slice(feats, 2 * feats), out_grad_ref[...], place)
    put_rows(grad_refs, slice(2 * feats, 2 * feats + 256), tap_grad_ref[...], place)
    proj = weights[:, 0:feats]
    proj_f = proj.astype(F32)
    gain_grad = jnp.sum(proj_f * back, axis=1, keepdims=True)
    bias_grad = jnp.sum(proj_f * mixed_sum, axis=1, keepdims=True)
    lane = lax.broadcasted_iota(jnp.int32, (feats, 128), 1)
    columns = jnp.where(lane == 0, gain_grad, jnp.where(lane == 1, bias_grad, columns))
    put_rows(grad_refs, slice(2 * feats + 256, 2 * feats + 384), columns, place)


def input_kernel(mixed_grad_ref, weights, vec_ref, xhat_ref, inv_ref, mid_grad_ref, input_grad_ref):
    length, feats = xhat_ref.shape
    proj = weights[:, 0:feats]
    for at in range(length // BLOCK):
        grad_normed = dot(mixed_grad_ref[span(at), :], proj, NT)
        input_grad_ref[span(at), :] = mid_grad_ref[span(at), :] + norm_back(
            xhat_ref[span(at), :].astype(F32), inv_ref[span(at), 0:1], grad_normed * vec_ref[0:1, :]
        )


def final_kernel(param_ref, scale_ref, wide_ref, *rest):
    sources, outs = rest[: len(rest) - 10], rest[len(rest) - 10 :]
    count = len(sources) // 2
    up_ref, down_ref, in_ref, out_ref, param_grad_ref = outs[:5]
    totals = []
    for group in range(2):
        total = sources[group * count][...].astype(F32)
        for k in range(1, count):
            total = total + sources[group * count + k][...].astype(F32)
        totals.append(total)
    mlp, mixer = totals
    half = mlp.shape[1] // 4
    up_ref[:, :half], up_ref[:, half:] = mlp[:, :half], mlp[:, 2 * half : 3 * half]
    down_ref[:, :half], down_ref[:, half:] = mlp[:, half : 2 * half], mlp[:, 3 * half :]
    feats = in_ref.shape[1]
    in_ref[...] = mixer[:, :feats]
    out_ref[...] = mixer[:, feats : 2 * feats]
    taps = param_ref.shape[1]
    tap_rows = mixer[:, 2 * feats : 2 * feats + taps]
    scale, wide = scale_ref[:, :taps], wide_ref[:, :taps]
    raw = param_ref[...].astype(F32) * scale
    inverse = lax.rsqrt(jnp.sum(raw * raw * wide, axis=1, keepdims=True) + 1e-05)
    own = raw * inverse
    along = jnp.sum(tap_rows * own, axis=1, keepdims=True)
    param_grad_ref[...] = scale * inverse * (tap_rows - wide * own * along)
    tail = mixer[:, 2 * feats + 256 :]
    rows = tail.shape[0]
    diagonal = lax.broadcasted_iota(jnp.int32, (rows, rows), 0) == lax.broadcasted_iota(
        jnp.int32, (rows, rows), 1
    )
    columns = (tail[:, 0:1], tail[:, 1:2], tap_rows[:, 0:1], tail[:, 8:9], tail[:, 9:10])
    for ref, column in zip(outs[5:], columns):
        ref[...] = jnp.sum(jnp.where(diagonal, column, 0.0), axis=0, keepdims=True)


def call(kernel, operands, outs, scratch=(), flops=0, spaces=None, limit=12):
    spaces = spaces or [pltpu.VMEM] * len(operands)
    operands = [
        pltpu.with_memory_space_constraint(operand, pltpu.HBM) if space is pltpu.HBM else operand
        for operand, space in zip(operands, spaces)
    ]
    return pl.pallas_call(
        kernel,
        out_shape=[jax.ShapeDtypeStruct(shape, dtype) for shape, dtype in outs],
        in_specs=[pl.BlockSpec(memory_space=space) for space in spaces],
        out_specs=[pl.BlockSpec(memory_space=pltpu.VMEM)] * len(outs),
        scratch_shapes=list(scratch),
        compiler_params=pltpu.CompilerParams(vmem_limit_bytes=limit << 20),
        cost_estimate=pl.CostEstimate(flops=flops, bytes_accessed=1 << 16, transcendentals=0),
    )(*operands)


def body(
    block_input,
    mixer_gain,
    mixer_bias,
    in_proj,
    kernel_param,
    skip_gain,
    out_proj,
    mlp_gain,
    mlp_bias,
    up_proj,
    down_proj,
    out_cotangent,
):
    _, length, feats = block_input.shape
    hidden = up_proj.shape[1]
    half = hidden // 2
    blocks = length // BLOCK
    pooled = length // POOL
    taps = TAPS * SCALES
    own_rows = in_proj.shape[0]
    x_own, cot = block_input[0], out_cotangent[0]
    core_at = jnp.stack([lax.axis_index("seq"), lax.axis_index("dp")]).astype(jnp.int32)
    x_prior = lax.ppermute(x_own, "seq", [(0, 1)])
    vectors = [v.reshape(1, -1) for v in (mixer_gain, mixer_bias, skip_gain, mlp_gain, mlp_bias)]
    shard, shard_b = call(
        pack_kernel,
        [core_at, in_proj, kernel_param, out_proj, up_proj, down_proj, *vectors],
        [((own_rows, PACK + feats + 2 * half), BF16), ((own_rows, 2 * half), BF16)],
        [
            pltpu.VMEM(kernel_param.shape, BF16), pltpu.VMEM((5, 1, own_rows), BF16),
            pltpu.SemaphoreType.DMA,
        ],
        spaces=[pltpu.SMEM] + [pltpu.HBM] * 10,
    )
    basis_np = odd_basis(np.arange(BLOCK))
    basis, basis_t = bf16_const(basis_np), bf16_const(basis_np.T)
    basis_pool = bf16_const(odd_basis(np.arange(-pooled, pooled)))
    back_pool = bf16_const(np.repeat(odd_basis(np.arange(pooled)).T, POOL, axis=0))
    fine_basis = bf16_const(tap_basis(0, 0))
    coarse_basis = bf16_const(tap_basis(OFFSET, TAPS * FINE))
    pool_rows = bf16_const(np.kron(np.eye(BLOCK // POOL), np.ones((1, POOL))) / POOL)
    scale_np = np.zeros((1, 256), np.float32)
    scale_np[0, :taps] = np.repeat(0.5 ** np.arange(SCALES), TAPS)
    wide_np = np.zeros((1, 256), np.float32)
    wide_np[0, :taps] = np.repeat(2.0 ** (np.arange(SCALES) % FINE), TAPS)

    xhat, inv_one, cot_t = call(
        prepare_kernel,
        [x_own, cot],
        [((length, feats), BF16), ((length, 128), F32), ((feats, length), BF16)],
        [
            pltpu.VMEM((length, feats), BF16), pltpu.VMEM((length, feats), BF16),
            pltpu.SemaphoreType.DMA((2, blocks)),
        ],
        spaces=[pltpu.HBM] * 2,
    )
    (prior_hat,) = call(prior_kernel, [x_prior], [((length, feats), BF16)])
    held_b = jnp.concatenate(gather_plane(tie(shard_b, prior_hat)[None]))
    held = shard[None]
    for at, step in enumerate(far_steps()):
        got = from_line(held, step)
        got = tie(got, xhat) if at == 0 else got
        held = paired(held, got)
    held = tie(held, xhat, prior_hat, held_b)
    steps = far_steps()
    held_b = held_b[None]
    for step in steps[:-1]:
        held_b = gather_line(held_b, step)
    xhat_in = tie(xhat, held_b)
    first, held_a = held[:, :, :PACK], held[:, :, PACK:]
    first = gather_near(first)
    pieces_a = gather_plane(held_a)
    first = in_order(gather_core(first), False)
    smem = pltpu.SMEM
    n_first = len(first)
    weights, vec, fine_h, coarse_h, window, pool_win, act, slope = call(
        lambda *refs: forward_kernel(n_first, *refs),
        [
            core_at, xhat_in, prior_hat, basis, basis_t, basis_pool,
            back_pool, fine_basis, coarse_basis, pool_rows, jnp.asarray(scale_np), jnp.asarray(wide_np),
            *first,
        ],
        [
            ((feats, PACK), BF16), ((8, feats), F32), ((2 * FREQ, feats), BF16),
            ((2 * FREQ, feats), BF16), ((blocks, 2 * FREQ, feats), BF16), ((2 * FREQ, feats), BF16),
            ((length, feats), BF16), ((length, feats), BF16),
        ],
        [
            pltpu.VMEM((length, feats), BF16), pltpu.VMEM((2 * pooled, feats), BF16),
        ],
        flops=6 << 30,
        spaces=[smem] + [pltpu.VMEM] * (11 + n_first),
    )
    got_b = [from_line(held_b, step) for step in steps[-1:]]
    pieces_a = in_order(gather_core(list(tie(tuple(pieces_a), act))), False)
    n_a = len(pieces_a)
    rows = own_rows


    def grad_shapes(columns):
        if rows % 16 == 0:
            return [((feats // (2 * rows), rows, columns), BF16)] * 2
        return [((feats, columns), BF16)]

    token_f32, token_bf16 = ((length, feats), F32), ((length, feats), BF16)
    vmem = pltpu.VMEM
    proj_out, mid, xhat_two, inv_two, normed, normed_t, hidden_a, grad_up_a, weights_a, *grads_a = call(
        lambda *refs: middle_first_kernel(n_a, *refs),
        [core_at, act, x_own, cot, cot_t, vec, *pieces_a],
        [
            ((feats, feats), BF16), token_f32, token_f32, ((length, 128), F32), token_bf16,
            ((feats, length), BF16), ((length, half), BF16), ((length, half), BF16),
            ((feats, feats + 2 * half), BF16), *grad_shapes(2 * half),
        ],
        flops=8 << 30,
        spaces=[smem] + [vmem] * (5 + n_a),
    )
    for got in got_b:
        held_b = paired(held_b, tie(got, mid))
    held_b = held_b.reshape((-1,) + held_b.shape[2:])
    pieces_b = in_order(gather_core([held_b]), True)
    n_b = len(pieces_b)
    hidden_b, grad_up_b, weights_b, *grads_b = call(
        lambda *refs: middle_second_kernel(n_b, *refs),
        [core_at, cot, cot_t, normed, normed_t, *pieces_b],
        [((length, half), BF16), ((length, half), BF16), ((feats, 2 * half), BF16), *grad_shapes(2 * half)],
        flops=5 << 24,
        spaces=[smem] + [vmem] * (4 + n_b),
    )
    near_a = reduce_core(grads_a)
    grad_up_b = tie(grad_up_b, *near_a)
    spread_a = spread_near(near_a)
    grad_mid, vec_grad, grad_pre, halo = call(
        middle_third_kernel,
        [slope, cot, vec, pool_rows, proj_out, xhat_two, inv_two, grad_up_a, grad_up_b, weights_a, weights_b],
        [token_f32, ((8, feats), F32), token_bf16, ((BLOCK + pooled, feats), BF16)],
        flops=4 << 24,
    )
    after = lax.ppermute(halo, "seq", [(1, 0)])
    near_b = reduce_core(grads_b)
    grad_pre = tie(grad_pre, *near_b)
    spread_b = spread_near(near_b)
    out_grad, tap_grad, z_grad = call(
        taps_kernel,
        [act, grad_mid, grad_pre, halo, window, pool_win, basis, fine_basis, coarse_basis],
        [
            ((feats, feats), BF16), ((feats, 256), BF16), ((blocks, 2 * FREQ, feats), BF16),
        ],
        [pltpu.VMEM((length, feats), BF16)],
        flops=2 << 24,
    )
    z_grad = tie(z_grad, after)
    grad_mixed, *grads_c = call(
        backward_kernel,
        [
            core_at, z_grad, halo, after, grad_pre, fine_h, coarse_h, basis, basis_t, back_pool, weights,
            vec, vec_grad, xhat, out_grad, tap_grad,
        ],
        [token_bf16, *grad_shapes(2 * feats + 384)],
        [pltpu.VMEM((2 * pooled, feats), BF16)],
        flops=4 << 24,
        spaces=[smem] + [vmem] * 15,
    )
    (input_grad,) = call(
        input_kernel, [grad_mixed, weights, vec, xhat, inv_one, grad_mid], [token_f32], flops=2 << 24
    )
    part_a = add_up(tie(tuple(spread_a), grad_mixed), BF16)
    part_b = add_up(tie(tuple(spread_b), grad_mixed), BF16)
    part_ab = jnp.concatenate([part_a, part_b], axis=2)
    far_ab = spread_far(part_ab)
    near_c = reduce_core(grads_c, part_ab, input_grad)
    spread_c = spread_near(near_c)
    (block_output,) = call(
        output_kernel, [tie(mid, *near_c), hidden_a, hidden_b, weights_a, weights_b], [token_bf16], flops=4 << 24
    )
    far_c = spread_far(add_up(tie(tuple(spread_c), block_output), BF16))
    vector = ((1, rows), F32)
    up_sum, down_sum, in_sum, out_sum, param_sum, *vectors = call(
        final_kernel,
        [kernel_param, jnp.asarray(scale_np), jnp.asarray(wide_np), *far_ab, *far_c],
        [
            ((rows, hidden), F32), ((rows, hidden), F32), ((rows, feats), F32), ((rows, feats), F32),
            ((rows, taps), F32), vector, vector, vector, vector, vector,
        ],
    )
    gain_one, bias_one, skip_sum, gain_two, bias_two = (v.reshape(rows) for v in vectors)
    return (
        block_output[None], input_grad[None], gain_one, bias_one, in_sum, param_sum, skip_sum, out_sum,
        gain_two, bias_two, up_sum, down_sum,
    )


def solution(mesh):
    rows = P(("dp", "seq"), None)
    vector = P(("dp", "seq"))
    tokens = P("dp", "seq", None)
    return jax.shard_map(
        body,
        mesh=mesh,
        in_specs=(
            tokens, vector, vector, rows, rows, vector, rows, vector, vector, rows, rows, tokens,
        ),
        out_specs=(
            tokens, tokens, vector, vector, rows, rows, vector, rows, vector, vector, rows, rows,
        ),
        check_vma=False,
    )
```

profile of v0, /device:TPU:0, one launch (start us, length us, event | category | flops | bytes accessed | tf_op | source)
XLA Modules:
  0.0 121.0 jit_solution(671687188460037834)
XLA Ops:
  0.6 2.4 %collective-permute-start = (bf16[1024,512]{1,0:T(8,128)(2,1)}, bf16[1024,512]{1,0:T(8,128)(2,1)S(1)}, u32[]{:S(2)}, u32[]{:S(2)}) collective-permute-start(bf16[1024,512]{1,0:T(8,128)(2,1)} %bitcast.59), channel_id=1, source_target_pairs={{0,1},{2,3},{4,5},{6,7},{8,9},{10,11},{12,13},{14,15},{16,17},{18,... | collective-permute-start | bytes 3145736 | tf_op jit(solution)/shard_map/ppermute | solution.py:653
  4.8 3.5 %collective-permute-start.5 = (bf16[1,16,3328]{2,1,0:T(8,128)(2,1)S(1)}, bf16[1,16,3328]{2,1,0:T(8,128)(2,1)S(1)}, u32[]{:S(2)}, u32[]{:S(2)}) collective-permute-start(bf16[1,16,3328]{2,1,0:T(8,128)(2,1)S(1)} %bitcast.62), channel_id=1, source_target_pairs={{0,16},{2,18},{4,20},{6,22},{8,24},{10,26},{12,28},{14,30},{16,0},... | collective-permute-start | bytes 319496 | tf_op jit(solution)/shard_map/ppermute | solution.py:83
  8.3 2.4 %shard_map.292 = (bf16[1024,512]{1,0:T(8,128)(2,1)S(1)}, f32[1024,128]{1,0:T(8,128)S(1)}, bf16[512,1024]{1,0:T(8,128)(2,1)S(1)}) custom-call(bf16[1024,512]{1,0:T(8,128)(2,1)} %bitcast.60, bf16[1024,512]{1,0:T(8,128)(2,1)} %bitcast.53), custom_call_target="tpu_custom_call" | custom-call | bytes 65536 | tf_op jit(solution)/shard_map/pallas_call | solution.py:619
  10.7 2.3 %collective-permute-done.5 = bf16[1,16,3328]{2,1,0:T(8,128)(2,1)S(1)} collective-permute-done((bf16[1,16,3328]{2,1,0:T(8,128)(2,1)S(1)}, bf16[1,16,3328]{2,1,0:T(8,128)(2,1)S(1)}, u32[]{:S(2)}, u32[]{:S(2)}) %collective-permute-start.5) | collective-permute-done | bytes 106528 | tf_op jit(solution)/shard_map/ppermute | solution.py:83
  27.2 3.4 %collective-permute-start.4 = (bf16[1,4,16,2048]{3,2,1,0:T(8,128)(2,1)S(1)}, bf16[1,4,16,2048]{3,2,1,0:T(8,128)(2,1)S(1)}, u32[]{:S(2)}, u32[]{:S(2)}) collective-permute-start(bf16[1,4,16,2048]{3,2,1,0:T(8,128)(2,1)S(1)} %get-tuple-element.183), channel_id=1, source_target_pairs={{0,16},{2,18},{4,20},{6,22},{8,24},{10,26},{12,28},{14,30},{16,0},... | collective-permute-start | bytes 786440 | tf_op jit(solution)/shard_map/ppermute | solution.py:83
  30.8 2.6 %collective-permute-done.12 = bf16[4,16,2560]{2,1,0:T(8,128)(2,1)S(1)} collective-permute-done((bf16[4,16,2560]{2,1,0:T(8,128)(2,1)S(1)}, bf16[4,16,2560]{2,1,0:T(8,128)(2,1)S(1)}, u32[]{:S(2)}, u32[]{:S(2)}) %collective-permute-start.12) | collective-permute-done | bytes 327712 | tf_op jit(solution)/shard_map/ppermute | solution.py:118
  35.6 3.2 %collective-permute-done.4 = bf16[1,4,16,2048]{3,2,1,0:T(8,128)(2,1)S(1)} collective-permute-done((bf16[1,4,16,2048]{3,2,1,0:T(8,128)(2,1)S(1)}, bf16[1,4,16,2048]{3,2,1,0:T(8,128)(2,1)S(1)}, u32[]{:S(2)}, u32[]{:S(2)}) %collective-permute-start.4) | collective-permute-done | bytes 262176 | tf_op jit(solution)/shard_map/ppermute | solution.py:83
  38.9 7.3 %shard_map.295 = (bf16[512,768]{1,0:T(8,128)(2,1)S(1)}, f32[8,512]{1,0:T(8,128)S(1)}, bf16[512,512]{1,0:T(8,128)(2,1)S(1)}, bf16[512,512]{1,0:T(8,128)(2,1)S(1)}...) custom-call(s32[2]{0:T(128)S(1)} %pad_add_fusion.core_ref.refs_0_, ...), custom_call_target="tpu_custom_call" | custom-call | flops 6442450944 | bytes 65536 | tf_op jit(solution)/shard_map/pallas_call | solution.py:619
  47.2 2.3 %collective-permute-done.15.refs_7_ = bf16[16,16,2560]{2,1,0:T(8,128)(2,1)S(1)} collective-permute-done((bf16[16,16,2560]{2,1,0:T(8,128)(2,1)S(1)}, bf16[16,16,2560]{2,1,0:T(8,128)(2,1)S(1)}, u32[]{:S(2)}, u32[]{:S(2)}) %collective-permute-start.15) | collective-permute-done | bytes 1310752 | tf_op jit(solution)/shard_map/ppermute | solution.py:109
  49.5 7.3 %shard_map.296 = (bf16[512,512]{1,0:T(8,128)(2,1)S(1)}, f32[1024,512]{1,0:T(8,128)S(1)}, f32[1024,512]{1,0:T(8,128)S(1)}, f32[1024,128]{1,0:T(8,128)S(1)}, bf16[...) custom-call(s32[2]{0:T(128)S(1)} %pad_add_fusion.core_ref.refs_0_, ...), custom_call_target="tpu_custom_call" | custom-call | flops 8589934592 | bytes 65536 | tf_op jit(solution)/shard_map/pallas_call | solution.py:619
  56.8 4.0 %collective-permute-done.16 = bf16[2,4,16,2048]{3,2,1,0:T(8,128)(2,1)S(1)} collective-permute-done((bf16[2,4,16,2048]{3,2,1,0:T(8,128)(2,1)S(1)}, bf16[2,4,16,2048]{3,2,1,0:T(8,128)(2,1)S(1)}, u32[]{:S(2)}, u32[]{:S(2)}) %collective-permute-start.16) | collective-permute-done | bytes 524320 | tf_op jit(solution)/shard_map/ppermute | solution.py:83
  61.6 2.1 %collective-permute-done.17.refs_6_ = bf16[16,16,2048]{2,1,0:T(8,128)(2,1)S(1)} collective-permute-done((bf16[16,16,2048]{2,1,0:T(8,128)(2,1)S(1)}, bf16[16,16,2048]{2,1,0:T(8,128)(2,1)S(1)}, u32[]{:S(2)}, u32[]{:S(2)}) %collective-permute-start.17) | collective-permute-done | bytes 1048608 | tf_op jit(solution)/shard_map/ppermute | solution.py:109
  63.7 6.2 %shard_map.297 = (bf16[1024,1024]{1,0:T(8,128)(2,1)S(1)}, bf16[1024,1024]{1,0:T(8,128)(2,1)S(1)}, bf16[512,2048]{1,0:T(8,128)(2,1)S(1)}, bf16[16,16,2048]{2,1,0:T(8,128)(2,1)S(1)}, bf16[16,16,2048]{2,1,0:T(8,128)(2,1)S(1)}) custom-call(s32[2]{0:T(128)S(1)} %pad_add_fusion.core_ref.refs_0_, bf16[1024,512]{1,0:T(8,128)(2,1)S(1)} %bitcast.55, ...), custom_call_target="tpu_custom_call" | custom-call | flops 83886080 | bytes 65536 | tf_op jit(solution)/shard_map/pallas_call | solution.py:619
  70.6 1.9 %collective-permute-start.24 = (bf16[4,16,2048]{2,1,0:T(8,128)(2,1)S(1)}, bf16[4,16,2048]{2,1,0:T(8,128)(2,1)S(1)}, u32[]{:S(2)}, u32[]{:S(2)}) collective-permute-start(bf16[4,16,2048]{2,1,0:T(8,128)(2,1)S(1)} %get-tuple-element.168), channel_id=1, source_target_pairs={{0,6},{2,4},{4,2},{6,0},{8,14},{10,12},{12,10},{14,8},{16,22},{18,... | collective-permute-start | bytes 786440 | tf_op jit(solution)/shard_map/ppermute | solution.py:173
  74.2 4.7 %shard_map.298 = (f32[1024,512]{1,0:T(8,128)S(1)}, f32[8,512]{1,0:T(8,128)S(1)}, bf16[1024,512]{1,0:T(8,128)(2,1)S(1)}, bf16[384,512]{1,0:T(8,128)(2,1)S(1)}) custom-call(bf16[1024,512]{1,0:T(8,128)(2,1)S(1)} %get-tuple-element.104.slope_ref, bf16[1024,512]{1,0:T(8,128)(2,1)S(1)} %bitcast.56, f32[8,512]{1,0:T(8,128)S(1)} %get-tuple-element.97.refs_5_.vec_ref, ...), custom_call_target="tpu_custom_call" | custom-call | flops 67108864 | bytes 65536 | tf_op jit(solution)/shard_map/pallas_call | solution.py:619
  80.9 1.8 %collective-permute-start.27 = (bf16[4,16,2048]{2,1,0:T(8,128)(2,1)S(1)}, bf16[4,16,2048]{2,1,0:T(8,128)(2,1)S(1)}, u32[]{:S(2)}, u32[]{:S(2)}) collective-permute-start(bf16[4,16,2048]{2,1,0:T(8,128)(2,1)S(1)} %get-tuple-element.164), channel_id=1, source_target_pairs={{0,6},{2,4},{4,2},{6,0},{8,14},{10,12},{12,10},{14,8},{16,22},{18,... | collective-permute-start | bytes 786440 | tf_op jit(solution)/shard_map/ppermute | solution.py:173
  84.4 3.0 %shard_map.299 = (bf16[512,512]{1,0:T(8,128)(2,1)S(1)}, bf16[512,256]{1,0:T(8,128)(2,1)S(1)}, bf16[4,512,512]{2,1,0:T(8,128)(2,1)S(1)}) custom-call(bf16[1024,512]{1,0:T(8,128)(2,1)S(1)} %get-tuple-element.95.refs_1_.act_ref, f32[1024,512]{1,0:T(8,128)S(1)} %get-tuple-element.118.mid_grad_ref, bf16[1024,512]{1,0:T(8,128)(2,1)S(1)} %get-tuple-element.122.pre_grad_ref, ...), custom_call_target="tpu_custom_call" | custom-call | flops 33554432 | bytes 65536 | tf_op jit(solution)/shard_map/pallas_call | solution.py:619
  87.4 4.2 %shard_map.300 = (bf16[1024,512]{1,0:T(8,128)(2,1)S(1)}, bf16[16,16,1408]{2,1,0:T(8,128)(2,1)S(1)}, bf16[16,16,1408]{2,1,0:T(8,128)(2,1)S(1)}) custom-call(s32[2]{0:T(128)S(1)} %pad_add_fusion.core_ref.refs_0_, bf16[4,512,512]{2,1,0:T(8,128)(2,1)S(1)} %get-tuple-element.127.z_ref, bf16[384,512]{1,0:T(8,128)(2,1)S(1)} %get-tuple-element.123.halo_ref, ...), custom_call_target="tpu_custom_call" | custom-call | flops 67108864 | bytes 65536 | tf_op jit(solution)/shard_map/pallas_call | solution.py:619
  92.2 2.5 %shard_map.301 = f32[1024,512]{1,0:T(8,128)} custom-call(bf16[1024,512]{1,0:T(8,128)(2,1)S(1)} %get-tuple-element.136.mixed_grad_ref, bf16[512,768]{1,0:T(8,128)(2,1)S(1)} %get-tuple-element.130.weights, f32[8,512]{1,0:T(8,128)S(1)} %get-tuple-element.97.refs_5_.vec_ref, bf16[1024,512]{1,0:T(8,128)(2,1)S(1)} %get-tuple-element.91.refs_1_.xhat_ref, ...), custom_call_target="tpu_custom_call" | custom-call | flops 33554432 | bytes 65536 | tf_op jit(solution)/shard_map/pallas_call | solution.py:619
  94.6 2.4 %collective-permute-done.26 = bf16[4,16,2048]{2,1,0:T(8,128)(2,1)S(1)} collective-permute-done((bf16[4,16,2048]{2,1,0:T(8,128)(2,1)S(1)}, bf16[4,16,2048]{2,1,0:T(8,128)(2,1)S(1)}, u32[]{:S(2)}, u32[]{:S(2)}) %collective-permute-start.26) | collective-permute-done | bytes 262176 | tf_op jit(solution)/shard_map/ppermute | solution.py:173
  101.7 3.1 %collective-permute-start.30 = (bf16[16,4096]{1,0:T(8,128)(2,1)S(1)}, bf16[16,4096]{1,0:T(8,128)(2,1)S(1)}, u32[]{:S(2)}, u32[]{:S(2)}) collective-permute-start(bf16[16,4096]{1,0:T(8,128)(2,1)S(1)} %get-tuple-element.176), channel_id=1, source_target_pairs={{0,24},{2,26},{4,28},{6,30},{8,16},{10,18},{12,20},{14,22},{16,8},... | collective-permute-start | bytes 393224 | tf_op jit(solution)/shard_map/ppermute | solution.py:181
  104.8 3.3 %shard_map.302 = bf16[1024,512]{1,0:T(8,128)(2,1)} custom-call(f32[1024,512]{1,0:T(8,128)S(1)} %get-tuple-element.147.mid_ref, bf16[1024,1024]{1,0:T(8,128)(2,1)S(1)} %get-tuple-element.148.hidden_a_ref, bf16[1024,1024]{1,0:T(8,128)(2,1)S(1)} %get-tuple-element.149.hidden_b_ref, bf16[512,2560]{1,0:T(8,128)(2,1)S(1)} %get-tuple-element.116.weights_a, ...), custom_call_target="tpu_custom_call" | custom-call | flops 67108864 | bytes 65536 | tf_op jit(solution)/shard_map/pallas_call | solution.py:619
  109.6 3.1 %collective-permute-start.36 = (bf16[16,1408]{1,0:T(8,128)(2,1)S(1)}, bf16[16,1408]{1,0:T(8,128)(2,1)S(1)}, u32[]{:S(2)}, u32[]{:S(2)}) collective-permute-start(bf16[16,1408]{1,0:T(8,128)(2,1)S(1)} %get-tuple-element.186), channel_id=1, source_target_pairs={{0,24},{2,26},{4,28},{6,30},{8,16},{10,18},{12,20},{14,22},{16,8},... | collective-permute-start | bytes 135176 | tf_op jit(solution)/shard_map/ppermute | solution.py:181
  114.1 5.1 %collective-permute-done.29.rest_2_ = bf16[16,4096]{1,0:T(8,128)(2,1)S(1)} collective-permute-done((bf16[16,4096]{1,0:T(8,128)(2,1)S(1)}, bf16[16,4096]{1,0:T(8,128)(2,1)S(1)}, u32[]{:S(2)}, u32[]{:S(2)}) %collective-permute-start.29) | collective-permute-done | bytes 131104 | tf_op jit(solution)/shard_map/ppermute | solution.py:181
  (114 shorter events, 35.8 us)
Async XLA Ops:
  0.6 13.2 %collective-permute-start = (bf16[1024,512]{1,0:T(8,128)(2,1)}, bf16[1024,512]{1,0:T(8,128)(2,1)S(1)}, u32[]{:S(2)}, u32[]{:S(2)}) collective-permute-start(bf16[1024,512]{1,0:T(8,128)(2,1)} %bitcast.59), channel_id=1, source_target_pairs={{0,1},{2,3},{4,5},{6,7},{8,9},{10,11},{12,13},{14,15},{16,17},{18,... | collective-permute-start | bytes 3145736 | tf_op jit(solution)/shard_map/ppermute | solution.py:653
  4.8 8.2 %collective-permute-start.5 = (bf16[1,16,3328]{2,1,0:T(8,128)(2,1)S(1)}, bf16[1,16,3328]{2,1,0:T(8,128)(2,1)S(1)}, u32[]{:S(2)}, u32[]{:S(2)}) collective-permute-start(bf16[1,16,3328]{2,1,0:T(8,128)(2,1)S(1)} %bitcast.62), channel_id=1, source_target_pairs={{0,16},{2,18},{4,20},{6,22},{8,24},{10,26},{12,28},{14,30},{16,0},... | collective-permute-start | bytes 319496 | tf_op jit(solution)/shard_map/ppermute | solution.py:83
  22.0 8.6 %collective-permute-start.8 = (bf16[4,16,768]{2,1,0:T(8,128)(2,1)S(1)}, bf16[4,16,768]{2,1,0:T(8,128)(2,1)S(1)}, u32[]{:S(2)}, u32[]{:S(2)}) collective-permute-start(bf16[4,16,768]{2,1,0:T(8,128)(2,1)S(1)} %slice.72), channel_id=1, source_target_pairs={{0,4},{2,6},{4,0},{6,2},{8,12},{10,14},{12,8},{14,10},{16,20},{18,... | collective-permute-start | bytes 294920 | tf_op jit(solution)/shard_map/ppermute | solution.py:104
  24.0 9.4 %collective-permute-start.12 = (bf16[4,16,2560]{2,1,0:T(8,128)(2,1)S(1)}, bf16[4,16,2560]{2,1,0:T(8,128)(2,1)S(1)}, u32[]{:S(2)}, u32[]{:S(2)}) collective-permute-start(bf16[4,16,2560]{2,1,0:T(8,128)(2,1)S(1)} %slice.73), channel_id=1, source_target_pairs={{0,4},{2,6},{4,0},{6,2},{8,12},{10,14},{12,8},{14,10},{16,20},{18,... | collective-permute-start | bytes 983048 | tf_op jit(solution)/shard_map/ppermute | solution.py:118
  25.5 8.8 %collective-permute-start.11 = (bf16[4,16,2560]{2,1,0:T(8,128)(2,1)S(1)}, bf16[4,16,2560]{2,1,0:T(8,128)(2,1)S(1)}, u32[]{:S(2)}, u32[]{:S(2)}) collective-permute-start(bf16[4,16,2560]{2,1,0:T(8,128)(2,1)S(1)} %slice.73), channel_id=1, source_target_pairs={{0,2},{2,0},{4,6},{6,4},{8,10},{10,8},{12,14},{14,12},{16,18},{18,... | collective-permute-start | bytes 983048 | tf_op jit(solution)/shard_map/ppermute | solution.py:117
  27.2 11.5 %collective-permute-start.4 = (bf16[1,4,16,2048]{3,2,1,0:T(8,128)(2,1)S(1)}, bf16[1,4,16,2048]{3,2,1,0:T(8,128)(2,1)S(1)}, u32[]{:S(2)}, u32[]{:S(2)}) collective-permute-start(bf16[1,4,16,2048]{3,2,1,0:T(8,128)(2,1)S(1)} %get-tuple-element.183), channel_id=1, source_target_pairs={{0,16},{2,18},{4,20},{6,22},{8,24},{10,26},{12,28},{14,30},{16,0},... | collective-permute-start | bytes 786440 | tf_op jit(solution)/shard_map/ppermute | solution.py:83
  33.4 12.8 %collective-permute-start.13 = (bf16[2,16,2560]{2,1,0:T(8,128)(2,1)S(1)}, bf16[2,16,2560]{2,1,0:T(8,128)(2,1)S(1)}, u32[]{:S(2)}, u32[]{:S(2)}) collective-permute-start(bf16[2,16,2560]{2,1,0:T(8,128)(2,1)S(1)} %slice.96), channel_id=1, source_target_pairs={{0,2},{2,0},{4,6},{6,4},{8,10},{10,8},{12,14},{14,12},{16,18},{18,... | collective-permute-start | bytes 491528 | tf_op jit(solution)/shard_map/ppermute | solution.py:123
  34.3 11.9 %collective-permute-start.14 = (bf16[2,16,2560]{2,1,0:T(8,128)(2,1)S(1)}, bf16[2,16,2560]{2,1,0:T(8,128)(2,1)S(1)}, u32[]{:S(2)}, u32[]{:S(2)}) collective-permute-start(bf16[2,16,2560]{2,1,0:T(8,128)(2,1)S(1)} %slice.97), channel_id=1, source_target_pairs={{0,4},{2,6},{4,0},{6,2},{8,12},{10,14},{12,8},{14,10},{16,20},{18,... | collective-permute-start | bytes 491528 | tf_op jit(solution)/shard_map/ppermute | solution.py:124
  46.5 14.3 %collective-permute-start.16 = (bf16[2,4,16,2048]{3,2,1,0:T(8,128)(2,1)S(1)}, bf16[2,4,16,2048]{3,2,1,0:T(8,128)(2,1)S(1)}, u32[]{:S(2)}, u32[]{:S(2)}) collective-permute-start(bf16[2,4,16,2048]{3,2,1,0:T(8,128)(2,1)S(1)} %get-tuple-element.181), channel_id=1, source_target_pairs={{0,8},{2,10},{4,12},{6,14},{8,0},{10,2},{12,4},{14,6},{16,24},{18,... | collective-permute-start | bytes 1572872 | tf_op jit(solution)/shard_map/ppermute | solution.py:83
  61.1 9.0 %collective-permute-start.18 = (bf16[16,16,2048]{2,1,0:T(8,128)(2,1)S(1)}, bf16[16,16,2048]{2,1,0:T(8,128)(2,1)S(1)}, u32[]{:S(2)}, u32[]{:S(2)}) collective-permute-start(bf16[16,16,2048]{2,1,0:T(8,128)(2,1)S(1)} %get-tuple-element.114), channel_id=1, source_target_pairs={{0,1},{1,0},{2,3},{3,2},{4,5},{5,4},{6,7},{7,6},{8,9},{9,8},{10,11... | collective-permute-start | bytes 3145736 | tf_op jit(solution)/shard_map/ppermute | solution.py:164
  69.9 10.5 %collective-permute-start.19 = (bf16[16,16,2048]{2,1,0:T(8,128)(2,1)S(1)}, bf16[16,16,2048]{2,1,0:T(8,128)(2,1)S(1)}, u32[]{:S(2)}, u32[]{:S(2)}) collective-permute-start(bf16[16,16,2048]{2,1,0:T(8,128)(2,1)S(1)} %get-tuple-element.121), channel_id=1, source_target_pairs={{0,1},{1,0},{2,3},{3,2},{4,5},{5,4},{6,7},{7,6},{8,9},{9,8},{10,11... | collective-permute-start | bytes 3145736 | tf_op jit(solution)/shard_map/ppermute | solution.py:164
  70.6 12.1 %collective-permute-start.24 = (bf16[4,16,2048]{2,1,0:T(8,128)(2,1)S(1)}, bf16[4,16,2048]{2,1,0:T(8,128)(2,1)S(1)}, u32[]{:S(2)}, u32[]{:S(2)}) collective-permute-start(bf16[4,16,2048]{2,1,0:T(8,128)(2,1)S(1)} %get-tuple-element.168), channel_id=1, source_target_pairs={{0,6},{2,4},{4,2},{6,0},{8,14},{10,12},{12,10},{14,8},{16,22},{18,... | collective-permute-start | bytes 786440 | tf_op jit(solution)/shard_map/ppermute | solution.py:173
  72.5 19.2 %collective-permute-start.23 = (bf16[4,16,2048]{2,1,0:T(8,128)(2,1)S(1)}, bf16[4,16,2048]{2,1,0:T(8,128)(2,1)S(1)}, u32[]{:S(2)}, u32[]{:S(2)}) collective-permute-start(bf16[4,16,2048]{2,1,0:T(8,128)(2,1)S(1)} %get-tuple-element.169), channel_id=1, source_target_pairs={{0,4},{2,6},{4,0},{6,2},{8,12},{10,14},{12,8},{14,10},{16,20},{18,... | collective-permute-start | bytes 786440 | tf_op jit(solution)/shard_map/ppermute | solution.py:173
  73.4 18.8 %collective-permute-start.22 = (bf16[4,16,2048]{2,1,0:T(8,128)(2,1)S(1)}, bf16[4,16,2048]{2,1,0:T(8,128)(2,1)S(1)}, u32[]{:S(2)}, u32[]{:S(2)}) collective-permute-start(bf16[4,16,2048]{2,1,0:T(8,128)(2,1)S(1)} %get-tuple-element.170), channel_id=1, source_target_pairs={{0,2},{2,0},{4,6},{6,4},{8,10},{10,8},{12,14},{14,12},{16,18},{18,... | collective-permute-start | bytes 786440 | tf_op jit(solution)/shard_map/ppermute | solution.py:173
  80.9 13.8 %collective-permute-start.27 = (bf16[4,16,2048]{2,1,0:T(8,128)(2,1)S(1)}, bf16[4,16,2048]{2,1,0:T(8,128)(2,1)S(1)}, u32[]{:S(2)}, u32[]{:S(2)}) collective-permute-start(bf16[4,16,2048]{2,1,0:T(8,128)(2,1)S(1)} %get-tuple-element.164), channel_id=1, source_target_pairs={{0,6},{2,4},{4,2},{6,0},{8,14},{10,12},{12,10},{14,8},{16,22},{18,... | collective-permute-start | bytes 786440 | tf_op jit(solution)/shard_map/ppermute | solution.py:173
  82.7 14.3 %collective-permute-start.26 = (bf16[4,16,2048]{2,1,0:T(8,128)(2,1)S(1)}, bf16[4,16,2048]{2,1,0:T(8,128)(2,1)S(1)}, u32[]{:S(2)}, u32[]{:S(2)}) collective-permute-start(bf16[4,16,2048]{2,1,0:T(8,128)(2,1)S(1)} %get-tuple-element.165), channel_id=1, source_target_pairs={{0,4},{2,6},{4,0},{6,2},{8,12},{10,14},{12,8},{14,10},{16,20},{18,... | collective-permute-start | bytes 786440 | tf_op jit(solution)/shard_map/ppermute | solution.py:173
  83.6 13.8 %collective-permute-start.25 = (bf16[4,16,2048]{2,1,0:T(8,128)(2,1)S(1)}, bf16[4,16,2048]{2,1,0:T(8,128)(2,1)S(1)}, u32[]{:S(2)}, u32[]{:S(2)}) collective-permute-start(bf16[4,16,2048]{2,1,0:T(8,128)(2,1)S(1)} %get-tuple-element.166), channel_id=1, source_target_pairs={{0,2},{2,0},{4,6},{6,4},{8,10},{10,8},{12,14},{14,12},{16,18},{18,... | collective-permute-start | bytes 786440 | tf_op jit(solution)/shard_map/ppermute | solution.py:173
  98.1 10.1 %collective-permute-start.33 = (bf16[4,16,1408]{2,1,0:T(8,128)(2,1)S(1)}, bf16[4,16,1408]{2,1,0:T(8,128)(2,1)S(1)}, u32[]{:S(2)}, u32[]{:S(2)}) collective-permute-start(bf16[4,16,1408]{2,1,0:T(8,128)(2,1)S(1)} %get-tuple-element.172), channel_id=1, source_target_pairs={{0,6},{2,4},{4,2},{6,0},{8,14},{10,12},{12,10},{14,8},{16,22},{18,... | collective-permute-start | bytes 540680 | tf_op jit(solution)/shard_map/ppermute | solution.py:173
  99.4 10.0 %collective-permute-start.32 = (bf16[4,16,1408]{2,1,0:T(8,128)(2,1)S(1)}, bf16[4,16,1408]{2,1,0:T(8,128)(2,1)S(1)}, u32[]{:S(2)}, u32[]{:S(2)}) collective-permute-start(bf16[4,16,1408]{2,1,0:T(8,128)(2,1)S(1)} %get-tuple-element.173), channel_id=1, source_target_pairs={{0,4},{2,6},{4,0},{6,2},{8,12},{10,14},{12,8},{14,10},{16,20},{18,... | collective-permute-start | bytes 540680 | tf_op jit(solution)/shard_map/ppermute | solution.py:173
  100.4 9.1 %collective-permute-start.31 = (bf16[4,16,1408]{2,1,0:T(8,128)(2,1)S(1)}, bf16[4,16,1408]{2,1,0:T(8,128)(2,1)S(1)}, u32[]{:S(2)}, u32[]{:S(2)}) collective-permute-start(bf16[4,16,1408]{2,1,0:T(8,128)(2,1)S(1)} %get-tuple-element.174), channel_id=1, source_target_pairs={{0,2},{2,0},{4,6},{6,4},{8,10},{10,8},{12,14},{14,12},{16,18},{18,... | collective-permute-start | bytes 540680 | tf_op jit(solution)/shard_map/ppermute | solution.py:173
  101.7 11.0 %collective-permute-start.30 = (bf16[16,4096]{1,0:T(8,128)(2,1)S(1)}, bf16[16,4096]{1,0:T(8,128)(2,1)S(1)}, u32[]{:S(2)}, u32[]{:S(2)}) collective-permute-start(bf16[16,4096]{1,0:T(8,128)(2,1)S(1)} %get-tuple-element.176), channel_id=1, source_target_pairs={{0,24},{2,26},{4,28},{6,30},{8,16},{10,18},{12,20},{14,22},{16,8},... | collective-permute-start | bytes 393224 | tf_op jit(solution)/shard_map/ppermute | solution.py:181
  104.8 9.3 %collective-permute-start.28 = (bf16[16,4096]{1,0:T(8,128)(2,1)S(1)}, bf16[16,4096]{1,0:T(8,128)(2,1)S(1)}, u32[]{:S(2)}, u32[]{:S(2)}) collective-permute-start(bf16[16,4096]{1,0:T(8,128)(2,1)S(1)} %get-tuple-element.177), channel_id=1, source_target_pairs={{0,8},{2,10},{4,12},{6,14},{8,0},{10,2},{12,4},{14,6},{16,24},{18,... | collective-permute-start | bytes 393224 | tf_op jit(solution)/shard_map/ppermute | solution.py:181
  108.1 11.0 %collective-permute-start.29 = (bf16[16,4096]{1,0:T(8,128)(2,1)S(1)}, bf16[16,4096]{1,0:T(8,128)(2,1)S(1)}, u32[]{:S(2)}, u32[]{:S(2)}) collective-permute-start(bf16[16,4096]{1,0:T(8,128)(2,1)S(1)} %get-tuple-element.178), channel_id=1, source_target_pairs={{0,16},{2,18},{4,20},{6,22},{8,24},{10,26},{12,28},{14,30},{16,0},... | collective-permute-start | bytes 393224 | tf_op jit(solution)/shard_map/ppermute | solution.py:181
  109.6 9.6 %collective-permute-start.36 = (bf16[16,1408]{1,0:T(8,128)(2,1)S(1)}, bf16[16,1408]{1,0:T(8,128)(2,1)S(1)}, u32[]{:S(2)}, u32[]{:S(2)}) collective-permute-start(bf16[16,1408]{1,0:T(8,128)(2,1)S(1)} %get-tuple-element.186), channel_id=1, source_target_pairs={{0,24},{2,26},{4,28},{6,30},{8,16},{10,18},{12,20},{14,22},{16,8},... | collective-permute-start | bytes 135176 | tf_op jit(solution)/shard_map/ppermute | solution.py:181
  (25 other events, 208.3 us)
where the time goes:
time: 121 us
  starting transfers between devices  45.7 us (38%)
  Pallas kernels  44 us (36%)
  waiting for transfers between devices  27.8 us (23%)
  other arithmetic  1.82 us (2%)
    pallas_call x12, Pallas kernels, call(): pl.pallas_call(kernel, out_shape=[jax.ShapeDtypeStruct(shape, dtype) for...  44 us
    ppermute x9, starting transfers between devices, spread_near(): lax.ppermute(pieces[k], 'dp', swap_route(dp_count, k))  10.7 us
    ppermute x4, waiting for transfers between devices, from_line(): return lax.ppermute(held, 'dp', swap_route(dp_count, step * nxy))  9.49 us
    ppermute x6, starting transfers between devices, spread_far(): lax.ppermute(part[k], 'dp', swap_route(dp_count, k * nxy))  8.91 us
    ppermute x4, starting transfers between devices, from_line(): return lax.ppermute(held, 'dp', swap_route(dp_count, step * nxy))  8.42 us
    ppermute x6, waiting for transfers between devices, spread_far(): lax.ppermute(part[k], 'dp', swap_route(dp_count, k * nxy))  6.11 us
    ppermute x3, waiting for transfers between devices, gather_core(): return [held, lax.ppermute(held, 'seq', SWAP)]  4.44 us
    ppermute x2, waiting for transfers between devices, gather_plane(): by_y = lax.ppermute(held, 'dp', swap_route(dp_count, 2))  3.86 us
  transfers between devices with their start and end apart: 37, of which 12 were waited for; matrix products, arithmetic and copies ran while one was open for 2% of the time, Pallas kernels for 36%

commit v1 on v0

--- a/solution.py
+++ b/solution.py
@@ -104,9 +104,11 @@
     return [held] + [lax.ppermute(held, "dp", swap_route(dp_count, k)) for k in range(1, nxy)]
 
 
-def gather_core(pieces):
+def gather_core(pieces, parts=1):
     held = jnp.concatenate(pieces)
-    return [held, lax.ppermute(held, "seq", SWAP)]
+    size = held.shape[0] // parts
+    held = [held[at * size : (at + 1) * size] for at in range(parts)]
+    return held + [lax.ppermute(part, "seq", SWAP) for part in held]
 
 
 def gather_plane(held):
@@ -264,10 +266,15 @@
         ref[at, i * HALF : (i + 1) * HALF, :] = part.astype(ref.dtype)
 
 
+def first_part(hidden):
+    return hidden // 2
+
+
 def pack_kernel(core_ref, in_ref, param_ref, out_ref, up_ref, down_ref, *rest):
     vectors, (a_ref, b_ref, param, small, sem) = rest[:5], rest[5:]
     rows, feats = in_ref.shape
-    half = up_ref.shape[1] // 2
+    cut = first_part(up_ref.shape[1])
+    left = up_ref.shape[1] - cut
     copies = [
         pltpu.make_async_copy(in_ref, a_ref.at[:, pl.ds(0, feats)], sem),
         pltpu.make_async_copy(param_ref, param, sem),
@@ -275,9 +282,9 @@
     for i, vector in enumerate(vectors):
         copies.append(pltpu.make_async_copy(vector, small.at[i], sem))
     for source, start, size, target, at in (
-        (out_ref, 0, feats, a_ref, PACK), (up_ref, 0, half, a_ref, PACK + feats),
-        (down_ref, 0, half, a_ref, PACK + feats + half), (up_ref, half, half, b_ref, 0),
-        (down_ref, half, half, b_ref, half),
+        (out_ref, 0, feats, a_ref, PACK), (up_ref, 0, cut, a_ref, PACK + feats),
+        (down_ref, 0, cut, a_ref, PACK + feats + cut), (up_ref, cut, left, b_ref, 0),
+        (down_ref, cut, left, b_ref, left),
     ):
         copies.append(
             pltpu.make_async_copy(
@@ -405,9 +412,10 @@
     length = normed_ref.shape[0]
     count = hidden_ref.shape[1]
     for at in range(0, count, WIDE):
-        columns = slice(at, at + WIDE)
-        up = weights[:, up_at + at : up_at + at + WIDE]
-        down = weights[:, down_at + at : down_at + at + WIDE]
+        wide = min(WIDE, count - at)
+        columns = slice(at, at + wide)
+        up = weights[:, up_at + at : up_at + at + wide]
+        down = weights[:, down_at + at : down_at + at + wide]
         for row in range(0, length, TILE):
             rows = slice(row, row + TILE)
             up_val = dot(normed_ref[rows, :], up)
@@ -415,8 +423,8 @@
             cdf, pdf = normal_parts(up_val)
             hidden_ref[rows, columns] = (up_val * cdf).astype(BF16)
             grad_up_ref[rows, columns] = (grad_hidden * (cdf + up_val * pdf)).astype(BF16)
-        put_rows(grad_refs, slice(at, at + WIDE), dot(normed_t_ref[...], grad_up_ref[:, columns]), place)
-        put_rows(grad_refs, slice(count + at, count + at + WIDE), dot(cot_t_ref[...], hidden_ref[:, columns]), place)
+        put_rows(grad_refs, slice(at, at + wide), dot(normed_t_ref[...], grad_up_ref[:, columns]), place)
+        put_rows(grad_refs, slice(count + at, count + at + wide), dot(cot_t_ref[...], hidden_ref[:, columns]), place)
 
 
 def middle_first_kernel(
@@ -462,14 +470,14 @@
     weights_b, mid_grad_ref, vec_grad_ref, pre_grad_ref, halo_ref,
 ):
     length, feats = xhat_ref.shape
-    count = up_a_ref.shape[1]
+    count, left = up_a_ref.shape[1], up_b_ref.shape[1]
     gain = vec_ref[3:4, :]
     gain_grad = jnp.zeros((8, feats), F32)
     bias_grad = jnp.zeros((8, feats), F32)
     per = BLOCK // POOL
     for at in range(length // BLOCK):
         grad_normed = dot(up_a_ref[span(at), :], weights_a[:, feats : feats + count], NT)
-        grad_normed = grad_normed + dot(up_b_ref[span(at), :], weights_b[:, :count], NT)
+        grad_normed = grad_normed + dot(up_b_ref[span(at), :], weights_b[:, :left], NT)
         xhat = xhat_ref[span(at), :]
         bias_grad = bias_grad + jnp.sum(grad_normed.reshape(BLOCK // 8, 8, feats), axis=0)
         gain_grad = gain_grad + jnp.sum((grad_normed * xhat).reshape(BLOCK // 8, 8, feats), axis=0)
@@ -492,10 +500,10 @@
 
 def output_kernel(mid_ref, hidden_a_ref, hidden_b_ref, weights_a, weights_b, out_ref):
     length, feats = mid_ref.shape
-    count = hidden_a_ref.shape[1]
+    count, left = hidden_a_ref.shape[1], hidden_b_ref.shape[1]
     for at in range(length // BLOCK):
         total = mid_ref[span(at), :] + dot(hidden_a_ref[span(at), :], weights_a[:, feats + count :], NT)
-        total = total + dot(hidden_b_ref[span(at), :], weights_b[:, count:], NT)
+        total = total + dot(hidden_b_ref[span(at), :], weights_b[:, left:], NT)
         out_ref[span(at), :] = total.astype(BF16)
 
 
@@ -575,20 +583,20 @@
         )
 
 
-def final_kernel(param_ref, scale_ref, wide_ref, *rest):
+def final_kernel(n_mlp, param_ref, scale_ref, wide_ref, *rest):
     sources, outs = rest[: len(rest) - 10], rest[len(rest) - 10 :]
-    count = len(sources) // 2
     up_ref, down_ref, in_ref, out_ref, param_grad_ref = outs[:5]
     totals = []
-    for group in range(2):
-        total = sources[group * count][...].astype(F32)
-        for k in range(1, count):
-            total = total + sources[group * count + k][...].astype(F32)
+    for group in (sources[:n_mlp], sources[n_mlp:]):
+        total = group[0][...].astype(F32)
+        for source in group[1:]:
+            total = total + source[...].astype(F32)
         totals.append(total)
     mlp, mixer = totals
-    half = mlp.shape[1] // 4
-    up_ref[:, :half], up_ref[:, half:] = mlp[:, :half], mlp[:, 2 * half : 3 * half]
-    down_ref[:, :half], down_ref[:, half:] = mlp[:, half : 2 * half], mlp[:, 3 * half :]
+    hidden = mlp.shape[1] // 2
+    cut = first_part(hidden)
+    up_ref[:, :cut], up_ref[:, cut:] = mlp[:, :cut], mlp[:, 2 * cut : cut + hidden]
+    down_ref[:, :cut], down_ref[:, cut:] = mlp[:, cut : 2 * cut], mlp[:, cut + hidden :]
     feats = in_ref.shape[1]
     in_ref[...] = mixer[:, :feats]
     out_ref[...] = mixer[:, feats : 2 * feats]
@@ -643,7 +651,8 @@
 ):
     _, length, feats = block_input.shape
     hidden = up_proj.shape[1]
-    half = hidden // 2
+    cut = first_part(hidden)
+    left = hidden - cut
     blocks = length // BLOCK
     pooled = length // POOL
     taps = TAPS * SCALES
@@ -655,7 +664,7 @@
     shard, shard_b = call(
         pack_kernel,
         [core_at, in_proj, kernel_param, out_proj, up_proj, down_proj, *vectors],
-        [((own_rows, PACK + feats + 2 * half), BF16), ((own_rows, 2 * half), BF16)],
+        [((own_rows, PACK + feats + 2 * cut), BF16), ((own_rows, 2 * left), BF16)],
         [
             pltpu.VMEM(kernel_param.shape, BF16), pltpu.VMEM((5, 1, own_rows), BF16),
             pltpu.SemaphoreType.DMA,
@@ -722,7 +731,13 @@
         spaces=[smem] + [pltpu.VMEM] * (11 + n_first),
     )
     got_b = [from_line(held_b, step) for step in steps[-1:]]
-    pieces_a = in_order(gather_core(list(tie(tuple(pieces_a), act))), False)
+    *pieces_a, act = lax.optimization_barrier((*pieces_a, act))
+    pieces_a = in_order(gather_core(pieces_a, 4), False)
+    *got_b, act = lax.optimization_barrier((*got_b, act))
+    for got in got_b:
+        held_b = paired(held_b, got)
+    held_b = held_b.reshape((-1,) + held_b.shape[2:])
+    pieces_b = in_order(gather_core([held_b]), True)
     n_a = len(pieces_a)
     rows = own_rows
 
@@ -739,35 +754,31 @@
         [core_at, act, x_own, cot, cot_t, vec, *pieces_a],
         [
             ((feats, feats), BF16), token_f32, token_f32, ((length, 128), F32), token_bf16,
-            ((feats, length), BF16), ((length, half), BF16), ((length, half), BF16),
-            ((feats, feats + 2 * half), BF16), *grad_shapes(2 * half),
+            ((feats, length), BF16), ((length, cut), BF16), ((length, cut), BF16),
+            ((feats, feats + 2 * cut), BF16), *grad_shapes(2 * cut),
         ],
         flops=8 << 30,
         spaces=[smem] + [vmem] * (5 + n_a),
     )
-    for got in got_b:
-        held_b = paired(held_b, tie(got, mid))
-    held_b = held_b.reshape((-1,) + held_b.shape[2:])
-    pieces_b = in_order(gather_core([held_b]), True)
     n_b = len(pieces_b)
     hidden_b, grad_up_b, weights_b, *grads_b = call(
         lambda *refs: middle_second_kernel(n_b, *refs),
         [core_at, cot, cot_t, normed, normed_t, *pieces_b],
-        [((length, half), BF16), ((length, half), BF16), ((feats, 2 * half), BF16), *grad_shapes(2 * half)],
-        flops=5 << 24,
+        [((length, left), BF16), ((length, left), BF16), ((feats, 2 * left), BF16), *grad_shapes(2 * left)],
+        flops=16 << 30,
         spaces=[smem] + [vmem] * (4 + n_b),
     )
-    near_a = reduce_core(grads_a)
+    near_a = reduce_core(grads_a, hidden_b)
     grad_up_b = tie(grad_up_b, *near_a)
     spread_a = spread_near(near_a)
     grad_mid, vec_grad, grad_pre, halo = call(
         middle_third_kernel,
         [slope, cot, vec, pool_rows, proj_out, xhat_two, inv_two, grad_up_a, grad_up_b, weights_a, weights_b],
         [token_f32, ((8, feats), F32), token_bf16, ((BLOCK + pooled, feats), BF16)],
-        flops=4 << 24,
+        flops=4 << 30,
     )
     after = lax.ppermute(halo, "seq", [(1, 0)])
-    near_b = reduce_core(grads_b)
+    near_b = reduce_core(grads_b, grad_mid)
     grad_pre = tie(grad_pre, *near_b)
     spread_b = spread_near(near_b)
     out_grad, tap_grad, z_grad = call(
@@ -795,18 +806,27 @@
         input_kernel, [grad_mixed, weights, vec, xhat, inv_one, grad_mid], [token_f32], flops=2 << 24
     )
     part_a = add_up(tie(tuple(spread_a), grad_mixed), BF16)
-    part_b = add_up(tie(tuple(spread_b), grad_mixed), BF16)
+    part_b = add_up(tie(tuple(spread_b), input_grad), BF16)
     part_ab = jnp.concatenate([part_a, part_b], axis=2)
-    far_ab = spread_far(part_ab)
-    near_c = reduce_core(grads_c, part_ab, input_grad)
+    steps_ab = far_steps()[::-1]
+    pairs = part_ab.reshape((-1, 2) + part_ab.shape[1:])
+    far_ab = [pairs[:, 0], from_line(pairs[:, 1], steps_ab[0])] if steps_ab else [part_ab]
+    near_c = reduce_core(grads_c, input_grad)
     spread_c = spread_near(near_c)
     (block_output,) = call(
         output_kernel, [tie(mid, *near_c), hidden_a, hidden_b, weights_a, weights_b], [token_bf16], flops=4 << 24
     )
     far_c = spread_far(add_up(tie(tuple(spread_c), block_output), BF16))
+    if steps_ab:
+        far_ab = [far_ab[0], tie(far_ab[1], block_output)]
+    for step in steps_ab[1:]:
+        held = add_up(far_ab, BF16)
+        pairs = held.reshape((-1, 2) + held.shape[1:])
+        far_ab = [pairs[:, 0], from_line(pairs[:, 1], step)]
+    far_ab = [term[0] for term in far_ab]
     vector = ((1, rows), F32)
     up_sum, down_sum, in_sum, out_sum, param_sum, *vectors = call(
-        final_kernel,
+        lambda *refs: final_kernel(len(far_ab), *refs),
         [kernel_param, jnp.asarray(scale_np), jnp.asarray(wide_np), *far_ab, *far_c],
         [
             ((rows, hidden), F32), ((rows, hidden), F32), ((rows, feats), F32), ((rows, feats), F32),

time: 121 us -> 116 us (0.959)
  waiting for transfers between devices: 27.8 us -> 20.3 us
    ppermute x4 -> x6, starting transfers between devices: 8.42 us -> 13 us  [from_line(): return lax.ppermute(held, 'dp', swap_route(dp_count, step * nxy))]
    ppermute x6 -> x3, starting transfers between devices: 8.91 us -> 4.45 us  [spread_far(): lax.ppermute(part[k], 'dp', swap_route(dp_count, k * nxy))]
    ppermute x3 -> x6, waiting for transfers between devices: 4.44 us -> 0.02 us  [gather_core(): return held + [lax.ppermute(part, 'seq', SWAP) for part in held]]
    ppermute x6 -> x3, waiting for transfers between devices: 6.11 us -> 2.94 us  [spread_far(): lax.ppermute(part[k], 'dp', swap_route(dp_count, k * nxy))]
    ppermute x4 -> x6, waiting for transfers between devices: 9.49 us -> 9.31 us  [from_line(): return lax.ppermute(held, 'dp', swap_route(dp_count, step * nxy))]
  transfers between devices with their start and end apart: 37 -> 39, of which waited for: 12 -> 12; matrix products, arithmetic and copies ran while one was open for 2% -> 2% of each run, Pallas kernels for 36% -> 37%
where the time goes in v1:
time: 116 us
  starting transfers between devices  46.9 us (40%)
  Pallas kernels  43.9 us (38%)
  waiting for transfers between devices  20.3 us (18%)
  other arithmetic  1.91 us (2%)
  local copies, waits for them, and re-layouts  1.76 us (2%)
  between operations  1.16 us (1%)
    pallas_call x12, Pallas kernels, call(): pl.pallas_call(kernel, out_shape=[jax.ShapeDtypeStruct(shape, dtype) for...  43.9 us
    ppermute x6, starting transfers between devices, from_line(): return lax.ppermute(held, 'dp', swap_route(dp_count, step * nxy))  13 us
    ppermute x9, starting transfers between devices, spread_near(): lax.ppermute(pieces[k], 'dp', swap_route(dp_count, k))  10.7 us
    ppermute x6, waiting for transfers between devices, from_line(): return lax.ppermute(held, 'dp', swap_route(dp_count, step * nxy))  9.31 us
    ppermute x3, starting transfers between devices, spread_far(): lax.ppermute(part[k], 'dp', swap_route(dp_count, k * nxy))  4.45 us
    ppermute x2, waiting for transfers between devices, gather_plane(): by_y = lax.ppermute(held, 'dp', swap_route(dp_count, 2))  4.09 us
    ppermute x3, starting transfers between devices, gather_near(): lax.ppermute(held, 'dp', swap_route(dp_count, k))  3.55 us
    ppermute x2, starting transfers between devices, gather_plane(): by_y = lax.ppermute(held, 'dp', swap_route(dp_count, 2))  3.1 us
  transfers between devices with their start and end apart: 39, of which 12 were waited for; matrix products, arithmetic and copies ran while one was open for 2% of the time, Pallas kernels for 37%

profile of v1, /device:TPU:0, one launch (start us, length us, event | category | flops | bytes accessed | tf_op | source)
XLA Modules:
  0.0 115.9 jit_solution(4516653150374070665)
XLA Ops:
  0.6 2.4 %collective-permute-start = (bf16[1024,512]{1,0:T(8,128)(2,1)}, bf16[1024,512]{1,0:T(8,128)(2,1)S(1)}, u32[]{:S(2)}, u32[]{:S(2)}) collective-permute-start(bf16[1024,512]{1,0:T(8,128)(2,1)} %bitcast.64), channel_id=1, source_target_pairs={{0,1},{2,3},{4,5},{6,7},{8,9},{10,11},{12,13},{14,15},{16,17},{18,... | collective-permute-start | bytes 3145736 | tf_op jit(solution)/shard_map/ppermute | solution.py:662
  3.2 1.6 %shard_map.292 = (bf16[16,3328]{1,0:T(8,128)(2,1)S(1)}, bf16[16,2048]{1,0:T(8,128)(2,1)S(1)}) custom-call(s32[2]{0:T(128)S(1)} %pad_add_fusion.core_ref.refs_0_, bf16[16,512]{1,0:T(8,128)(2,1)} %in_ref.1, bf16[16,192]{1,0:T(8,128)(2,1)} %refs_0_.1, bf16[16,512]{1,0:T(8,128)(2,1)} %out_ref.1, bf16[16,2048]{1,0:T(8,128)(2,1)} %up_ref.1, ...), custom_call_target="tpu_custom_call" | custom-call | bytes 65536 | tf_op jit(solution)/shard_map/pallas_call | solution.py:627
  4.8 3.5 %collective-permute-start.6 = (bf16[1,16,3328]{2,1,0:T(8,128)(2,1)S(1)}, bf16[1,16,3328]{2,1,0:T(8,128)(2,1)S(1)}, u32[]{:S(2)}, u32[]{:S(2)}) collective-permute-start(bf16[1,16,3328]{2,1,0:T(8,128)(2,1)S(1)} %bitcast.74), channel_id=1, source_target_pairs={{0,16},{2,18},{4,20},{6,22},{8,24},{10,26},{12,28},{14,30},{16,0},... | collective-permute-start | bytes 319496 | tf_op jit(solution)/shard_map/ppermute | solution.py:83
  8.3 2.4 %shard_map.294 = (bf16[1024,512]{1,0:T(8,128)(2,1)S(1)}, f32[1024,128]{1,0:T(8,128)S(1)}, bf16[512,1024]{1,0:T(8,128)(2,1)S(1)}) custom-call(bf16[1024,512]{1,0:T(8,128)(2,1)} %bitcast.65, bf16[1024,512]{1,0:T(8,128)(2,1)} %bitcast.67), custom_call_target="tpu_custom_call" | custom-call | bytes 65536 | tf_op jit(solution)/shard_map/pallas_call | solution.py:627
  10.7 2.3 %collective-permute-done.6 = bf16[1,16,3328]{2,1,0:T(8,128)(2,1)S(1)} collective-permute-done((bf16[1,16,3328]{2,1,0:T(8,128)(2,1)S(1)}, bf16[1,16,3328]{2,1,0:T(8,128)(2,1)S(1)}, u32[]{:S(2)}, u32[]{:S(2)}) %collective-permute-start.6) | collective-permute-done | bytes 106528 | tf_op jit(solution)/shard_map/ppermute | solution.py:83
  27.1 3.4 %collective-permute-start.4 = (bf16[1,4,16,2048]{3,2,1,0:T(8,128)(2,1)S(1)}, bf16[1,4,16,2048]{3,2,1,0:T(8,128)(2,1)S(1)}, u32[]{:S(2)}, u32[]{:S(2)}) collective-permute-start(bf16[1,4,16,2048]{3,2,1,0:T(8,128)(2,1)S(1)} %get-tuple-element.191), channel_id=1, source_target_pairs={{0,16},{2,18},{4,20},{6,22},{8,24},{10,26},{12,28},{14,30},{16,0},... | collective-permute-start | bytes 786440 | tf_op jit(solution)/shard_map/ppermute | solution.py:83
  30.7 2.8 %collective-permute-done.9.refs_8_ = bf16[4,16,2560]{2,1,0:T(8,128)(2,1)S(1)} collective-permute-done((bf16[4,16,2560]{2,1,0:T(8,128)(2,1)S(1)}, bf16[4,16,2560]{2,1,0:T(8,128)(2,1)S(1)}, u32[]{:S(2)}, u32[]{:S(2)}) %collective-permute-start.9) | collective-permute-done | bytes 327712 | tf_op jit(solution)/shard_map/ppermute | solution.py:120
  35.7 3.0 %collective-permute-done.4 = bf16[1,4,16,2048]{3,2,1,0:T(8,128)(2,1)S(1)} collective-permute-done((bf16[1,4,16,2048]{3,2,1,0:T(8,128)(2,1)S(1)}, bf16[1,4,16,2048]{3,2,1,0:T(8,128)(2,1)S(1)}, u32[]{:S(2)}, u32[]{:S(2)}) %collective-permute-start.4) | collective-permute-done | bytes 262176 | tf_op jit(solution)/shard_map/ppermute | solution.py:83
  39.7 7.2 %shard_map.295 = (bf16[512,768]{1,0:T(8,128)(2,1)S(1)}, f32[8,512]{1,0:T(8,128)S(1)}, bf16[512,512]{1,0:T(8,128)(2,1)S(1)}, bf16[512,512]{1,0:T(8,128)(2,1)S(1)}...) custom-call(s32[2]{0:T(128)S(1)} %pad_add_fusion.core_ref.refs_0_, ...), custom_call_target="tpu_custom_call" | custom-call | flops 6442450944 | bytes 65536 | tf_op jit(solution)/shard_map/pallas_call | solution.py:627
  48.0 3.0 %collective-permute-done.5 = bf16[2,4,16,2048]{3,2,1,0:T(8,128)(2,1)S(1)} collective-permute-done((bf16[2,4,16,2048]{3,2,1,0:T(8,128)(2,1)S(1)}, bf16[2,4,16,2048]{3,2,1,0:T(8,128)(2,1)S(1)}, u32[]{:S(2)}, u32[]{:S(2)}) %collective-permute-start.5) | collective-permute-done | bytes 524320 | tf_op jit(solution)/shard_map/ppermute | solution.py:83
  52.6 7.2 %shard_map.296 = (bf16[512,512]{1,0:T(8,128)(2,1)S(1)}, f32[1024,512]{1,0:T(8,128)S(1)}, f32[1024,512]{1,0:T(8,128)S(1)}, f32[1024,128]{1,0:T(8,128)S(1)}, bf16[...) custom-call(s32[2]{0:T(128)S(1)} %pad_add_fusion.core_ref.refs_0_, ...), custom_call_target="tpu_custom_call" | custom-call | flops 8589934592 | bytes 65536 | tf_op jit(solution)/shard_map/pallas_call | solution.py:627
  59.9 6.2 %shard_map.297 = (bf16[1024,1024]{1,0:T(8,128)(2,1)S(1)}, bf16[1024,1024]{1,0:T(8,128)(2,1)S(1)}, bf16[512,2048]{1,0:T(8,128)(2,1)S(1)}, bf16[16,16,2048]{2,1,0:T(8,128)(2,1)S(1)}, bf16[16,16,2048]{2,1,0:T(8,128)(2,1)S(1)}) custom-call(s32[2]{0:T(128)S(1)} %pad_add_fusion.core_ref.refs_0_, bf16[1024,512]{1,0:T(8,128)(2,1)S(1)} %bitcast.69, ...), custom_call_target="tpu_custom_call" | custom-call | flops 17179869184 | bytes 65536 | tf_op jit(solution)/shard_map/pallas_call | solution.py:627
  67.2 2.2 %collective-permute-start.27 = (bf16[4,16,2048]{2,1,0:T(8,128)(2,1)S(1)}, bf16[4,16,2048]{2,1,0:T(8,128)(2,1)S(1)}, u32[]{:S(2)}, u32[]{:S(2)}) collective-permute-start(bf16[4,16,2048]{2,1,0:T(8,128)(2,1)S(1)} %get-tuple-element.178), channel_id=1, source_target_pairs={{0,6},{2,4},{4,2},{6,0},{8,14},{10,12},{12,10},{14,8},{16,22},{18,... | collective-permute-start | bytes 786440 | tf_op jit(solution)/shard_map/ppermute | solution.py:175
  70.7 4.7 %shard_map.298 = (f32[1024,512]{1,0:T(8,128)S(1)}, f32[8,512]{1,0:T(8,128)S(1)}, bf16[1024,512]{1,0:T(8,128)(2,1)S(1)}, bf16[384,512]{1,0:T(8,128)(2,1)S(1)}) custom-call(bf16[1024,512]{1,0:T(8,128)(2,1)S(1)} %get-tuple-element.111.slope_ref, bf16[1024,512]{1,0:T(8,128)(2,1)S(1)} %bitcast.70, f32[8,512]{1,0:T(8,128)S(1)} %get-tuple-element.104.refs_5_.vec_ref, ...), custom_call_target="tpu_custom_call" | custom-call | flops 4294967296 | bytes 65536 | tf_op jit(solution)/shard_map/pallas_call | solution.py:627
  77.4 2.2 %collective-permute-start.30 = (bf16[4,16,2048]{2,1,0:T(8,128)(2,1)S(1)}, bf16[4,16,2048]{2,1,0:T(8,128)(2,1)S(1)}, u32[]{:S(2)}, u32[]{:S(2)}) collective-permute-start(bf16[4,16,2048]{2,1,0:T(8,128)(2,1)S(1)} %get-tuple-element.174), channel_id=1, source_target_pairs={{0,6},{2,4},{4,2},{6,0},{8,14},{10,12},{12,10},{14,8},{16,22},{18,... | collective-permute-start | bytes 786440 | tf_op jit(solution)/shard_map/ppermute | solution.py:175
  81.0 2.9 %shard_map.299 = (bf16[512,512]{1,0:T(8,128)(2,1)S(1)}, bf16[512,256]{1,0:T(8,128)(2,1)S(1)}, bf16[4,512,512]{2,1,0:T(8,128)(2,1)S(1)}) custom-call(bf16[1024,512]{1,0:T(8,128)(2,1)S(1)} %get-tuple-element.102.refs_1_.act_ref, f32[1024,512]{1,0:T(8,128)S(1)} %get-tuple-element.127.mid_grad_ref, bf16[1024,512]{1,0:T(8,128)(2,1)S(1)} %get-tuple-element.132.pre_grad_ref, ...), custom_call_target="tpu_custom_call" | custom-call | flops 33554432 | bytes 65536 | tf_op jit(solution)/shard_map/pallas_call | solution.py:627
  83.9 4.2 %shard_map.300 = (bf16[1024,512]{1,0:T(8,128)(2,1)S(1)}, bf16[16,16,1408]{2,1,0:T(8,128)(2,1)S(1)}, bf16[16,16,1408]{2,1,0:T(8,128)(2,1)S(1)}) custom-call(s32[2]{0:T(128)S(1)} %pad_add_fusion.core_ref.refs_0_, bf16[4,512,512]{2,1,0:T(8,128)(2,1)S(1)} %get-tuple-element.137.z_ref, bf16[384,512]{1,0:T(8,128)(2,1)S(1)} %get-tuple-element.133.halo_ref, ...), custom_call_target="tpu_custom_call" | custom-call | flops 67108864 | bytes 65536 | tf_op jit(solution)/shard_map/pallas_call | solution.py:627
  88.8 2.5 %shard_map.301 = f32[1024,512]{1,0:T(8,128)} custom-call(bf16[1024,512]{1,0:T(8,128)(2,1)S(1)} %get-tuple-element.146.mixed_grad_ref, bf16[512,768]{1,0:T(8,128)(2,1)S(1)} %get-tuple-element.140.weights, f32[8,512]{1,0:T(8,128)S(1)} %get-tuple-element.104.refs_5_.vec_ref, bf16[1024,512]{1,0:T(8,128)(2,1)S(1)} %get-tuple-element.99.refs_1_.xhat_ref, ...), custom_call_target="tpu_custom_call" | custom-call | flops 33554432 | bytes 65536 | tf_op jit(solution)/shard_map/pallas_call | solution.py:627
  91.2 2.0 %collective-permute-done.29 = bf16[4,16,2048]{2,1,0:T(8,128)(2,1)S(1)} collective-permute-done((bf16[4,16,2048]{2,1,0:T(8,128)(2,1)S(1)}, bf16[4,16,2048]{2,1,0:T(8,128)(2,1)S(1)}, u32[]{:S(2)}, u32[]{:S(2)}) %collective-permute-start.29) | collective-permute-done | bytes 262176 | tf_op jit(solution)/shard_map/ppermute | solution.py:175
  95.5 1.7 %collective-permute-start.35 = (bf16[4,16,1408]{2,1,0:T(8,128)(2,1)S(1)}, bf16[4,16,1408]{2,1,0:T(8,128)(2,1)S(1)}, u32[]{:S(2)}, u32[]{:S(2)}) collective-permute-start(bf16[4,16,1408]{2,1,0:T(8,128)(2,1)S(1)} %get-tuple-element.182), channel_id=1, source_target_pairs={{0,6},{2,4},{4,2},{6,0},{8,14},{10,12},{12,10},{14,8},{16,22},{18,... | collective-permute-start | bytes 540680 | tf_op jit(solution)/shard_map/ppermute | solution.py:175
  99.0 3.3 %shard_map.302 = bf16[1024,512]{1,0:T(8,128)(2,1)} custom-call(f32[1024,512]{1,0:T(8,128)S(1)} %get-tuple-element.149.mid_ref, bf16[1024,1024]{1,0:T(8,128)(2,1)S(1)} %get-tuple-element.150.hidden_a_ref, bf16[1024,1024]{1,0:T(8,128)(2,1)S(1)} %get-tuple-element.122.hidden_b_ref, bf16[512,2560]{1,0:T(8,128)(2,1)S(1)} %get-tuple-element.125.weights_a, ...), custom_call_target="tpu_custom_call" | custom-call | flops 67108864 | bytes 65536 | tf_op jit(solution)/shard_map/pallas_call | solution.py:627
  102.5 3.4 %collective-permute-start.32 = (bf16[1,16,4096]{2,1,0:T(8,128)(2,1)S(1)}, bf16[1,16,4096]{2,1,0:T(8,128)(2,1)S(1)}, u32[]{:S(2)}, u32[]{:S(2)}) collective-permute-start(bf16[1,16,4096]{2,1,0:T(8,128)(2,1)S(1)} %get-tuple-element.188), channel_id=1, source_target_pairs={{0,16},{2,18},{4,20},{6,22},{8,24},{10,26},{12,28},{14,30},{16,0},... | collective-permute-start | bytes 393224 | tf_op jit(solution)/shard_map/ppermute | solution.py:83
  106.7 3.2 %collective-permute-start.38 = (bf16[16,1408]{1,0:T(8,128)(2,1)S(1)}, bf16[16,1408]{1,0:T(8,128)(2,1)S(1)}, u32[]{:S(2)}, u32[]{:S(2)}) collective-permute-start(bf16[16,1408]{1,0:T(8,128)(2,1)S(1)} %get-tuple-element.194), channel_id=1, source_target_pairs={{0,24},{2,26},{4,28},{6,30},{8,16},{10,18},{12,20},{14,22},{16,8},... | collective-permute-start | bytes 135176 | tf_op jit(solution)/shard_map/ppermute | solution.py:183
  112.7 2.3 %collective-permute-done.37.refs_7_ = bf16[16,1408]{1,0:T(8,128)(2,1)S(1)} collective-permute-done((bf16[16,1408]{1,0:T(8,128)(2,1)S(1)}, bf16[16,1408]{1,0:T(8,128)(2,1)S(1)}, u32[]{:S(2)}, u32[]{:S(2)}) %collective-permute-start.37) | collective-permute-done | bytes 45088 | tf_op jit(solution)/shard_map/ppermute | solution.py:183
  (118 shorter events, 34.9 us)
Async XLA Ops:
  0.6 13.2 %collective-permute-start = (bf16[1024,512]{1,0:T(8,128)(2,1)}, bf16[1024,512]{1,0:T(8,128)(2,1)S(1)}, u32[]{:S(2)}, u32[]{:S(2)}) collective-permute-start(bf16[1024,512]{1,0:T(8,128)(2,1)} %bitcast.64), channel_id=1, source_target_pairs={{0,1},{2,3},{4,5},{6,7},{8,9},{10,11},{12,13},{14,15},{16,17},{18,... | collective-permute-start | bytes 3145736 | tf_op jit(solution)/shard_map/ppermute | solution.py:662
  4.8 8.2 %collective-permute-start.6 = (bf16[1,16,3328]{2,1,0:T(8,128)(2,1)S(1)}, bf16[1,16,3328]{2,1,0:T(8,128)(2,1)S(1)}, u32[]{:S(2)}, u32[]{:S(2)}) collective-permute-start(bf16[1,16,3328]{2,1,0:T(8,128)(2,1)S(1)} %bitcast.74), channel_id=1, source_target_pairs={{0,16},{2,18},{4,20},{6,22},{8,24},{10,26},{12,28},{14,30},{16,0},... | collective-permute-start | bytes 319496 | tf_op jit(solution)/shard_map/ppermute | solution.py:83
  16.1 8.0 %collective-permute-start.1 = (bf16[1,16,2048]{2,1,0:T(8,128)(2,1)S(1)}, bf16[1,16,2048]{2,1,0:T(8,128)(2,1)S(1)}, u32[]{:S(2)}, u32[]{:S(2)}) collective-permute-start(bf16[1,16,2048]{2,1,0:T(8,128)(2,1)S(1)} %bitcast.77), channel_id=1, source_target_pairs={{0,2},{2,0},{4,6},{6,4},{8,10},{10,8},{12,14},{14,12},{16,18},{18,... | collective-permute-start | bytes 196616 | tf_op jit(solution)/shard_map/ppermute | solution.py:119
  22.1 8.4 %collective-permute-start.13 = (bf16[4,16,768]{2,1,0:T(8,128)(2,1)S(1)}, bf16[4,16,768]{2,1,0:T(8,128)(2,1)S(1)}, u32[]{:S(2)}, u32[]{:S(2)}) collective-permute-start(bf16[4,16,768]{2,1,0:T(8,128)(2,1)S(1)} %slice.75), channel_id=1, source_target_pairs={{0,4},{2,6},{4,0},{6,2},{8,12},{10,14},{12,8},{14,10},{16,20},{18,... | collective-permute-start | bytes 294920 | tf_op jit(solution)/shard_map/ppermute | solution.py:104
  24.1 9.4 %collective-permute-start.9 = (bf16[4,16,2560]{2,1,0:T(8,128)(2,1)S(1)}, bf16[4,16,2560]{2,1,0:T(8,128)(2,1)S(1)}, u32[]{:S(2)}, u32[]{:S(2)}) collective-permute-start(bf16[4,16,2560]{2,1,0:T(8,128)(2,1)S(1)} %slice.72.refs_6_), channel_id=1, source_target_pairs={{0,4},{2,6},{4,0},{6,2},{8,12},{10,14},{12,8},{14,10},{16,20},{18,... | collective-permute-start | bytes 983048 | tf_op jit(solution)/shard_map/ppermute | solution.py:120
  25.7 8.7 %collective-permute-start.8 = (bf16[4,16,2560]{2,1,0:T(8,128)(2,1)S(1)}, bf16[4,16,2560]{2,1,0:T(8,128)(2,1)S(1)}, u32[]{:S(2)}, u32[]{:S(2)}) collective-permute-start(bf16[4,16,2560]{2,1,0:T(8,128)(2,1)S(1)} %slice.72.refs_6_), channel_id=1, source_target_pairs={{0,2},{2,0},{4,6},{6,4},{8,10},{10,8},{12,14},{14,12},{16,18},{18,... | collective-permute-start | bytes 983048 | tf_op jit(solution)/shard_map/ppermute | solution.py:119
  27.1 11.6 %collective-permute-start.4 = (bf16[1,4,16,2048]{3,2,1,0:T(8,128)(2,1)S(1)}, bf16[1,4,16,2048]{3,2,1,0:T(8,128)(2,1)S(1)}, u32[]{:S(2)}, u32[]{:S(2)}) collective-permute-start(bf16[1,4,16,2048]{3,2,1,0:T(8,128)(2,1)S(1)} %get-tuple-element.191), channel_id=1, source_target_pairs={{0,16},{2,18},{4,20},{6,22},{8,24},{10,26},{12,28},{14,30},{16,0},... | collective-permute-start | bytes 786440 | tf_op jit(solution)/shard_map/ppermute | solution.py:83
  30.6 9.0 %collective-permute-start.15 = (bf16[16,16,768]{2,1,0:T(8,128)(2,1)S(1)}, bf16[16,16,768]{2,1,0:T(8,128)(2,1)S(1)}, u32[]{:S(2)}, u32[]{:S(2)}) collective-permute-start(bf16[16,16,768]{2,1,0:T(8,128)(2,1)S(1)} %pad_maximum_fusion.4.refs_12_), channel_id=1, source_target_pairs={{0,1},{1,0},{2,3},{3,2},{4,5},{5,4},{6,7},{7,6},{8,9},{9,8},{10,11... | collective-permute-start | bytes 1179656 | tf_op jit(solution)/shard_map/ppermute | solution.py:111
  33.5 13.4 %collective-permute-start.10 = (bf16[2,16,2560]{2,1,0:T(8,128)(2,1)S(1)}, bf16[2,16,2560]{2,1,0:T(8,128)(2,1)S(1)}, u32[]{:S(2)}, u32[]{:S(2)}) collective-permute-start(bf16[2,16,2560]{2,1,0:T(8,128)(2,1)S(1)} %slice.96), channel_id=1, source_target_pairs={{0,2},{2,0},{4,6},{6,4},{8,10},{10,8},{12,14},{14,12},{16,18},{18,... | collective-permute-start | bytes 491528 | tf_op jit(solution)/shard_map/ppermute | solution.py:125
  34.4 12.6 %collective-permute-start.11 = (bf16[2,16,2560]{2,1,0:T(8,128)(2,1)S(1)}, bf16[2,16,2560]{2,1,0:T(8,128)(2,1)S(1)}, u32[]{:S(2)}, u32[]{:S(2)}) collective-permute-start(bf16[2,16,2560]{2,1,0:T(8,128)(2,1)S(1)} %slice.97), channel_id=1, source_target_pairs={{0,4},{2,6},{4,0},{6,2},{8,12},{10,14},{12,8},{14,10},{16,20},{18,... | collective-permute-start | bytes 491528 | tf_op jit(solution)/shard_map/ppermute | solution.py:126
  38.8 12.2 %collective-permute-start.5 = (bf16[2,4,16,2048]{3,2,1,0:T(8,128)(2,1)S(1)}, bf16[2,4,16,2048]{3,2,1,0:T(8,128)(2,1)S(1)}, u32[]{:S(2)}, u32[]{:S(2)}) collective-permute-start(bf16[2,4,16,2048]{3,2,1,0:T(8,128)(2,1)S(1)} %get-tuple-element.187), channel_id=1, source_target_pairs={{0,8},{2,10},{4,12},{6,14},{8,0},{10,2},{12,4},{14,6},{16,24},{18,... | collective-permute-start | bytes 1572872 | tf_op jit(solution)/shard_map/ppermute | solution.py:83
  51.3 8.7 %collective-permute-start.20 = (bf16[16,16,2048]{2,1,0:T(8,128)(2,1)S(1)}, bf16[16,16,2048]{2,1,0:T(8,128)(2,1)S(1)}, u32[]{:S(2)}, u32[]{:S(2)}) collective-permute-start(bf16[16,16,2048]{2,1,0:T(8,128)(2,1)S(1)} %bitcast.71), channel_id=1, source_target_pairs={{0,1},{1,0},{2,3},{3,2},{4,5},{5,4},{6,7},{7,6},{8,9},{9,8},{10,11... | collective-permute-start | bytes 3145736 | tf_op jit(solution)/shard_map/ppermute | solution.py:111
  66.1 10.8 %collective-permute-start.22 = (bf16[16,16,2048]{2,1,0:T(8,128)(2,1)S(1)}, bf16[16,16,2048]{2,1,0:T(8,128)(2,1)S(1)}, u32[]{:S(2)}, u32[]{:S(2)}) collective-permute-start(bf16[16,16,2048]{2,1,0:T(8,128)(2,1)S(1)} %get-tuple-element.130), channel_id=1, source_target_pairs={{0,1},{1,0},{2,3},{3,2},{4,5},{5,4},{6,7},{7,6},{8,9},{9,8},{10,11... | collective-permute-start | bytes 3145736 | tf_op jit(solution)/shard_map/ppermute | solution.py:166
  67.2 12.5 %collective-permute-start.27 = (bf16[4,16,2048]{2,1,0:T(8,128)(2,1)S(1)}, bf16[4,16,2048]{2,1,0:T(8,128)(2,1)S(1)}, u32[]{:S(2)}, u32[]{:S(2)}) collective-permute-start(bf16[4,16,2048]{2,1,0:T(8,128)(2,1)S(1)} %get-tuple-element.178), channel_id=1, source_target_pairs={{0,6},{2,4},{4,2},{6,0},{8,14},{10,12},{12,10},{14,8},{16,22},{18,... | collective-permute-start | bytes 786440 | tf_op jit(solution)/shard_map/ppermute | solution.py:175
  69.3 18.8 %collective-permute-start.26 = (bf16[4,16,2048]{2,1,0:T(8,128)(2,1)S(1)}, bf16[4,16,2048]{2,1,0:T(8,128)(2,1)S(1)}, u32[]{:S(2)}, u32[]{:S(2)}) collective-permute-start(bf16[4,16,2048]{2,1,0:T(8,128)(2,1)S(1)} %get-tuple-element.179), channel_id=1, source_target_pairs={{0,4},{2,6},{4,0},{6,2},{8,12},{10,14},{12,8},{14,10},{16,20},{18,... | collective-permute-start | bytes 786440 | tf_op jit(solution)/shard_map/ppermute | solution.py:175
  70.2 17.9 %collective-permute-start.25 = (bf16[4,16,2048]{2,1,0:T(8,128)(2,1)S(1)}, bf16[4,16,2048]{2,1,0:T(8,128)(2,1)S(1)}, u32[]{:S(2)}, u32[]{:S(2)}) collective-permute-start(bf16[4,16,2048]{2,1,0:T(8,128)(2,1)S(1)} %get-tuple-element.180), channel_id=1, source_target_pairs={{0,2},{2,0},{4,6},{6,4},{8,10},{10,8},{12,14},{14,12},{16,18},{18,... | collective-permute-start | bytes 786440 | tf_op jit(solution)/shard_map/ppermute | solution.py:175
  77.4 13.8 %collective-permute-start.30 = (bf16[4,16,2048]{2,1,0:T(8,128)(2,1)S(1)}, bf16[4,16,2048]{2,1,0:T(8,128)(2,1)S(1)}, u32[]{:S(2)}, u32[]{:S(2)}) collective-permute-start(bf16[4,16,2048]{2,1,0:T(8,128)(2,1)S(1)} %get-tuple-element.174), channel_id=1, source_target_pairs={{0,6},{2,4},{4,2},{6,0},{8,14},{10,12},{12,10},{14,8},{16,22},{18,... | collective-permute-start | bytes 786440 | tf_op jit(solution)/shard_map/ppermute | solution.py:175
  79.6 13.7 %collective-permute-start.29 = (bf16[4,16,2048]{2,1,0:T(8,128)(2,1)S(1)}, bf16[4,16,2048]{2,1,0:T(8,128)(2,1)S(1)}, u32[]{:S(2)}, u32[]{:S(2)}) collective-permute-start(bf16[4,16,2048]{2,1,0:T(8,128)(2,1)S(1)} %get-tuple-element.175), channel_id=1, source_target_pairs={{0,4},{2,6},{4,0},{6,2},{8,12},{10,14},{12,8},{14,10},{16,20},{18,... | collective-permute-start | bytes 786440 | tf_op jit(solution)/shard_map/ppermute | solution.py:175
  80.5 13.0 %collective-permute-start.28 = (bf16[4,16,2048]{2,1,0:T(8,128)(2,1)S(1)}, bf16[4,16,2048]{2,1,0:T(8,128)(2,1)S(1)}, u32[]{:S(2)}, u32[]{:S(2)}) collective-permute-start(bf16[4,16,2048]{2,1,0:T(8,128)(2,1)S(1)} %get-tuple-element.176), channel_id=1, source_target_pairs={{0,2},{2,0},{4,6},{6,4},{8,10},{10,8},{12,14},{14,12},{16,18},{18,... | collective-permute-start | bytes 786440 | tf_op jit(solution)/shard_map/ppermute | solution.py:175
  94.0 8.4 %collective-permute-start.31 = (bf16[2,16,4096]{2,1,0:T(8,128)(2,1)S(1)}, bf16[2,16,4096]{2,1,0:T(8,128)(2,1)S(1)}, u32[]{:S(2)}, u32[]{:S(2)}) collective-permute-start(bf16[2,16,4096]{2,1,0:T(8,128)(2,1)S(1)} %slice_bitcast_fusion), channel_id=1, source_target_pairs={{0,8},{2,10},{4,12},{6,14},{8,0},{10,2},{12,4},{14,6},{16,24},{18,... | collective-permute-start | bytes 786440 | tf_op jit(solution)/shard_map/ppermute | solution.py:83
  95.5 10.4 %collective-permute-start.35 = (bf16[4,16,1408]{2,1,0:T(8,128)(2,1)S(1)}, bf16[4,16,1408]{2,1,0:T(8,128)(2,1)S(1)}, u32[]{:S(2)}, u32[]{:S(2)}) collective-permute-start(bf16[4,16,1408]{2,1,0:T(8,128)(2,1)S(1)} %get-tuple-element.182), channel_id=1, source_target_pairs={{0,6},{2,4},{4,2},{6,0},{8,14},{10,12},{12,10},{14,8},{16,22},{18,... | collective-permute-start | bytes 540680 | tf_op jit(solution)/shard_map/ppermute | solution.py:175
  97.1 9.4 %collective-permute-start.34 = (bf16[4,16,1408]{2,1,0:T(8,128)(2,1)S(1)}, bf16[4,16,1408]{2,1,0:T(8,128)(2,1)S(1)}, u32[]{:S(2)}, u32[]{:S(2)}) collective-permute-start(bf16[4,16,1408]{2,1,0:T(8,128)(2,1)S(1)} %get-tuple-element.183), channel_id=1, source_target_pairs={{0,4},{2,6},{4,0},{6,2},{8,12},{10,14},{12,8},{14,10},{16,20},{18,... | collective-permute-start | bytes 540680 | tf_op jit(solution)/shard_map/ppermute | solution.py:175
  98.1 8.5 %collective-permute-start.33 = (bf16[4,16,1408]{2,1,0:T(8,128)(2,1)S(1)}, bf16[4,16,1408]{2,1,0:T(8,128)(2,1)S(1)}, u32[]{:S(2)}, u32[]{:S(2)}) collective-permute-start(bf16[4,16,1408]{2,1,0:T(8,128)(2,1)S(1)} %get-tuple-element.184), channel_id=1, source_target_pairs={{0,2},{2,0},{4,6},{6,4},{8,10},{10,8},{12,14},{14,12},{16,18},{18,... | collective-permute-start | bytes 540680 | tf_op jit(solution)/shard_map/ppermute | solution.py:175
  102.5 9.6 %collective-permute-start.32 = (bf16[1,16,4096]{2,1,0:T(8,128)(2,1)S(1)}, bf16[1,16,4096]{2,1,0:T(8,128)(2,1)S(1)}, u32[]{:S(2)}, u32[]{:S(2)}) collective-permute-start(bf16[1,16,4096]{2,1,0:T(8,128)(2,1)S(1)} %get-tuple-element.188), channel_id=1, source_target_pairs={{0,16},{2,18},{4,20},{6,22},{8,24},{10,26},{12,28},{14,30},{16,0},... | collective-permute-start | bytes 393224 | tf_op jit(solution)/shard_map/ppermute | solution.py:83
  (27 other events, 271.2 us)

commit v2 on v1

--- a/solution.py
+++ b/solution.py
@@ -358,15 +358,15 @@
     has_prior = core_ref[0].astype(F32)
     per = BLOCK // POOL
     past = None
+    total = dot((prior_ref[...].astype(F32) * gain + bias).astype(BF16), proj)
     for at in range(blocks):
-        normed = (prior_ref[span(at), :].astype(F32) * gain + bias).astype(BF16)
-        mixed = (dot(normed, proj) * has_prior).astype(BF16)
+        mixed = (total[at * BLOCK : (at + 1) * BLOCK] * has_prior).astype(BF16)
         pooled_ref[span(at, per), :] = dot(pool_rows[...], mixed).astype(BF16)
         if at == blocks - 1:
             past = quarters(dot(basis[...], mixed))
+    total = dot((xhat_ref[...].astype(F32) * gain + bias).astype(BF16), proj)
     for at in range(blocks):
-        normed = (xhat_ref[span(at), :].astype(F32) * gain + bias).astype(BF16)
-        mixed = dot(normed, proj).astype(BF16)
+        mixed = total[at * BLOCK : (at + 1) * BLOCK].astype(BF16)
         mixed_ref[span(at), :] = mixed
         pooled_ref[span(blocks + at, per), :] = dot(pool_rows[...], mixed).astype(BF16)
     pool_win = dot(basis_pool[...], pooled_ref[...])
@@ -498,13 +498,18 @@
     vec_grad_ref[2:8, :] = jnp.zeros((6, feats), F32)
 
 
-def output_kernel(mid_ref, hidden_a_ref, hidden_b_ref, weights_a, weights_b, out_ref):
+def output_kernel(mid_ref, hidden_a_ref, hidden_b_ref, weights_a, weights_b, out_ref, stage, sem):
     length, feats = mid_ref.shape
     count, left = hidden_a_ref.shape[1], hidden_b_ref.shape[1]
+    copies = []
     for at in range(length // BLOCK):
         total = mid_ref[span(at), :] + dot(hidden_a_ref[span(at), :], weights_a[:, feats + count :], NT)
         total = total + dot(hidden_b_ref[span(at), :], weights_b[:, left:], NT)
-        out_ref[span(at), :] = total.astype(BF16)
+        stage[span(at), :] = total.astype(BF16)
+        copies.append(pltpu.make_async_copy(stage.at[span(at), :], out_ref.at[span(at), :], sem.at[at]))
+        copies[-1].start()
+    for copy in copies:
+        copy.wait()
 
 
 def taps_kernel(
@@ -618,7 +623,7 @@
         ref[...] = jnp.sum(jnp.where(diagonal, column, 0.0), axis=0, keepdims=True)
 
 
-def call(kernel, operands, outs, scratch=(), flops=0, spaces=None, limit=12):
+def call(kernel, operands, outs, scratch=(), flops=0, spaces=None, limit=12, out_space=pltpu.VMEM):
     spaces = spaces or [pltpu.VMEM] * len(operands)
     operands = [
         pltpu.with_memory_space_constraint(operand, pltpu.HBM) if space is pltpu.HBM else operand
@@ -628,7 +633,7 @@
         kernel,
         out_shape=[jax.ShapeDtypeStruct(shape, dtype) for shape, dtype in outs],
         in_specs=[pl.BlockSpec(memory_space=space) for space in spaces],
-        out_specs=[pl.BlockSpec(memory_space=pltpu.VMEM)] * len(outs),
+        out_specs=[pl.BlockSpec(memory_space=out_space)] * len(outs),
         scratch_shapes=list(scratch),
         compiler_params=pltpu.CompilerParams(vmem_limit_bytes=limit << 20),
         cost_estimate=pl.CostEstimate(flops=flops, bytes_accessed=1 << 16, transcendentals=0),
@@ -683,14 +688,14 @@
     wide_np = np.zeros((1, 256), np.float32)
     wide_np[0, :taps] = np.repeat(2.0 ** (np.arange(SCALES) % FINE), TAPS)
 
-    xhat, inv_one, cot_t = call(
+    xhat, inv_one, cot_t, cot, x_own = call(
         prepare_kernel,
         [x_own, cot],
-        [((length, feats), BF16), ((length, 128), F32), ((feats, length), BF16)],
         [
-            pltpu.VMEM((length, feats), BF16), pltpu.VMEM((length, feats), BF16),
-            pltpu.SemaphoreType.DMA((2, blocks)),
+            ((length, feats), BF16), ((length, 128), F32), ((feats, length), BF16),
+            ((length, feats), BF16), ((length, feats), BF16),
         ],
+        [pltpu.SemaphoreType.DMA((2, blocks))],
         spaces=[pltpu.HBM] * 2,
     )
     (prior_hat,) = call(prior_kernel, [x_prior], [((length, feats), BF16)])
@@ -814,7 +819,8 @@
     near_c = reduce_core(grads_c, input_grad)
     spread_c = spread_near(near_c)
     (block_output,) = call(
-        output_kernel, [tie(mid, *near_c), hidden_a, hidden_b, weights_a, weights_b], [token_bf16], flops=4 << 24
+        output_kernel, [tie(mid, *near_c), hidden_a, hidden_b, weights_a, weights_b], [token_bf16],
+        [pltpu.VMEM((length, feats), BF16), pltpu.SemaphoreType.DMA((blocks,))], flops=4 << 24, out_space=pltpu.HBM
     )
     far_c = spread_far(add_up(tie(tuple(spread_c), block_output), BF16))
     if steps_ab:

time: 116 us -> 115 us (level)
  waiting for transfers between devices: 20.3 us -> 22.2 us
  local copies, waits for them, and re-layouts: 1.76 us -> 0.52 us
  Pallas kernels: 43.9 us -> 42.7 us
    unnamed x25 -> x21, local copies, waits for them, and re-layouts: 1.29 us -> 0.08 us
  transfers between devices with their start and end apart: 39 -> 39, of which waited for: 12 -> 13; matrix products, arithmetic and copies ran while one was open for 2% -> 2% of each run, Pallas kernels for 37% -> 36%
where the time goes in v2:
time: 115 us
  starting transfers between devices  46.6 us (41%)
  Pallas kernels  42.7 us (37%)
  waiting for transfers between devices  22.2 us (19%)
  other arithmetic  1.91 us (2%)
  between operations  1.16 us (1%)
    pallas_call x12, Pallas kernels, call(): pl.pallas_call(kernel, out_shape=[jax.ShapeDtypeStruct(shape, dtype) for...  42.7 us
    ppermute x6, starting transfers between devices, from_line(): return lax.ppermute(held, 'dp', swap_route(dp_count, step * nxy))  12.7 us
    ppermute x9, starting transfers between devices, spread_near(): lax.ppermute(pieces[k], 'dp', swap_route(dp_count, k))  10.7 us
    ppermute x6, waiting for transfers between devices, from_line(): return lax.ppermute(held, 'dp', swap_route(dp_count, step * nxy))  9.5 us
    ppermute x3, starting transfers between devices, spread_far(): lax.ppermute(part[k], 'dp', swap_route(dp_count, k * nxy))  4.45 us
    ppermute x2, waiting for transfers between devices, gather_plane(): by_y = lax.ppermute(held, 'dp', swap_route(dp_count, 2))  4.09 us
    ppermute x9, waiting for transfers between devices, spread_near(): lax.ppermute(pieces[k], 'dp', swap_route(dp_count, k))  3.85 us
    ppermute x3, waiting for transfers between devices, spread_far(): lax.ppermute(part[k], 'dp', swap_route(dp_count, k * nxy))  3.77 us
  transfers between devices with their start and end apart: 39, of which 13 were waited for; matrix products, arithmetic and copies ran while one was open for 2% of the time, Pallas kernels for 36%

profile of v2, /device:TPU:0, one launch (start us, length us, event | category | flops | bytes accessed | tf_op | source)
XLA Modules:
  0.0 115.0 jit_solution(5984232964794734058)
XLA Ops:
  0.6 2.4 %collective-permute-start = (bf16[1024,512]{1,0:T(8,128)(2,1)}, bf16[1024,512]{1,0:T(8,128)(2,1)S(1)}, u32[]{:S(2)}, u32[]{:S(2)}) collective-permute-start(bf16[1024,512]{1,0:T(8,128)(2,1)} %bitcast.79), channel_id=1, source_target_pairs={{0,1},{2,3},{4,5},{6,7},{8,9},{10,11},{12,13},{14,15},{16,17},{18,... | collective-permute-start | bytes 3145736 | tf_op jit(solution)/shard_map/ppermute | solution.py:667
  3.2 1.6 %shard_map.292 = (bf16[16,3328]{1,0:T(8,128)(2,1)S(1)}, bf16[16,2048]{1,0:T(8,128)(2,1)S(1)}) custom-call(s32[2]{0:T(128)S(1)} %pad_add_fusion.core_ref.refs_0_, bf16[16,512]{1,0:T(8,128)(2,1)} %in_ref.1, bf16[16,192]{1,0:T(8,128)(2,1)} %refs_0_.1, bf16[16,512]{1,0:T(8,128)(2,1)} %out_ref.1, bf16[16,2048]{1,0:T(8,128)(2,1)} %up_ref.1, ...), custom_call_target="tpu_custom_call" | custom-call | bytes 65536 | tf_op jit(solution)/shard_map/pallas_call | solution.py:632
  4.8 3.5 %collective-permute-start.6 = (bf16[1,16,3328]{2,1,0:T(8,128)(2,1)S(1)}, bf16[1,16,3328]{2,1,0:T(8,128)(2,1)S(1)}, u32[]{:S(2)}, u32[]{:S(2)}) collective-permute-start(bf16[1,16,3328]{2,1,0:T(8,128)(2,1)S(1)} %bitcast.67), channel_id=1, source_target_pairs={{0,16},{2,18},{4,20},{6,22},{8,24},{10,26},{12,28},{14,30},{16,0},... | collective-permute-start | bytes 319496 | tf_op jit(solution)/shard_map/ppermute | solution.py:83
  8.3 2.5 %shard_map.294 = (bf16[1024,512]{1,0:T(8,128)(2,1)S(1)}, f32[1024,128]{1,0:T(8,128)S(1)}, bf16[512,1024]{1,0:T(8,128)(2,1)S(1)}, bf16[1024,512]{1,0:T(8,128)(2,1)S(1)}, bf16[1024,512]{1,0:T(8,128)(2,1)S(1)}) custom-call(bf16[1024,512]{1,0:T(8,128)(2,1)} %bitcast.80, bf16[1024,512]{1,0:T(8,128)(2,1)} %bitcast.78), custom_call_target="tpu_custom_call" | custom-call | bytes 65536 | tf_op jit(solution)/shard_map/pallas_call | solution.py:632
  10.8 2.2 %collective-permute-done.6 = bf16[1,16,3328]{2,1,0:T(8,128)(2,1)S(1)} collective-permute-done((bf16[1,16,3328]{2,1,0:T(8,128)(2,1)S(1)}, bf16[1,16,3328]{2,1,0:T(8,128)(2,1)S(1)}, u32[]{:S(2)}, u32[]{:S(2)}) %collective-permute-start.6) | collective-permute-done | bytes 106528 | tf_op jit(solution)/shard_map/ppermute | solution.py:83
  27.1 3.4 %collective-permute-start.4 = (bf16[1,4,16,2048]{3,2,1,0:T(8,128)(2,1)S(1)}, bf16[1,4,16,2048]{3,2,1,0:T(8,128)(2,1)S(1)}, u32[]{:S(2)}, u32[]{:S(2)}) collective-permute-start(bf16[1,4,16,2048]{3,2,1,0:T(8,128)(2,1)S(1)} %get-tuple-element.195), channel_id=1, source_target_pairs={{0,16},{2,18},{4,20},{6,22},{8,24},{10,26},{12,28},{14,30},{16,0},... | collective-permute-start | bytes 786440 | tf_op jit(solution)/shard_map/ppermute | solution.py:83
  30.7 2.8 %collective-permute-done.9.refs_8_ = bf16[4,16,2560]{2,1,0:T(8,128)(2,1)S(1)} collective-permute-done((bf16[4,16,2560]{2,1,0:T(8,128)(2,1)S(1)}, bf16[4,16,2560]{2,1,0:T(8,128)(2,1)S(1)}, u32[]{:S(2)}, u32[]{:S(2)}) %collective-permute-start.9) | collective-permute-done | bytes 327712 | tf_op jit(solution)/shard_map/ppermute | solution.py:120
  35.7 3.0 %collective-permute-done.4 = bf16[1,4,16,2048]{3,2,1,0:T(8,128)(2,1)S(1)} collective-permute-done((bf16[1,4,16,2048]{3,2,1,0:T(8,128)(2,1)S(1)}, bf16[1,4,16,2048]{3,2,1,0:T(8,128)(2,1)S(1)}, u32[]{:S(2)}, u32[]{:S(2)}) %collective-permute-start.4) | collective-permute-done | bytes 262176 | tf_op jit(solution)/shard_map/ppermute | solution.py:83
  39.7 6.2 %shard_map.295 = (bf16[512,768]{1,0:T(8,128)(2,1)S(1)}, f32[8,512]{1,0:T(8,128)S(1)}, bf16[512,512]{1,0:T(8,128)(2,1)S(1)}, bf16[512,512]{1,0:T(8,128)(2,1)S(1)}...) custom-call(s32[2]{0:T(128)S(1)} %pad_add_fusion.core_ref.refs_0_, ...), custom_call_target="tpu_custom_call" | custom-call | flops 6442450944 | bytes 65536 | tf_op jit(solution)/shard_map/pallas_call | solution.py:632
  47.0 4.0 %collective-permute-done.5 = bf16[2,4,16,2048]{3,2,1,0:T(8,128)(2,1)S(1)} collective-permute-done((bf16[2,4,16,2048]{3,2,1,0:T(8,128)(2,1)S(1)}, bf16[2,4,16,2048]{3,2,1,0:T(8,128)(2,1)S(1)}, u32[]{:S(2)}, u32[]{:S(2)}) %collective-permute-start.5) | collective-permute-done | bytes 524320 | tf_op jit(solution)/shard_map/ppermute | solution.py:83
  51.4 7.3 %shard_map.296 = (bf16[512,512]{1,0:T(8,128)(2,1)S(1)}, f32[1024,512]{1,0:T(8,128)S(1)}, f32[1024,512]{1,0:T(8,128)S(1)}, f32[1024,128]{1,0:T(8,128)S(1)}, bf16[...) custom-call(s32[2]{0:T(128)S(1)} %pad_add_fusion.core_ref.refs_0_, ...), custom_call_target="tpu_custom_call" | custom-call | flops 8589934592 | bytes 65536 | tf_op jit(solution)/shard_map/pallas_call | solution.py:632
  59.2 6.2 %shard_map.297 = (bf16[1024,1024]{1,0:T(8,128)(2,1)S(1)}, bf16[1024,1024]{1,0:T(8,128)(2,1)S(1)}, bf16[512,2048]{1,0:T(8,128)(2,1)S(1)}, bf16[16,16,2048]{2,1,0:T(8,128)(2,1)S(1)}, bf16[16,16,2048]{2,1,0:T(8,128)(2,1)S(1)}) custom-call(s32[2]{0:T(128)S(1)} %pad_add_fusion.core_ref.refs_0_, bf16[1024,512]{1,0:T(8,128)(2,1)S(1)} %get-tuple-element.106.refs_3_.refs_1_.cot_ref, ...), custom_call_target="tpu_custom_call" | custom-call | flops 17179869184 | bytes 65536 | tf_op jit(solution)/shard_map/pallas_call | solution.py:632
  65.9 2.2 %collective-permute-start.27 = (bf16[4,16,2048]{2,1,0:T(8,128)(2,1)S(1)}, bf16[4,16,2048]{2,1,0:T(8,128)(2,1)S(1)}, u32[]{:S(2)}, u32[]{:S(2)}) collective-permute-start(bf16[4,16,2048]{2,1,0:T(8,128)(2,1)S(1)} %get-tuple-element.182), channel_id=1, source_target_pairs={{0,6},{2,4},{4,2},{6,0},{8,14},{10,12},{12,10},{14,8},{16,22},{18,... | collective-permute-start | bytes 786440 | tf_op jit(solution)/shard_map/ppermute | solution.py:175
  69.5 4.7 %shard_map.298 = (f32[1024,512]{1,0:T(8,128)S(1)}, f32[8,512]{1,0:T(8,128)S(1)}, bf16[1024,512]{1,0:T(8,128)(2,1)S(1)}, bf16[384,512]{1,0:T(8,128)(2,1)S(1)}) custom-call(bf16[1024,512]{1,0:T(8,128)(2,1)S(1)} %get-tuple-element.115.slope_ref, bf16[1024,512]{1,0:T(8,128)(2,1)S(1)} %get-tuple-element.106.refs_3_.refs_1_.cot_ref, ...), custom_call_target="tpu_custom_call" | custom-call | flops 4294967296 | bytes 65536 | tf_op jit(solution)/shard_map/pallas_call | solution.py:632
  76.2 2.2 %collective-permute-start.30 = (bf16[4,16,2048]{2,1,0:T(8,128)(2,1)S(1)}, bf16[4,16,2048]{2,1,0:T(8,128)(2,1)S(1)}, u32[]{:S(2)}, u32[]{:S(2)}) collective-permute-start(bf16[4,16,2048]{2,1,0:T(8,128)(2,1)S(1)} %get-tuple-element.178), channel_id=1, source_target_pairs={{0,6},{2,4},{4,2},{6,0},{8,14},{10,12},{12,10},{14,8},{16,22},{18,... | collective-permute-start | bytes 786440 | tf_op jit(solution)/shard_map/ppermute | solution.py:175
  79.7 3.0 %shard_map.299 = (bf16[512,512]{1,0:T(8,128)(2,1)S(1)}, bf16[512,256]{1,0:T(8,128)(2,1)S(1)}, bf16[4,512,512]{2,1,0:T(8,128)(2,1)S(1)}) custom-call(bf16[1024,512]{1,0:T(8,128)(2,1)S(1)} %get-tuple-element.104.refs_1_.act_ref, f32[1024,512]{1,0:T(8,128)S(1)} %get-tuple-element.131.mid_grad_ref, bf16[1024,512]{1,0:T(8,128)(2,1)S(1)} %get-tuple-element.136.pre_grad_ref, ...), custom_call_target="tpu_custom_call" | custom-call | flops 33554432 | bytes 65536 | tf_op jit(solution)/shard_map/pallas_call | solution.py:632
  82.7 4.2 %shard_map.300 = (bf16[1024,512]{1,0:T(8,128)(2,1)S(1)}, bf16[16,16,1408]{2,1,0:T(8,128)(2,1)S(1)}, bf16[16,16,1408]{2,1,0:T(8,128)(2,1)S(1)}) custom-call(s32[2]{0:T(128)S(1)} %pad_add_fusion.core_ref.refs_0_, bf16[4,512,512]{2,1,0:T(8,128)(2,1)S(1)} %get-tuple-element.141.z_ref, bf16[384,512]{1,0:T(8,128)(2,1)S(1)} %get-tuple-element.137.halo_ref, ...), custom_call_target="tpu_custom_call" | custom-call | flops 67108864 | bytes 65536 | tf_op jit(solution)/shard_map/pallas_call | solution.py:632
  87.5 2.5 %shard_map.301 = f32[1024,512]{1,0:T(8,128)} custom-call(bf16[1024,512]{1,0:T(8,128)(2,1)S(1)} %get-tuple-element.150.mixed_grad_ref, bf16[512,768]{1,0:T(8,128)(2,1)S(1)} %get-tuple-element.144.weights, f32[8,512]{1,0:T(8,128)S(1)} %get-tuple-element.108.refs_5_.vec_ref, bf16[1024,512]{1,0:T(8,128)(2,1)S(1)} %get-tuple-element.101.refs_1_.xhat_ref, ...), custom_call_target="tpu_custom_call" | custom-call | flops 33554432 | bytes 65536 | tf_op jit(solution)/shard_map/pallas_call | solution.py:632
  90.0 2.5 %collective-permute-done.29 = bf16[4,16,2048]{2,1,0:T(8,128)(2,1)S(1)} collective-permute-done((bf16[4,16,2048]{2,1,0:T(8,128)(2,1)S(1)}, bf16[4,16,2048]{2,1,0:T(8,128)(2,1)S(1)}, u32[]{:S(2)}, u32[]{:S(2)}) %collective-permute-start.29) | collective-permute-done | bytes 262176 | tf_op jit(solution)/shard_map/ppermute | solution.py:175
  94.7 1.7 %collective-permute-start.35 = (bf16[4,16,1408]{2,1,0:T(8,128)(2,1)S(1)}, bf16[4,16,1408]{2,1,0:T(8,128)(2,1)S(1)}, u32[]{:S(2)}, u32[]{:S(2)}) collective-permute-start(bf16[4,16,1408]{2,1,0:T(8,128)(2,1)S(1)} %get-tuple-element.186), channel_id=1, source_target_pairs={{0,6},{2,4},{4,2},{6,0},{8,14},{10,12},{12,10},{14,8},{16,22},{18,... | collective-permute-start | bytes 540680 | tf_op jit(solution)/shard_map/ppermute | solution.py:175
  98.2 3.1 %shard_map.302 = bf16[1024,512]{1,0:T(8,128)(2,1)} custom-call(f32[1024,512]{1,0:T(8,128)S(1)} %get-tuple-element.153.mid_ref, bf16[1024,1024]{1,0:T(8,128)(2,1)S(1)} %get-tuple-element.154.hidden_a_ref, bf16[1024,1024]{1,0:T(8,128)(2,1)S(1)} %get-tuple-element.126.hidden_b_ref, bf16[512,2560]{1,0:T(8,128)(2,1)S(1)} %get-tuple-element.129.weights_a, ...), custom_call_target="tpu_custom_call" | custom-call | flops 67108864 | bytes 65536 | tf_op jit(solution)/shard_map/pallas_call | solution.py:632
  101.6 3.3 %collective-permute-start.32 = (bf16[1,16,4096]{2,1,0:T(8,128)(2,1)S(1)}, bf16[1,16,4096]{2,1,0:T(8,128)(2,1)S(1)}, u32[]{:S(2)}, u32[]{:S(2)}) collective-permute-start(bf16[1,16,4096]{2,1,0:T(8,128)(2,1)S(1)} %get-tuple-element.192), channel_id=1, source_target_pairs={{0,16},{2,18},{4,20},{6,22},{8,24},{10,26},{12,28},{14,30},{16,0},... | collective-permute-start | bytes 393224 | tf_op jit(solution)/shard_map/ppermute | solution.py:83
  105.9 3.2 %collective-permute-start.38 = (bf16[16,1408]{1,0:T(8,128)(2,1)S(1)}, bf16[16,1408]{1,0:T(8,128)(2,1)S(1)}, u32[]{:S(2)}, u32[]{:S(2)}) collective-permute-start(bf16[16,1408]{1,0:T(8,128)(2,1)S(1)} %get-tuple-element.198), channel_id=1, source_target_pairs={{0,24},{2,26},{4,28},{6,30},{8,16},{10,18},{12,20},{14,22},{16,8},... | collective-permute-start | bytes 135176 | tf_op jit(solution)/shard_map/ppermute | solution.py:183
  111.9 2.3 %collective-permute-done.37.refs_7_ = bf16[16,1408]{1,0:T(8,128)(2,1)S(1)} collective-permute-done((bf16[16,1408]{1,0:T(8,128)(2,1)S(1)}, bf16[16,1408]{1,0:T(8,128)(2,1)S(1)}, u32[]{:S(2)}, u32[]{:S(2)}) %collective-permute-start.37) | collective-permute-done | bytes 45088 | tf_op jit(solution)/shard_map/ppermute | solution.py:183
  (114 shorter events, 33.9 us)
Async XLA Ops:
  0.6 13.2 %collective-permute-start = (bf16[1024,512]{1,0:T(8,128)(2,1)}, bf16[1024,512]{1,0:T(8,128)(2,1)S(1)}, u32[]{:S(2)}, u32[]{:S(2)}) collective-permute-start(bf16[1024,512]{1,0:T(8,128)(2,1)} %bitcast.79), channel_id=1, source_target_pairs={{0,1},{2,3},{4,5},{6,7},{8,9},{10,11},{12,13},{14,15},{16,17},{18,... | collective-permute-start | bytes 3145736 | tf_op jit(solution)/shard_map/ppermute | solution.py:667
  4.8 8.2 %collective-permute-start.6 = (bf16[1,16,3328]{2,1,0:T(8,128)(2,1)S(1)}, bf16[1,16,3328]{2,1,0:T(8,128)(2,1)S(1)}, u32[]{:S(2)}, u32[]{:S(2)}) collective-permute-start(bf16[1,16,3328]{2,1,0:T(8,128)(2,1)S(1)} %bitcast.67), channel_id=1, source_target_pairs={{0,16},{2,18},{4,20},{6,22},{8,24},{10,26},{12,28},{14,30},{16,0},... | collective-permute-start | bytes 319496 | tf_op jit(solution)/shard_map/ppermute | solution.py:83
  16.1 8.0 %collective-permute-start.1 = (bf16[1,16,2048]{2,1,0:T(8,128)(2,1)S(1)}, bf16[1,16,2048]{2,1,0:T(8,128)(2,1)S(1)}, u32[]{:S(2)}, u32[]{:S(2)}) collective-permute-start(bf16[1,16,2048]{2,1,0:T(8,128)(2,1)S(1)} %bitcast.70), channel_id=1, source_target_pairs={{0,2},{2,0},{4,6},{6,4},{8,10},{10,8},{12,14},{14,12},{16,18},{18,... | collective-permute-start | bytes 196616 | tf_op jit(solution)/shard_map/ppermute | solution.py:119
  22.1 8.4 %collective-permute-start.13 = (bf16[4,16,768]{2,1,0:T(8,128)(2,1)S(1)}, bf16[4,16,768]{2,1,0:T(8,128)(2,1)S(1)}, u32[]{:S(2)}, u32[]{:S(2)}) collective-permute-start(bf16[4,16,768]{2,1,0:T(8,128)(2,1)S(1)} %slice.75), channel_id=1, source_target_pairs={{0,4},{2,6},{4,0},{6,2},{8,12},{10,14},{12,8},{14,10},{16,20},{18,... | collective-permute-start | bytes 294920 | tf_op jit(solution)/shard_map/ppermute | solution.py:104
  24.1 9.4 %collective-permute-start.9 = (bf16[4,16,2560]{2,1,0:T(8,128)(2,1)S(1)}, bf16[4,16,2560]{2,1,0:T(8,128)(2,1)S(1)}, u32[]{:S(2)}, u32[]{:S(2)}) collective-permute-start(bf16[4,16,2560]{2,1,0:T(8,128)(2,1)S(1)} %slice.72.refs_6_), channel_id=1, source_target_pairs={{0,4},{2,6},{4,0},{6,2},{8,12},{10,14},{12,8},{14,10},{16,20},{18,... | collective-permute-start | bytes 983048 | tf_op jit(solution)/shard_map/ppermute | solution.py:120
  25.7 8.7 %collective-permute-start.8 = (bf16[4,16,2560]{2,1,0:T(8,128)(2,1)S(1)}, bf16[4,16,2560]{2,1,0:T(8,128)(2,1)S(1)}, u32[]{:S(2)}, u32[]{:S(2)}) collective-permute-start(bf16[4,16,2560]{2,1,0:T(8,128)(2,1)S(1)} %slice.72.refs_6_), channel_id=1, source_target_pairs={{0,2},{2,0},{4,6},{6,4},{8,10},{10,8},{12,14},{14,12},{16,18},{18,... | collective-permute-start | bytes 983048 | tf_op jit(solution)/shard_map/ppermute | solution.py:119
  27.1 11.6 %collective-permute-start.4 = (bf16[1,4,16,2048]{3,2,1,0:T(8,128)(2,1)S(1)}, bf16[1,4,16,2048]{3,2,1,0:T(8,128)(2,1)S(1)}, u32[]{:S(2)}, u32[]{:S(2)}) collective-permute-start(bf16[1,4,16,2048]{3,2,1,0:T(8,128)(2,1)S(1)} %get-tuple-element.195), channel_id=1, source_target_pairs={{0,16},{2,18},{4,20},{6,22},{8,24},{10,26},{12,28},{14,30},{16,0},... | collective-permute-start | bytes 786440 | tf_op jit(solution)/shard_map/ppermute | solution.py:83
  30.6 9.0 %collective-permute-start.15 = (bf16[16,16,768]{2,1,0:T(8,128)(2,1)S(1)}, bf16[16,16,768]{2,1,0:T(8,128)(2,1)S(1)}, u32[]{:S(2)}, u32[]{:S(2)}) collective-permute-start(bf16[16,16,768]{2,1,0:T(8,128)(2,1)S(1)} %pad_maximum_fusion.4.refs_12_), channel_id=1, source_target_pairs={{0,1},{1,0},{2,3},{3,2},{4,5},{5,4},{6,7},{7,6},{8,9},{9,8},{10,11... | collective-permute-start | bytes 1179656 | tf_op jit(solution)/shard_map/ppermute | solution.py:111
  33.5 12.4 %collective-permute-start.10 = (bf16[2,16,2560]{2,1,0:T(8,128)(2,1)S(1)}, bf16[2,16,2560]{2,1,0:T(8,128)(2,1)S(1)}, u32[]{:S(2)}, u32[]{:S(2)}) collective-permute-start(bf16[2,16,2560]{2,1,0:T(8,128)(2,1)S(1)} %slice.96), channel_id=1, source_target_pairs={{0,2},{2,0},{4,6},{6,4},{8,10},{10,8},{12,14},{14,12},{16,18},{18,... | collective-permute-start | bytes 491528 | tf_op jit(solution)/shard_map/ppermute | solution.py:125
  34.4 11.5 %collective-permute-start.11 = (bf16[2,16,2560]{2,1,0:T(8,128)(2,1)S(1)}, bf16[2,16,2560]{2,1,0:T(8,128)(2,1)S(1)}, u32[]{:S(2)}, u32[]{:S(2)}) collective-permute-start(bf16[2,16,2560]{2,1,0:T(8,128)(2,1)S(1)} %slice.97), channel_id=1, source_target_pairs={{0,4},{2,6},{4,0},{6,2},{8,12},{10,14},{12,8},{14,10},{16,20},{18,... | collective-permute-start | bytes 491528 | tf_op jit(solution)/shard_map/ppermute | solution.py:126
  38.8 12.2 %collective-permute-start.5 = (bf16[2,4,16,2048]{3,2,1,0:T(8,128)(2,1)S(1)}, bf16[2,4,16,2048]{3,2,1,0:T(8,128)(2,1)S(1)}, u32[]{:S(2)}, u32[]{:S(2)}) collective-permute-start(bf16[2,4,16,2048]{3,2,1,0:T(8,128)(2,1)S(1)} %get-tuple-element.191), channel_id=1, source_target_pairs={{0,8},{2,10},{4,12},{6,14},{8,0},{10,2},{12,4},{14,6},{16,24},{18,... | collective-permute-start | bytes 1572872 | tf_op jit(solution)/shard_map/ppermute | solution.py:83
  51.2 7.9 %collective-permute-start.20 = (bf16[16,16,2048]{2,1,0:T(8,128)(2,1)S(1)}, bf16[16,16,2048]{2,1,0:T(8,128)(2,1)S(1)}, u32[]{:S(2)}, u32[]{:S(2)}) collective-permute-start(bf16[16,16,2048]{2,1,0:T(8,128)(2,1)S(1)} %bitcast.64), channel_id=1, source_target_pairs={{0,1},{1,0},{2,3},{3,2},{4,5},{5,4},{6,7},{7,6},{8,9},{9,8},{10,11... | collective-permute-start | bytes 3145736 | tf_op jit(solution)/shard_map/ppermute | solution.py:111
  65.3 10.3 %collective-permute-start.22 = (bf16[16,16,2048]{2,1,0:T(8,128)(2,1)S(1)}, bf16[16,16,2048]{2,1,0:T(8,128)(2,1)S(1)}, u32[]{:S(2)}, u32[]{:S(2)}) collective-permute-start(bf16[16,16,2048]{2,1,0:T(8,128)(2,1)S(1)} %get-tuple-element.134), channel_id=1, source_target_pairs={{0,1},{1,0},{2,3},{3,2},{4,5},{5,4},{6,7},{7,6},{8,9},{9,8},{10,11... | collective-permute-start | bytes 3145736 | tf_op jit(solution)/shard_map/ppermute | solution.py:166
  65.9 12.4 %collective-permute-start.27 = (bf16[4,16,2048]{2,1,0:T(8,128)(2,1)S(1)}, bf16[4,16,2048]{2,1,0:T(8,128)(2,1)S(1)}, u32[]{:S(2)}, u32[]{:S(2)}) collective-permute-start(bf16[4,16,2048]{2,1,0:T(8,128)(2,1)S(1)} %get-tuple-element.182), channel_id=1, source_target_pairs={{0,6},{2,4},{4,2},{6,0},{8,14},{10,12},{12,10},{14,8},{16,22},{18,... | collective-permute-start | bytes 786440 | tf_op jit(solution)/shard_map/ppermute | solution.py:175
  68.1 18.8 %collective-permute-start.26 = (bf16[4,16,2048]{2,1,0:T(8,128)(2,1)S(1)}, bf16[4,16,2048]{2,1,0:T(8,128)(2,1)S(1)}, u32[]{:S(2)}, u32[]{:S(2)}) collective-permute-start(bf16[4,16,2048]{2,1,0:T(8,128)(2,1)S(1)} %get-tuple-element.183), channel_id=1, source_target_pairs={{0,4},{2,6},{4,0},{6,2},{8,12},{10,14},{12,8},{14,10},{16,20},{18,... | collective-permute-start | bytes 786440 | tf_op jit(solution)/shard_map/ppermute | solution.py:175
  69.0 17.9 %collective-permute-start.25 = (bf16[4,16,2048]{2,1,0:T(8,128)(2,1)S(1)}, bf16[4,16,2048]{2,1,0:T(8,128)(2,1)S(1)}, u32[]{:S(2)}, u32[]{:S(2)}) collective-permute-start(bf16[4,16,2048]{2,1,0:T(8,128)(2,1)S(1)} %get-tuple-element.184), channel_id=1, source_target_pairs={{0,2},{2,0},{4,6},{6,4},{8,10},{10,8},{12,14},{14,12},{16,18},{18,... | collective-permute-start | bytes 786440 | tf_op jit(solution)/shard_map/ppermute | solution.py:175
  76.2 13.8 %collective-permute-start.30 = (bf16[4,16,2048]{2,1,0:T(8,128)(2,1)S(1)}, bf16[4,16,2048]{2,1,0:T(8,128)(2,1)S(1)}, u32[]{:S(2)}, u32[]{:S(2)}) collective-permute-start(bf16[4,16,2048]{2,1,0:T(8,128)(2,1)S(1)} %get-tuple-element.178), channel_id=1, source_target_pairs={{0,6},{2,4},{4,2},{6,0},{8,14},{10,12},{12,10},{14,8},{16,22},{18,... | collective-permute-start | bytes 786440 | tf_op jit(solution)/shard_map/ppermute | solution.py:175
  78.4 14.1 %collective-permute-start.29 = (bf16[4,16,2048]{2,1,0:T(8,128)(2,1)S(1)}, bf16[4,16,2048]{2,1,0:T(8,128)(2,1)S(1)}, u32[]{:S(2)}, u32[]{:S(2)}) collective-permute-start(bf16[4,16,2048]{2,1,0:T(8,128)(2,1)S(1)} %get-tuple-element.179), channel_id=1, source_target_pairs={{0,4},{2,6},{4,0},{6,2},{8,12},{10,14},{12,8},{14,10},{16,20},{18,... | collective-permute-start | bytes 786440 | tf_op jit(solution)/shard_map/ppermute | solution.py:175
  79.3 13.7 %collective-permute-start.28 = (bf16[4,16,2048]{2,1,0:T(8,128)(2,1)S(1)}, bf16[4,16,2048]{2,1,0:T(8,128)(2,1)S(1)}, u32[]{:S(2)}, u32[]{:S(2)}) collective-permute-start(bf16[4,16,2048]{2,1,0:T(8,128)(2,1)S(1)} %get-tuple-element.180), channel_id=1, source_target_pairs={{0,2},{2,0},{4,6},{6,4},{8,10},{10,8},{12,14},{14,12},{16,18},{18,... | collective-permute-start | bytes 786440 | tf_op jit(solution)/shard_map/ppermute | solution.py:175
  93.4 8.1 %collective-permute-start.31 = (bf16[2,16,4096]{2,1,0:T(8,128)(2,1)S(1)}, bf16[2,16,4096]{2,1,0:T(8,128)(2,1)S(1)}, u32[]{:S(2)}, u32[]{:S(2)}) collective-permute-start(bf16[2,16,4096]{2,1,0:T(8,128)(2,1)S(1)} %slice_bitcast_fusion), channel_id=1, source_target_pairs={{0,8},{2,10},{4,12},{6,14},{8,0},{10,2},{12,4},{14,6},{16,24},{18,... | collective-permute-start | bytes 786440 | tf_op jit(solution)/shard_map/ppermute | solution.py:83
  94.7 10.2 %collective-permute-start.35 = (bf16[4,16,1408]{2,1,0:T(8,128)(2,1)S(1)}, bf16[4,16,1408]{2,1,0:T(8,128)(2,1)S(1)}, u32[]{:S(2)}, u32[]{:S(2)}) collective-permute-start(bf16[4,16,1408]{2,1,0:T(8,128)(2,1)S(1)} %get-tuple-element.186), channel_id=1, source_target_pairs={{0,6},{2,4},{4,2},{6,0},{8,14},{10,12},{12,10},{14,8},{16,22},{18,... | collective-permute-start | bytes 540680 | tf_op jit(solution)/shard_map/ppermute | solution.py:175
  96.3 9.4 %collective-permute-start.34 = (bf16[4,16,1408]{2,1,0:T(8,128)(2,1)S(1)}, bf16[4,16,1408]{2,1,0:T(8,128)(2,1)S(1)}, u32[]{:S(2)}, u32[]{:S(2)}) collective-permute-start(bf16[4,16,1408]{2,1,0:T(8,128)(2,1)S(1)} %get-tuple-element.187), channel_id=1, source_target_pairs={{0,4},{2,6},{4,0},{6,2},{8,12},{10,14},{12,8},{14,10},{16,20},{18,... | collective-permute-start | bytes 540680 | tf_op jit(solution)/shard_map/ppermute | solution.py:175
  97.2 8.6 %collective-permute-start.33 = (bf16[4,16,1408]{2,1,0:T(8,128)(2,1)S(1)}, bf16[4,16,1408]{2,1,0:T(8,128)(2,1)S(1)}, u32[]{:S(2)}, u32[]{:S(2)}) collective-permute-start(bf16[4,16,1408]{2,1,0:T(8,128)(2,1)S(1)} %get-tuple-element.188), channel_id=1, source_target_pairs={{0,2},{2,0},{4,6},{6,4},{8,10},{10,8},{12,14},{14,12},{16,18},{18,... | collective-permute-start | bytes 540680 | tf_op jit(solution)/shard_map/ppermute | solution.py:175
  101.6 8.9 %collective-permute-start.32 = (bf16[1,16,4096]{2,1,0:T(8,128)(2,1)S(1)}, bf16[1,16,4096]{2,1,0:T(8,128)(2,1)S(1)}, u32[]{:S(2)}, u32[]{:S(2)}) collective-permute-start(bf16[1,16,4096]{2,1,0:T(8,128)(2,1)S(1)} %get-tuple-element.192), channel_id=1, source_target_pairs={{0,16},{2,18},{4,20},{6,22},{8,24},{10,26},{12,28},{14,30},{16,0},... | collective-permute-start | bytes 393224 | tf_op jit(solution)/shard_map/ppermute | solution.py:83
  (25 other events, 273.3 us)

commit v3 on v2

--- a/solution.py
+++ b/solution.py
@@ -699,7 +699,7 @@
         spaces=[pltpu.HBM] * 2,
     )
     (prior_hat,) = call(prior_kernel, [x_prior], [((length, feats), BF16)])
-    held_b = jnp.concatenate(gather_plane(tie(shard_b, prior_hat)[None]))
+    held_b = jnp.concatenate(gather_near(tie(shard_b, prior_hat)[None]))
     held = shard[None]
     for at, step in enumerate(far_steps()):
         got = from_line(held, step)

time: 115 us -> 114 us (level)
  waiting for transfers between devices: 22.2 us -> 20.1 us
    ppermute x2 -> x1, waiting for transfers between devices: 4.09 us -> 0.12 us  [gather_plane(): by_y = lax.ppermute(held, 'dp', swap_route(dp_count, 2))]
    ppermute x3 -> x6, starting transfers between devices: 3.55 us -> 7.11 us  [gather_near(): lax.ppermute(held, 'dp', swap_route(dp_count, k))]
    ppermute x6, waiting for transfers between devices: 9.5 us -> 11.8 us  [from_line(): return lax.ppermute(held, 'dp', swap_route(dp_count, step * nxy))]
    ppermute x2 -> x1, starting transfers between devices: 3.1 us -> 1.58 us  [gather_plane(): by_y = lax.ppermute(held, 'dp', swap_route(dp_count, 2))]
    ppermute x1 -> x0, starting transfers between devices: 1.49 us -> none  [gather_plane(): return [held, by_x, by_y, lax.ppermute(by_y, 'dp', swap_route(dp_count, 1))]]
    ppermute x2 -> x1, starting transfers between devices: 2.03 us -> 0.71 us  [gather_plane(): by_x = lax.ppermute(held, 'dp', swap_route(dp_count, 1))]
  transfers between devices with their start and end apart: 39 -> 39, of which waited for: 13 -> 14; matrix products, arithmetic and copies ran while one was open for 2% -> 2% of each run, Pallas kernels for 36% -> 37%
where the time goes in v3:
time: 114 us; the launch traced here: 113 us
  starting transfers between devices  47.1 us (41%)
  Pallas kernels  42.7 us (37%)
  waiting for transfers between devices  20.1 us (18%)
  other arithmetic  1.91 us (2%)
  between operations  1.16 us (1%)
    pallas_call x12, Pallas kernels, call(): pl.pallas_call(kernel, out_shape=[jax.ShapeDtypeStruct(shape, dtype) for...  42.7 us
    ppermute x6, starting transfers between devices, from_line(): return lax.ppermute(held, 'dp', swap_route(dp_count, step * nxy))  13.4 us
    ppermute x6, waiting for transfers between devices, from_line(): return lax.ppermute(held, 'dp', swap_route(dp_count, step * nxy))  11.8 us
    ppermute x9, starting transfers between devices, spread_near(): lax.ppermute(pieces[k], 'dp', swap_route(dp_count, k))  10.7 us
    ppermute x6, starting transfers between devices, gather_near(): lax.ppermute(held, 'dp', swap_route(dp_count, k))  7.11 us
    ppermute x3, starting transfers between devices, spread_far(): lax.ppermute(part[k], 'dp', swap_route(dp_count, k * nxy))  4.45 us
    ppermute x3, waiting for transfers between devices, spread_far(): lax.ppermute(part[k], 'dp', swap_route(dp_count, k * nxy))  3.77 us
    ppermute x9, waiting for transfers between devices, spread_near(): lax.ppermute(pieces[k], 'dp', swap_route(dp_count, k))  3.46 us
  transfers between devices with their start and end apart: 39, of which 14 were waited for; matrix products, arithmetic and copies ran while one was open for 2% of the time, Pallas kernels for 37%

profile of v3, /device:TPU:0, one launch (start us, length us, event | category | flops | bytes accessed | tf_op | source)
XLA Modules:
  0.0 113.4 jit_solution(12780235610882083282)
XLA Ops:
  0.6 2.4 %collective-permute-start = (bf16[1024,512]{1,0:T(8,128)(2,1)}, bf16[1024,512]{1,0:T(8,128)(2,1)S(1)}, u32[]{:S(2)}, u32[]{:S(2)}) collective-permute-start(bf16[1024,512]{1,0:T(8,128)(2,1)} %bitcast.80), channel_id=1, source_target_pairs={{0,1},{2,3},{4,5},{6,7},{8,9},{10,11},{12,13},{14,15},{16,17},{18,... | collective-permute-start | bytes 3145736 | tf_op jit(solution)/shard_map/ppermute | solution.py:667
  3.2 1.6 %shard_map.292 = (bf16[16,3328]{1,0:T(8,128)(2,1)S(1)}, bf16[16,2048]{1,0:T(8,128)(2,1)S(1)}) custom-call(s32[2]{0:T(128)S(1)} %pad_add_fusion.core_ref.refs_0_, bf16[16,512]{1,0:T(8,128)(2,1)} %in_ref.1, bf16[16,192]{1,0:T(8,128)(2,1)} %refs_0_.1, bf16[16,512]{1,0:T(8,128)(2,1)} %out_ref.1, bf16[16,2048]{1,0:T(8,128)(2,1)} %up_ref.1, ...), custom_call_target="tpu_custom_call" | custom-call | bytes 65536 | tf_op jit(solution)/shard_map/pallas_call | solution.py:632
  4.8 3.5 %collective-permute-start.6 = (bf16[1,16,3328]{2,1,0:T(8,128)(2,1)S(1)}, bf16[1,16,3328]{2,1,0:T(8,128)(2,1)S(1)}, u32[]{:S(2)}, u32[]{:S(2)}) collective-permute-start(bf16[1,16,3328]{2,1,0:T(8,128)(2,1)S(1)} %bitcast.67), channel_id=1, source_target_pairs={{0,16},{2,18},{4,20},{6,22},{8,24},{10,26},{12,28},{14,30},{16,0},... | collective-permute-start | bytes 319496 | tf_op jit(solution)/shard_map/ppermute | solution.py:83
  8.3 2.5 %shard_map.294 = (bf16[1024,512]{1,0:T(8,128)(2,1)S(1)}, f32[1024,128]{1,0:T(8,128)S(1)}, bf16[512,1024]{1,0:T(8,128)(2,1)S(1)}, bf16[1024,512]{1,0:T(8,128)(2,1)S(1)}, bf16[1024,512]{1,0:T(8,128)(2,1)S(1)}) custom-call(bf16[1024,512]{1,0:T(8,128)(2,1)} %bitcast.81, bf16[1024,512]{1,0:T(8,128)(2,1)} %bitcast.79), custom_call_target="tpu_custom_call" | custom-call | bytes 65536 | tf_op jit(solution)/shard_map/pallas_call | solution.py:632
  10.8 2.2 %collective-permute-done.6 = bf16[1,16,3328]{2,1,0:T(8,128)(2,1)S(1)} collective-permute-done((bf16[1,16,3328]{2,1,0:T(8,128)(2,1)S(1)}, bf16[1,16,3328]{2,1,0:T(8,128)(2,1)S(1)}, u32[]{:S(2)}, u32[]{:S(2)}) %collective-permute-start.6) | collective-permute-done | bytes 106528 | tf_op jit(solution)/shard_map/ppermute | solution.py:83
  14.5 2.5 %collective-permute-start.3 = (bf16[1,16,2048]{2,1,0:T(8,128)(2,1)S(1)}, bf16[1,16,2048]{2,1,0:T(8,128)(2,1)S(1)}, u32[]{:S(2)}, u32[]{:S(2)}) collective-permute-start(bf16[1,16,2048]{2,1,0:T(8,128)(2,1)S(1)} %bitcast.69), channel_id=1, source_target_pairs={{0,6},{2,4},{4,2},{6,0},{8,14},{10,12},{12,10},{14,8},{16,22},{18,... | collective-permute-start | bytes 196616 | tf_op jit(solution)/shard_map/ppermute | solution.py:104
  19.2 2.6 %collective-permute-start.14 = (bf16[4,16,768]{2,1,0:T(8,128)(2,1)S(1)}, bf16[4,16,768]{2,1,0:T(8,128)(2,1)S(1)}, u32[]{:S(2)}, u32[]{:S(2)}) collective-permute-start(bf16[4,16,768]{2,1,0:T(8,128)(2,1)S(1)} %slice.75), channel_id=1, source_target_pairs={{0,6},{2,4},{4,2},{6,0},{8,14},{10,12},{12,10},{14,8},{16,22},{18,... | collective-permute-start | bytes 294920 | tf_op jit(solution)/shard_map/ppermute | solution.py:104
  22.8 3.3 %collective-permute-start.4 = (bf16[1,4,16,2048]{3,2,1,0:T(8,128)(2,1)S(1)}, bf16[1,4,16,2048]{3,2,1,0:T(8,128)(2,1)S(1)}, u32[]{:S(2)}, u32[]{:S(2)}) collective-permute-start(bf16[1,4,16,2048]{3,2,1,0:T(8,128)(2,1)S(1)} %get-tuple-element.195), channel_id=1, source_target_pairs={{0,16},{2,18},{4,20},{6,22},{8,24},{10,26},{12,28},{14,30},{16,0},... | collective-permute-start | bytes 786440 | tf_op jit(solution)/shard_map/ppermute | solution.py:83
  29.3 6.9 %collective-permute-done.4 = bf16[1,4,16,2048]{3,2,1,0:T(8,128)(2,1)S(1)} collective-permute-done((bf16[1,4,16,2048]{3,2,1,0:T(8,128)(2,1)S(1)}, bf16[1,4,16,2048]{3,2,1,0:T(8,128)(2,1)S(1)}, u32[]{:S(2)}, u32[]{:S(2)}) %collective-permute-start.4) | collective-permute-done | bytes 262176 | tf_op jit(solution)/shard_map/ppermute | solution.py:83
  40.3 6.2 %shard_map.295 = (bf16[512,768]{1,0:T(8,128)(2,1)S(1)}, f32[8,512]{1,0:T(8,128)S(1)}, bf16[512,512]{1,0:T(8,128)(2,1)S(1)}, bf16[512,512]{1,0:T(8,128)(2,1)S(1)}...) custom-call(s32[2]{0:T(128)S(1)} %pad_add_fusion.core_ref.refs_0_, ...), custom_call_target="tpu_custom_call" | custom-call | flops 6442450944 | bytes 65536 | tf_op jit(solution)/shard_map/pallas_call | solution.py:632
  49.7 7.2 %shard_map.296 = (bf16[512,512]{1,0:T(8,128)(2,1)S(1)}, f32[1024,512]{1,0:T(8,128)S(1)}, f32[1024,512]{1,0:T(8,128)S(1)}, f32[1024,128]{1,0:T(8,128)S(1)}, bf16[...) custom-call(s32[2]{0:T(128)S(1)} %pad_add_fusion.core_ref.refs_0_, ...), custom_call_target="tpu_custom_call" | custom-call | flops 8589934592 | bytes 65536 | tf_op jit(solution)/shard_map/pallas_call | solution.py:632
  57.4 6.2 %shard_map.297 = (bf16[1024,1024]{1,0:T(8,128)(2,1)S(1)}, bf16[1024,1024]{1,0:T(8,128)(2,1)S(1)}, bf16[512,2048]{1,0:T(8,128)(2,1)S(1)}, bf16[16,16,2048]{2,1,0:T(8,128)(2,1)S(1)}, bf16[16,16,2048]{2,1,0:T(8,128)(2,1)S(1)}) custom-call(s32[2]{0:T(128)S(1)} %pad_add_fusion.core_ref.refs_0_, bf16[1024,512]{1,0:T(8,128)(2,1)S(1)} %get-tuple-element.106.refs_3_.refs_1_.cot_ref, ...), custom_call_target="tpu_custom_call" | custom-call | flops 17179869184 | bytes 65536 | tf_op jit(solution)/shard_map/pallas_call | solution.py:632
  64.3 2.4 %collective-permute-start.27 = (bf16[4,16,2048]{2,1,0:T(8,128)(2,1)S(1)}, bf16[4,16,2048]{2,1,0:T(8,128)(2,1)S(1)}, u32[]{:S(2)}, u32[]{:S(2)}) collective-permute-start(bf16[4,16,2048]{2,1,0:T(8,128)(2,1)S(1)} %get-tuple-element.182), channel_id=1, source_target_pairs={{0,6},{2,4},{4,2},{6,0},{8,14},{10,12},{12,10},{14,8},{16,22},{18,... | collective-permute-start | bytes 786440 | tf_op jit(solution)/shard_map/ppermute | solution.py:175
  67.9 4.7 %shard_map.298 = (f32[1024,512]{1,0:T(8,128)S(1)}, f32[8,512]{1,0:T(8,128)S(1)}, bf16[1024,512]{1,0:T(8,128)(2,1)S(1)}, bf16[384,512]{1,0:T(8,128)(2,1)S(1)}) custom-call(bf16[1024,512]{1,0:T(8,128)(2,1)S(1)} %get-tuple-element.115.slope_ref, bf16[1024,512]{1,0:T(8,128)(2,1)S(1)} %get-tuple-element.106.refs_3_.refs_1_.cot_ref, ...), custom_call_target="tpu_custom_call" | custom-call | flops 4294967296 | bytes 65536 | tf_op jit(solution)/shard_map/pallas_call | solution.py:632
  74.6 2.4 %collective-permute-start.30 = (bf16[4,16,2048]{2,1,0:T(8,128)(2,1)S(1)}, bf16[4,16,2048]{2,1,0:T(8,128)(2,1)S(1)}, u32[]{:S(2)}, u32[]{:S(2)}) collective-permute-start(bf16[4,16,2048]{2,1,0:T(8,128)(2,1)S(1)} %get-tuple-element.178), channel_id=1, source_target_pairs={{0,6},{2,4},{4,2},{6,0},{8,14},{10,12},{12,10},{14,8},{16,22},{18,... | collective-permute-start | bytes 786440 | tf_op jit(solution)/shard_map/ppermute | solution.py:175
  78.1 3.0 %shard_map.299 = (bf16[512,512]{1,0:T(8,128)(2,1)S(1)}, bf16[512,256]{1,0:T(8,128)(2,1)S(1)}, bf16[4,512,512]{2,1,0:T(8,128)(2,1)S(1)}) custom-call(bf16[1024,512]{1,0:T(8,128)(2,1)S(1)} %get-tuple-element.104.refs_1_.act_ref, f32[1024,512]{1,0:T(8,128)S(1)} %get-tuple-element.131.mid_grad_ref, bf16[1024,512]{1,0:T(8,128)(2,1)S(1)} %get-tuple-element.136.pre_grad_ref, ...), custom_call_target="tpu_custom_call" | custom-call | flops 33554432 | bytes 65536 | tf_op jit(solution)/shard_map/pallas_call | solution.py:632
  81.1 4.2 %shard_map.300 = (bf16[1024,512]{1,0:T(8,128)(2,1)S(1)}, bf16[16,16,1408]{2,1,0:T(8,128)(2,1)S(1)}, bf16[16,16,1408]{2,1,0:T(8,128)(2,1)S(1)}) custom-call(s32[2]{0:T(128)S(1)} %pad_add_fusion.core_ref.refs_0_, bf16[4,512,512]{2,1,0:T(8,128)(2,1)S(1)} %get-tuple-element.141.z_ref, bf16[384,512]{1,0:T(8,128)(2,1)S(1)} %get-tuple-element.137.halo_ref, ...), custom_call_target="tpu_custom_call" | custom-call | flops 67108864 | bytes 65536 | tf_op jit(solution)/shard_map/pallas_call | solution.py:632
  85.7 2.5 %shard_map.301 = f32[1024,512]{1,0:T(8,128)} custom-call(bf16[1024,512]{1,0:T(8,128)(2,1)S(1)} %get-tuple-element.150.mixed_grad_ref, bf16[512,768]{1,0:T(8,128)(2,1)S(1)} %get-tuple-element.144.weights, f32[8,512]{1,0:T(8,128)S(1)} %get-tuple-element.108.refs_5_.vec_ref, bf16[1024,512]{1,0:T(8,128)(2,1)S(1)} %get-tuple-element.101.refs_1_.xhat_ref, ...), custom_call_target="tpu_custom_call" | custom-call | flops 33554432 | bytes 65536 | tf_op jit(solution)/shard_map/pallas_call | solution.py:632
  88.2 2.6 %collective-permute-done.29 = bf16[4,16,2048]{2,1,0:T(8,128)(2,1)S(1)} collective-permute-done((bf16[4,16,2048]{2,1,0:T(8,128)(2,1)S(1)}, bf16[4,16,2048]{2,1,0:T(8,128)(2,1)S(1)}, u32[]{:S(2)}, u32[]{:S(2)}) %collective-permute-start.29) | collective-permute-done | bytes 262176 | tf_op jit(solution)/shard_map/ppermute | solution.py:175
  93.2 1.7 %collective-permute-start.35 = (bf16[4,16,1408]{2,1,0:T(8,128)(2,1)S(1)}, bf16[4,16,1408]{2,1,0:T(8,128)(2,1)S(1)}, u32[]{:S(2)}, u32[]{:S(2)}) collective-permute-start(bf16[4,16,1408]{2,1,0:T(8,128)(2,1)S(1)} %get-tuple-element.186), channel_id=1, source_target_pairs={{0,6},{2,4},{4,2},{6,0},{8,14},{10,12},{12,10},{14,8},{16,22},{18,... | collective-permute-start | bytes 540680 | tf_op jit(solution)/shard_map/ppermute | solution.py:175
  96.7 3.1 %shard_map.302 = bf16[1024,512]{1,0:T(8,128)(2,1)} custom-call(f32[1024,512]{1,0:T(8,128)S(1)} %get-tuple-element.153.mid_ref, bf16[1024,1024]{1,0:T(8,128)(2,1)S(1)} %get-tuple-element.154.hidden_a_ref, bf16[1024,1024]{1,0:T(8,128)(2,1)S(1)} %get-tuple-element.126.hidden_b_ref, bf16[512,2560]{1,0:T(8,128)(2,1)S(1)} %get-tuple-element.129.weights_a, ...), custom_call_target="tpu_custom_call" | custom-call | flops 67108864 | bytes 65536 | tf_op jit(solution)/shard_map/pallas_call | solution.py:632
  99.9 3.4 %collective-permute-start.32 = (bf16[1,16,4096]{2,1,0:T(8,128)(2,1)S(1)}, bf16[1,16,4096]{2,1,0:T(8,128)(2,1)S(1)}, u32[]{:S(2)}, u32[]{:S(2)}) collective-permute-start(bf16[1,16,4096]{2,1,0:T(8,128)(2,1)S(1)} %get-tuple-element.192), channel_id=1, source_target_pairs={{0,16},{2,18},{4,20},{6,22},{8,24},{10,26},{12,28},{14,30},{16,0},... | collective-permute-start | bytes 393224 | tf_op jit(solution)/shard_map/ppermute | solution.py:83
  104.3 3.2 %collective-permute-start.38 = (bf16[16,1408]{1,0:T(8,128)(2,1)S(1)}, bf16[16,1408]{1,0:T(8,128)(2,1)S(1)}, u32[]{:S(2)}, u32[]{:S(2)}) collective-permute-start(bf16[16,1408]{1,0:T(8,128)(2,1)S(1)} %get-tuple-element.198), channel_id=1, source_target_pairs={{0,24},{2,26},{4,28},{6,30},{8,16},{10,18},{12,20},{14,22},{16,8},... | collective-permute-start | bytes 135176 | tf_op jit(solution)/shard_map/ppermute | solution.py:183
  110.3 2.3 %collective-permute-done.37.refs_7_ = bf16[16,1408]{1,0:T(8,128)(2,1)S(1)} collective-permute-done((bf16[16,1408]{1,0:T(8,128)(2,1)S(1)}, bf16[16,1408]{1,0:T(8,128)(2,1)S(1)}, u32[]{:S(2)}, u32[]{:S(2)}) %collective-permute-start.37) | collective-permute-done | bytes 45088 | tf_op jit(solution)/shard_map/ppermute | solution.py:183
  (114 shorter events, 29.6 us)
Async XLA Ops:
  0.6 13.2 %collective-permute-start = (bf16[1024,512]{1,0:T(8,128)(2,1)}, bf16[1024,512]{1,0:T(8,128)(2,1)S(1)}, u32[]{:S(2)}, u32[]{:S(2)}) collective-permute-start(bf16[1024,512]{1,0:T(8,128)(2,1)} %bitcast.80), channel_id=1, source_target_pairs={{0,1},{2,3},{4,5},{6,7},{8,9},{10,11},{12,13},{14,15},{16,17},{18,... | collective-permute-start | bytes 3145736 | tf_op jit(solution)/shard_map/ppermute | solution.py:667
  4.8 8.2 %collective-permute-start.6 = (bf16[1,16,3328]{2,1,0:T(8,128)(2,1)S(1)}, bf16[1,16,3328]{2,1,0:T(8,128)(2,1)S(1)}, u32[]{:S(2)}, u32[]{:S(2)}) collective-permute-start(bf16[1,16,3328]{2,1,0:T(8,128)(2,1)S(1)} %bitcast.67), channel_id=1, source_target_pairs={{0,16},{2,18},{4,20},{6,22},{8,24},{10,26},{12,28},{14,30},{16,0},... | collective-permute-start | bytes 319496 | tf_op jit(solution)/shard_map/ppermute | solution.py:83
  14.5 7.8 %collective-permute-start.3 = (bf16[1,16,2048]{2,1,0:T(8,128)(2,1)S(1)}, bf16[1,16,2048]{2,1,0:T(8,128)(2,1)S(1)}, u32[]{:S(2)}, u32[]{:S(2)}) collective-permute-start(bf16[1,16,2048]{2,1,0:T(8,128)(2,1)S(1)} %bitcast.69), channel_id=1, source_target_pairs={{0,6},{2,4},{4,2},{6,0},{8,14},{10,12},{12,10},{14,8},{16,22},{18,... | collective-permute-start | bytes 196616 | tf_op jit(solution)/shard_map/ppermute | solution.py:104
  22.8 13.5 %collective-permute-start.4 = (bf16[1,4,16,2048]{3,2,1,0:T(8,128)(2,1)S(1)}, bf16[1,4,16,2048]{3,2,1,0:T(8,128)(2,1)S(1)}, u32[]{:S(2)}, u32[]{:S(2)}) collective-permute-start(bf16[1,4,16,2048]{3,2,1,0:T(8,128)(2,1)S(1)} %get-tuple-element.195), channel_id=1, source_target_pairs={{0,16},{2,18},{4,20},{6,22},{8,24},{10,26},{12,28},{14,30},{16,0},... | collective-permute-start | bytes 786440 | tf_op jit(solution)/shard_map/ppermute | solution.py:83
  26.9 13.3 %collective-permute-start.15 = (bf16[16,16,768]{2,1,0:T(8,128)(2,1)S(1)}, bf16[16,16,768]{2,1,0:T(8,128)(2,1)S(1)}, u32[]{:S(2)}, u32[]{:S(2)}) collective-permute-start(bf16[16,16,768]{2,1,0:T(8,128)(2,1)S(1)} %pad_maximum_fusion.4.refs_12_), channel_id=1, source_target_pairs={{0,1},{1,0},{2,3},{3,2},{4,5},{5,4},{6,7},{7,6},{8,9},{9,8},{10,11... | collective-permute-start | bytes 1179656 | tf_op jit(solution)/shard_map/ppermute | solution.py:111
  27.0 10.2 %collective-permute-start.9 = (bf16[4,16,2560]{2,1,0:T(8,128)(2,1)S(1)}, bf16[4,16,2560]{2,1,0:T(8,128)(2,1)S(1)}, u32[]{:S(2)}, u32[]{:S(2)}) collective-permute-start(bf16[4,16,2560]{2,1,0:T(8,128)(2,1)S(1)} %slice.72.refs_6_), channel_id=1, source_target_pairs={{0,4},{2,6},{4,0},{6,2},{8,12},{10,14},{12,8},{14,10},{16,20},{18,... | collective-permute-start | bytes 983048 | tf_op jit(solution)/shard_map/ppermute | solution.py:120
  28.6 10.0 %collective-permute-start.8 = (bf16[4,16,2560]{2,1,0:T(8,128)(2,1)S(1)}, bf16[4,16,2560]{2,1,0:T(8,128)(2,1)S(1)}, u32[]{:S(2)}, u32[]{:S(2)}) collective-permute-start(bf16[4,16,2560]{2,1,0:T(8,128)(2,1)S(1)} %slice.72.refs_6_), channel_id=1, source_target_pairs={{0,2},{2,0},{4,6},{6,4},{8,10},{10,8},{12,14},{14,12},{16,18},{18,... | collective-permute-start | bytes 983048 | tf_op jit(solution)/shard_map/ppermute | solution.py:119
  36.3 13.0 %collective-permute-start.5 = (bf16[2,4,16,2048]{3,2,1,0:T(8,128)(2,1)S(1)}, bf16[2,4,16,2048]{3,2,1,0:T(8,128)(2,1)S(1)}, u32[]{:S(2)}, u32[]{:S(2)}) collective-permute-start(bf16[2,4,16,2048]{3,2,1,0:T(8,128)(2,1)S(1)} %get-tuple-element.191), channel_id=1, source_target_pairs={{0,8},{2,10},{4,12},{6,14},{8,0},{10,2},{12,4},{14,6},{16,24},{18,... | collective-permute-start | bytes 1572872 | tf_op jit(solution)/shard_map/ppermute | solution.py:83
  37.2 9.4 %collective-permute-start.10 = (bf16[2,16,2560]{2,1,0:T(8,128)(2,1)S(1)}, bf16[2,16,2560]{2,1,0:T(8,128)(2,1)S(1)}, u32[]{:S(2)}, u32[]{:S(2)}) collective-permute-start(bf16[2,16,2560]{2,1,0:T(8,128)(2,1)S(1)} %slice.96), channel_id=1, source_target_pairs={{0,2},{2,0},{4,6},{6,4},{8,10},{10,8},{12,14},{14,12},{16,18},{18,... | collective-permute-start | bytes 491528 | tf_op jit(solution)/shard_map/ppermute | solution.py:125
  38.7 7.9 %collective-permute-start.11 = (bf16[2,16,2560]{2,1,0:T(8,128)(2,1)S(1)}, bf16[2,16,2560]{2,1,0:T(8,128)(2,1)S(1)}, u32[]{:S(2)}, u32[]{:S(2)}) collective-permute-start(bf16[2,16,2560]{2,1,0:T(8,128)(2,1)S(1)} %slice.97), channel_id=1, source_target_pairs={{0,4},{2,6},{4,0},{6,2},{8,12},{10,14},{12,8},{14,10},{16,20},{18,... | collective-permute-start | bytes 491528 | tf_op jit(solution)/shard_map/ppermute | solution.py:126
  49.5 7.9 %collective-permute-start.20 = (bf16[16,16,2048]{2,1,0:T(8,128)(2,1)S(1)}, bf16[16,16,2048]{2,1,0:T(8,128)(2,1)S(1)}, u32[]{:S(2)}, u32[]{:S(2)}) collective-permute-start(bf16[16,16,2048]{2,1,0:T(8,128)(2,1)S(1)} %bitcast.64), channel_id=1, source_target_pairs={{0,1},{1,0},{2,3},{3,2},{4,5},{5,4},{6,7},{7,6},{8,9},{9,8},{10,11... | collective-permute-start | bytes 3145736 | tf_op jit(solution)/shard_map/ppermute | solution.py:111
  63.6 10.5 %collective-permute-start.22 = (bf16[16,16,2048]{2,1,0:T(8,128)(2,1)S(1)}, bf16[16,16,2048]{2,1,0:T(8,128)(2,1)S(1)}, u32[]{:S(2)}, u32[]{:S(2)}) collective-permute-start(bf16[16,16,2048]{2,1,0:T(8,128)(2,1)S(1)} %get-tuple-element.134), channel_id=1, source_target_pairs={{0,1},{1,0},{2,3},{3,2},{4,5},{5,4},{6,7},{7,6},{8,9},{9,8},{10,11... | collective-permute-start | bytes 3145736 | tf_op jit(solution)/shard_map/ppermute | solution.py:166
  64.3 12.7 %collective-permute-start.27 = (bf16[4,16,2048]{2,1,0:T(8,128)(2,1)S(1)}, bf16[4,16,2048]{2,1,0:T(8,128)(2,1)S(1)}, u32[]{:S(2)}, u32[]{:S(2)}) collective-permute-start(bf16[4,16,2048]{2,1,0:T(8,128)(2,1)S(1)} %get-tuple-element.182), channel_id=1, source_target_pairs={{0,6},{2,4},{4,2},{6,0},{8,14},{10,12},{12,10},{14,8},{16,22},{18,... | collective-permute-start | bytes 786440 | tf_op jit(solution)/shard_map/ppermute | solution.py:175
  66.7 18.6 %collective-permute-start.26 = (bf16[4,16,2048]{2,1,0:T(8,128)(2,1)S(1)}, bf16[4,16,2048]{2,1,0:T(8,128)(2,1)S(1)}, u32[]{:S(2)}, u32[]{:S(2)}) collective-permute-start(bf16[4,16,2048]{2,1,0:T(8,128)(2,1)S(1)} %get-tuple-element.183), channel_id=1, source_target_pairs={{0,4},{2,6},{4,0},{6,2},{8,12},{10,14},{12,8},{14,10},{16,20},{18,... | collective-permute-start | bytes 786440 | tf_op jit(solution)/shard_map/ppermute | solution.py:175
  67.2 18.1 %collective-permute-start.25 = (bf16[4,16,2048]{2,1,0:T(8,128)(2,1)S(1)}, bf16[4,16,2048]{2,1,0:T(8,128)(2,1)S(1)}, u32[]{:S(2)}, u32[]{:S(2)}) collective-permute-start(bf16[4,16,2048]{2,1,0:T(8,128)(2,1)S(1)} %get-tuple-element.184), channel_id=1, source_target_pairs={{0,2},{2,0},{4,6},{6,4},{8,10},{10,8},{12,14},{14,12},{16,18},{18,... | collective-permute-start | bytes 786440 | tf_op jit(solution)/shard_map/ppermute | solution.py:175
  74.6 13.6 %collective-permute-start.30 = (bf16[4,16,2048]{2,1,0:T(8,128)(2,1)S(1)}, bf16[4,16,2048]{2,1,0:T(8,128)(2,1)S(1)}, u32[]{:S(2)}, u32[]{:S(2)}) collective-permute-start(bf16[4,16,2048]{2,1,0:T(8,128)(2,1)S(1)} %get-tuple-element.178), channel_id=1, source_target_pairs={{0,6},{2,4},{4,2},{6,0},{8,14},{10,12},{12,10},{14,8},{16,22},{18,... | collective-permute-start | bytes 786440 | tf_op jit(solution)/shard_map/ppermute | solution.py:175
  77.0 13.8 %collective-permute-start.29 = (bf16[4,16,2048]{2,1,0:T(8,128)(2,1)S(1)}, bf16[4,16,2048]{2,1,0:T(8,128)(2,1)S(1)}, u32[]{:S(2)}, u32[]{:S(2)}) collective-permute-start(bf16[4,16,2048]{2,1,0:T(8,128)(2,1)S(1)} %get-tuple-element.179), channel_id=1, source_target_pairs={{0,4},{2,6},{4,0},{6,2},{8,12},{10,14},{12,8},{14,10},{16,20},{18,... | collective-permute-start | bytes 786440 | tf_op jit(solution)/shard_map/ppermute | solution.py:175
  77.5 13.4 %collective-permute-start.28 = (bf16[4,16,2048]{2,1,0:T(8,128)(2,1)S(1)}, bf16[4,16,2048]{2,1,0:T(8,128)(2,1)S(1)}, u32[]{:S(2)}, u32[]{:S(2)}) collective-permute-start(bf16[4,16,2048]{2,1,0:T(8,128)(2,1)S(1)} %get-tuple-element.180), channel_id=1, source_target_pairs={{0,2},{2,0},{4,6},{6,4},{8,10},{10,8},{12,14},{14,12},{16,18},{18,... | collective-permute-start | bytes 786440 | tf_op jit(solution)/shard_map/ppermute | solution.py:175
  85.3 7.6 %collective-permute-start.24 = (bf16[16,16,1408]{2,1,0:T(8,128)(2,1)S(1)}, bf16[16,16,1408]{2,1,0:T(8,128)(2,1)S(1)}, u32[]{:S(2)}, u32[]{:S(2)}) collective-permute-start(bf16[16,16,1408]{2,1,0:T(8,128)(2,1)S(1)} %get-tuple-element.149), channel_id=1, source_target_pairs={{0,1},{1,0},{2,3},{3,2},{4,5},{5,4},{6,7},{7,6},{8,9},{9,8},{10,11... | collective-permute-start | bytes 2162696 | tf_op jit(solution)/shard_map/ppermute | solution.py:166
  91.3 8.6 %collective-permute-start.31 = (bf16[2,16,4096]{2,1,0:T(8,128)(2,1)S(1)}, bf16[2,16,4096]{2,1,0:T(8,128)(2,1)S(1)}, u32[]{:S(2)}, u32[]{:S(2)}) collective-permute-start(bf16[2,16,4096]{2,1,0:T(8,128)(2,1)S(1)} %slice_bitcast_fusion), channel_id=1, source_target_pairs={{0,8},{2,10},{4,12},{6,14},{8,0},{10,2},{12,4},{14,6},{16,24},{18,... | collective-permute-start | bytes 786440 | tf_op jit(solution)/shard_map/ppermute | solution.py:83
  93.2 10.2 %collective-permute-start.35 = (bf16[4,16,1408]{2,1,0:T(8,128)(2,1)S(1)}, bf16[4,16,1408]{2,1,0:T(8,128)(2,1)S(1)}, u32[]{:S(2)}, u32[]{:S(2)}) collective-permute-start(bf16[4,16,1408]{2,1,0:T(8,128)(2,1)S(1)} %get-tuple-element.186), channel_id=1, source_target_pairs={{0,6},{2,4},{4,2},{6,0},{8,14},{10,12},{12,10},{14,8},{16,22},{18,... | collective-permute-start | bytes 540680 | tf_op jit(solution)/shard_map/ppermute | solution.py:175
  94.8 9.3 %collective-permute-start.34 = (bf16[4,16,1408]{2,1,0:T(8,128)(2,1)S(1)}, bf16[4,16,1408]{2,1,0:T(8,128)(2,1)S(1)}, u32[]{:S(2)}, u32[]{:S(2)}) collective-permute-start(bf16[4,16,1408]{2,1,0:T(8,128)(2,1)S(1)} %get-tuple-element.187), channel_id=1, source_target_pairs={{0,4},{2,6},{4,0},{6,2},{8,12},{10,14},{12,8},{14,10},{16,20},{18,... | collective-permute-start | bytes 540680 | tf_op jit(solution)/shard_map/ppermute | solution.py:175
  96.2 8.0 %collective-permute-start.33 = (bf16[4,16,1408]{2,1,0:T(8,128)(2,1)S(1)}, bf16[4,16,1408]{2,1,0:T(8,128)(2,1)S(1)}, u32[]{:S(2)}, u32[]{:S(2)}) collective-permute-start(bf16[4,16,1408]{2,1,0:T(8,128)(2,1)S(1)} %get-tuple-element.188), channel_id=1, source_target_pairs={{0,2},{2,0},{4,6},{6,4},{8,10},{10,8},{12,14},{14,12},{16,18},{18,... | collective-permute-start | bytes 540680 | tf_op jit(solution)/shard_map/ppermute | solution.py:175
  99.9 8.9 %collective-permute-start.32 = (bf16[1,16,4096]{2,1,0:T(8,128)(2,1)S(1)}, bf16[1,16,4096]{2,1,0:T(8,128)(2,1)S(1)}, u32[]{:S(2)}, u32[]{:S(2)}) collective-permute-start(bf16[1,16,4096]{2,1,0:T(8,128)(2,1)S(1)} %get-tuple-element.192), channel_id=1, source_target_pairs={{0,16},{2,18},{4,20},{6,22},{8,24},{10,26},{12,28},{14,30},{16,0},... | collective-permute-start | bytes 393224 | tf_op jit(solution)/shard_map/ppermute | solution.py:83
  (25 other events, 274.5 us)

commit v4 on v3

--- a/solution.py
+++ b/solution.py
@@ -564,18 +564,20 @@
         sums = sums + jnp.sum(grad_mixed.astype(F32).reshape(BLOCK // 8, 8, feats), axis=0)
     back = dot(xhat_ref[...], mixed_grad_ref[...], TN)
     mixed_sum = jnp.sum(sums, axis=0, keepdims=True)
-    padded = jnp.concatenate([vec_ref[...], vec_grad_ref[...], jnp.zeros((112, feats), F32)], axis=0)
+    blank = jnp.zeros((64, feats), F32)
+    padded = jnp.concatenate([blank, vec_ref[...], vec_grad_ref[...], blank[:48]], axis=0)
     columns = padded.T
-    put_rows(grad_refs, slice(0, feats), columns[:, 0:1] * back + columns[:, 1:2] * mixed_sum, place)
+    put_rows(grad_refs, slice(0, feats), columns[:, 64:65] * back + columns[:, 65:66] * mixed_sum, place)
     put_rows(grad_refs, slice(feats, 2 * feats), out_grad_ref[...], place)
-    put_rows(grad_refs, slice(2 * feats, 2 * feats + 256), tap_grad_ref[...], place)
+    put_rows(grad_refs, slice(2 * feats, 2 * feats + 128), tap_grad_ref[:, :128], place)
     proj = weights[:, 0:feats]
     proj_f = proj.astype(F32)
     gain_grad = jnp.sum(proj_f * back, axis=1, keepdims=True)
     bias_grad = jnp.sum(proj_f * mixed_sum, axis=1, keepdims=True)
     lane = lax.broadcasted_iota(jnp.int32, (feats, 128), 1)
-    columns = jnp.where(lane == 0, gain_grad, jnp.where(lane == 1, bias_grad, columns))
-    put_rows(grad_refs, slice(2 * feats + 256, 2 * feats + 384), columns, place)
+    columns = jnp.where(lane == 64, gain_grad, jnp.where(lane == 65, bias_grad, columns))
+    columns = jnp.where(lane < 64, tap_grad_ref[:, 128:].astype(F32), columns)
+    put_rows(grad_refs, slice(2 * feats + 128, 2 * feats + 256), columns, place)
 
 
 def input_kernel(mixed_grad_ref, weights, vec_ref, xhat_ref, inv_ref, mid_grad_ref, input_grad_ref):
@@ -613,12 +615,12 @@
     own = raw * inverse
     along = jnp.sum(tap_rows * own, axis=1, keepdims=True)
     param_grad_ref[...] = scale * inverse * (tap_rows - wide * own * along)
-    tail = mixer[:, 2 * feats + 256 :]
+    tail = mixer[:, 2 * feats + 128 :]
     rows = tail.shape[0]
     diagonal = lax.broadcasted_iota(jnp.int32, (rows, rows), 0) == lax.broadcasted_iota(
         jnp.int32, (rows, rows), 1
     )
-    columns = (tail[:, 0:1], tail[:, 1:2], tap_rows[:, 0:1], tail[:, 8:9], tail[:, 9:10])
+    columns = (tail[:, 64:65], tail[:, 65:66], tap_rows[:, 0:1], tail[:, 72:73], tail[:, 73:74])
     for ref, column in zip(outs[5:], columns):
         ref[...] = jnp.sum(jnp.where(diagonal, column, 0.0), axis=0, keepdims=True)
 
@@ -802,7 +804,7 @@
             core_at, z_grad, halo, after, grad_pre, fine_h, coarse_h, basis, basis_t, back_pool, weights,
             vec, vec_grad, xhat, out_grad, tap_grad,
         ],
-        [token_bf16, *grad_shapes(2 * feats + 384)],
+        [token_bf16, *grad_shapes(2 * feats + 256)],
         [pltpu.VMEM((2 * pooled, feats), BF16)],
         flops=4 << 24,
         spaces=[smem] + [vmem] * 15,

time: 114 us -> 113 us (level)
    ppermute x6, waiting for transfers between devices: 11.8 us -> 13.7 us  [from_line(): return lax.ppermute(held, 'dp', swap_route(dp_count, step * nxy))]
    ppermute x3, waiting for transfers between devices: 3.77 us -> 2.15 us  [spread_far(): lax.ppermute(part[k], 'dp', swap_route(dp_count, k * nxy))]
  transfers between devices with their start and end apart: 39 -> 39, of which waited for: 14 -> 13; matrix products, arithmetic and copies ran while one was open for 2% -> 2% of each run, Pallas kernels for 37% -> 37%
where the time goes in v4:
time: 113 us
  starting transfers between devices  47.1 us (42%)
  Pallas kernels  42.7 us (38%)
  waiting for transfers between devices  19.7 us (17%)
  other arithmetic  1.87 us (2%)
  between operations  1.16 us (1%)
    pallas_call x12, Pallas kernels, call(): pl.pallas_call(kernel, out_shape=[jax.ShapeDtypeStruct(shape, dtype) for...  42.7 us
    ppermute x6, waiting for transfers between devices, from_line(): return lax.ppermute(held, 'dp', swap_route(dp_count, step * nxy))  13.7 us
    ppermute x6, starting transfers between devices, from_line(): return lax.ppermute(held, 'dp', swap_route(dp_count, step * nxy))  13.3 us
    ppermute x9, starting transfers between devices, spread_near(): lax.ppermute(pieces[k], 'dp', swap_route(dp_count, k))  10.7 us
    ppermute x6, starting transfers between devices, gather_near(): lax.ppermute(held, 'dp', swap_route(dp_count, k))  7.11 us
    ppermute x3, starting transfers between devices, spread_far(): lax.ppermute(part[k], 'dp', swap_route(dp_count, k * nxy))  4.45 us
    ppermute x9, waiting for transfers between devices, spread_near(): lax.ppermute(pieces[k], 'dp', swap_route(dp_count, k))  2.76 us
    ppermute x1, starting transfers between devices, body(): x_prior = lax.ppermute(x_own, 'seq', [(0, 1)])  2.43 us
  transfers between devices with their start and end apart: 39, of which 13 were waited for; matrix products, arithmetic and copies ran while one was open for 2% of the time, Pallas kernels for 37%

profile of v4, /device:TPU:0, one launch (start us, length us, event | category | flops | bytes accessed | tf_op | source)
XLA Modules:
  0.0 113.1 jit_solution(2744452085184896084)
XLA Ops:
  0.6 2.4 %collective-permute-start = (bf16[1024,512]{1,0:T(8,128)(2,1)}, bf16[1024,512]{1,0:T(8,128)(2,1)S(1)}, u32[]{:S(2)}, u32[]{:S(2)}) collective-permute-start(bf16[1024,512]{1,0:T(8,128)(2,1)} %bitcast.80), channel_id=1, source_target_pairs={{0,1},{2,3},{4,5},{6,7},{8,9},{10,11},{12,13},{14,15},{16,17},{18,... | collective-permute-start | bytes 3145736 | tf_op jit(solution)/shard_map/ppermute | solution.py:669
  4.8 3.5 %collective-permute-start.6 = (bf16[1,16,3328]{2,1,0:T(8,128)(2,1)S(1)}, bf16[1,16,3328]{2,1,0:T(8,128)(2,1)S(1)}, u32[]{:S(2)}, u32[]{:S(2)}) collective-permute-start(bf16[1,16,3328]{2,1,0:T(8,128)(2,1)S(1)} %bitcast.67), channel_id=1, source_target_pairs={{0,16},{2,18},{4,20},{6,22},{8,24},{10,26},{12,28},{14,30},{16,0},... | collective-permute-start | bytes 319496 | tf_op jit(solution)/shard_map/ppermute | solution.py:83
  8.3 2.5 %shard_map.294 = (bf16[1024,512]{1,0:T(8,128)(2,1)S(1)}, f32[1024,128]{1,0:T(8,128)S(1)}, bf16[512,1024]{1,0:T(8,128)(2,1)S(1)}, bf16[1024,512]{1,0:T(8,128)(2,1)S(1)}, bf16[1024,512]{1,0:T(8,128)(2,1)S(1)}) custom-call(bf16[1024,512]{1,0:T(8,128)(2,1)} %bitcast.81, bf16[1024,512]{1,0:T(8,128)(2,1)} %bitcast.79), custom_call_target="tpu_custom_call" | custom-call | bytes 65536 | tf_op jit(solution)/shard_map/pallas_call | solution.py:634
  10.8 2.2 %collective-permute-done.6 = bf16[1,16,3328]{2,1,0:T(8,128)(2,1)S(1)} collective-permute-done((bf16[1,16,3328]{2,1,0:T(8,128)(2,1)S(1)}, bf16[1,16,3328]{2,1,0:T(8,128)(2,1)S(1)}, u32[]{:S(2)}, u32[]{:S(2)}) %collective-permute-start.6) | collective-permute-done | bytes 106528 | tf_op jit(solution)/shard_map/ppermute | solution.py:83
  14.5 2.5 %collective-permute-start.3 = (bf16[1,16,2048]{2,1,0:T(8,128)(2,1)S(1)}, bf16[1,16,2048]{2,1,0:T(8,128)(2,1)S(1)}, u32[]{:S(2)}, u32[]{:S(2)}) collective-permute-start(bf16[1,16,2048]{2,1,0:T(8,128)(2,1)S(1)} %bitcast.69), channel_id=1, source_target_pairs={{0,6},{2,4},{4,2},{6,0},{8,14},{10,12},{12,10},{14,8},{16,22},{18,... | collective-permute-start | bytes 196616 | tf_op jit(solution)/shard_map/ppermute | solution.py:104
  19.2 2.6 %collective-permute-start.14 = (bf16[4,16,768]{2,1,0:T(8,128)(2,1)S(1)}, bf16[4,16,768]{2,1,0:T(8,128)(2,1)S(1)}, u32[]{:S(2)}, u32[]{:S(2)}) collective-permute-start(bf16[4,16,768]{2,1,0:T(8,128)(2,1)S(1)} %slice.75), channel_id=1, source_target_pairs={{0,6},{2,4},{4,2},{6,0},{8,14},{10,12},{12,10},{14,8},{16,22},{18,... | collective-permute-start | bytes 294920 | tf_op jit(solution)/shard_map/ppermute | solution.py:104
  22.8 3.3 %collective-permute-start.4 = (bf16[1,4,16,2048]{3,2,1,0:T(8,128)(2,1)S(1)}, bf16[1,4,16,2048]{3,2,1,0:T(8,128)(2,1)S(1)}, u32[]{:S(2)}, u32[]{:S(2)}) collective-permute-start(bf16[1,4,16,2048]{3,2,1,0:T(8,128)(2,1)S(1)} %get-tuple-element.195), channel_id=1, source_target_pairs={{0,16},{2,18},{4,20},{6,22},{8,24},{10,26},{12,28},{14,30},{16,0},... | collective-permute-start | bytes 786440 | tf_op jit(solution)/shard_map/ppermute | solution.py:83
  29.3 6.9 %collective-permute-done.4 = bf16[1,4,16,2048]{3,2,1,0:T(8,128)(2,1)S(1)} collective-permute-done((bf16[1,4,16,2048]{3,2,1,0:T(8,128)(2,1)S(1)}, bf16[1,4,16,2048]{3,2,1,0:T(8,128)(2,1)S(1)}, u32[]{:S(2)}, u32[]{:S(2)}) %collective-permute-start.4) | collective-permute-done | bytes 262176 | tf_op jit(solution)/shard_map/ppermute | solution.py:83
  40.3 6.2 %shard_map.295 = (bf16[512,768]{1,0:T(8,128)(2,1)S(1)}, f32[8,512]{1,0:T(8,128)S(1)}, bf16[512,512]{1,0:T(8,128)(2,1)S(1)}, bf16[512,512]{1,0:T(8,128)(2,1)S(1)}...) custom-call(s32[2]{0:T(128)S(1)} %pad_add_fusion.core_ref.refs_0_, ...), custom_call_target="tpu_custom_call" | custom-call | flops 6442450944 | bytes 65536 | tf_op jit(solution)/shard_map/pallas_call | solution.py:634
  49.7 7.2 %shard_map.296 = (bf16[512,512]{1,0:T(8,128)(2,1)S(1)}, f32[1024,512]{1,0:T(8,128)S(1)}, f32[1024,512]{1,0:T(8,128)S(1)}, f32[1024,128]{1,0:T(8,128)S(1)}, bf16[...) custom-call(s32[2]{0:T(128)S(1)} %pad_add_fusion.core_ref.refs_0_, ...), custom_call_target="tpu_custom_call" | custom-call | flops 8589934592 | bytes 65536 | tf_op jit(solution)/shard_map/pallas_call | solution.py:634
  57.4 6.2 %shard_map.297 = (bf16[1024,1024]{1,0:T(8,128)(2,1)S(1)}, bf16[1024,1024]{1,0:T(8,128)(2,1)S(1)}, bf16[512,2048]{1,0:T(8,128)(2,1)S(1)}, bf16[16,16,2048]{2,1,0:T(8,128)(2,1)S(1)}, bf16[16,16,2048]{2,1,0:T(8,128)(2,1)S(1)}) custom-call(s32[2]{0:T(128)S(1)} %pad_add_fusion.core_ref.refs_0_, bf16[1024,512]{1,0:T(8,128)(2,1)S(1)} %get-tuple-element.106.refs_3_.refs_1_.cot_ref, ...), custom_call_target="tpu_custom_call" | custom-call | flops 17179869184 | bytes 65536 | tf_op jit(solution)/shard_map/pallas_call | solution.py:634
  64.3 2.4 %collective-permute-start.27 = (bf16[4,16,2048]{2,1,0:T(8,128)(2,1)S(1)}, bf16[4,16,2048]{2,1,0:T(8,128)(2,1)S(1)}, u32[]{:S(2)}, u32[]{:S(2)}) collective-permute-start(bf16[4,16,2048]{2,1,0:T(8,128)(2,1)S(1)} %get-tuple-element.182), channel_id=1, source_target_pairs={{0,6},{2,4},{4,2},{6,0},{8,14},{10,12},{12,10},{14,8},{16,22},{18,... | collective-permute-start | bytes 786440 | tf_op jit(solution)/shard_map/ppermute | solution.py:175
  67.9 4.7 %shard_map.298 = (f32[1024,512]{1,0:T(8,128)S(1)}, f32[8,512]{1,0:T(8,128)S(1)}, bf16[1024,512]{1,0:T(8,128)(2,1)S(1)}, bf16[384,512]{1,0:T(8,128)(2,1)S(1)}) custom-call(bf16[1024,512]{1,0:T(8,128)(2,1)S(1)} %get-tuple-element.115.slope_ref, bf16[1024,512]{1,0:T(8,128)(2,1)S(1)} %get-tuple-element.106.refs_3_.refs_1_.cot_ref, ...), custom_call_target="tpu_custom_call" | custom-call | flops 4294967296 | bytes 65536 | tf_op jit(solution)/shard_map/pallas_call | solution.py:634
  74.6 2.4 %collective-permute-start.30 = (bf16[4,16,2048]{2,1,0:T(8,128)(2,1)S(1)}, bf16[4,16,2048]{2,1,0:T(8,128)(2,1)S(1)}, u32[]{:S(2)}, u32[]{:S(2)}) collective-permute-start(bf16[4,16,2048]{2,1,0:T(8,128)(2,1)S(1)} %get-tuple-element.178), channel_id=1, source_target_pairs={{0,6},{2,4},{4,2},{6,0},{8,14},{10,12},{12,10},{14,8},{16,22},{18,... | collective-permute-start | bytes 786440 | tf_op jit(solution)/shard_map/ppermute | solution.py:175
  78.2 3.0 %shard_map.299 = (bf16[512,512]{1,0:T(8,128)(2,1)S(1)}, bf16[512,256]{1,0:T(8,128)(2,1)S(1)}, bf16[4,512,512]{2,1,0:T(8,128)(2,1)S(1)}) custom-call(bf16[1024,512]{1,0:T(8,128)(2,1)S(1)} %get-tuple-element.104.refs_1_.act_ref, f32[1024,512]{1,0:T(8,128)S(1)} %get-tuple-element.131.mid_grad_ref, bf16[1024,512]{1,0:T(8,128)(2,1)S(1)} %get-tuple-element.136.pre_grad_ref, ...), custom_call_target="tpu_custom_call" | custom-call | flops 33554432 | bytes 65536 | tf_op jit(solution)/shard_map/pallas_call | solution.py:634
  81.1 4.2 %shard_map.300 = (bf16[1024,512]{1,0:T(8,128)(2,1)S(1)}, bf16[16,16,1280]{2,1,0:T(8,128)(2,1)S(1)}, bf16[16,16,1280]{2,1,0:T(8,128)(2,1)S(1)}) custom-call(s32[2]{0:T(128)S(1)} %pad_add_fusion.core_ref.refs_0_, bf16[4,512,512]{2,1,0:T(8,128)(2,1)S(1)} %get-tuple-element.141.z_ref, bf16[384,512]{1,0:T(8,128)(2,1)S(1)} %get-tuple-element.137.halo_ref, ...), custom_call_target="tpu_custom_call" | custom-call | flops 67108864 | bytes 65536 | tf_op jit(solution)/shard_map/pallas_call | solution.py:634
  85.8 2.5 %shard_map.301 = f32[1024,512]{1,0:T(8,128)} custom-call(bf16[1024,512]{1,0:T(8,128)(2,1)S(1)} %get-tuple-element.150.mixed_grad_ref, bf16[512,768]{1,0:T(8,128)(2,1)S(1)} %get-tuple-element.144.weights, f32[8,512]{1,0:T(8,128)S(1)} %get-tuple-element.108.refs_5_.vec_ref, bf16[1024,512]{1,0:T(8,128)(2,1)S(1)} %get-tuple-element.101.refs_1_.xhat_ref, ...), custom_call_target="tpu_custom_call" | custom-call | flops 33554432 | bytes 65536 | tf_op jit(solution)/shard_map/pallas_call | solution.py:634
  88.2 2.5 %collective-permute-done.29 = bf16[4,16,2048]{2,1,0:T(8,128)(2,1)S(1)} collective-permute-done((bf16[4,16,2048]{2,1,0:T(8,128)(2,1)S(1)}, bf16[4,16,2048]{2,1,0:T(8,128)(2,1)S(1)}, u32[]{:S(2)}, u32[]{:S(2)}) %collective-permute-start.29) | collective-permute-done | bytes 262176 | tf_op jit(solution)/shard_map/ppermute | solution.py:175
  93.1 1.7 %collective-permute-start.35 = (bf16[4,16,1280]{2,1,0:T(8,128)(2,1)S(1)}, bf16[4,16,1280]{2,1,0:T(8,128)(2,1)S(1)}, u32[]{:S(2)}, u32[]{:S(2)}) collective-permute-start(bf16[4,16,1280]{2,1,0:T(8,128)(2,1)S(1)} %get-tuple-element.186), channel_id=1, source_target_pairs={{0,6},{2,4},{4,2},{6,0},{8,14},{10,12},{12,10},{14,8},{16,22},{18,... | collective-permute-start | bytes 491528 | tf_op jit(solution)/shard_map/ppermute | solution.py:175
  96.7 3.1 %shard_map.302 = bf16[1024,512]{1,0:T(8,128)(2,1)} custom-call(f32[1024,512]{1,0:T(8,128)S(1)} %get-tuple-element.153.mid_ref, bf16[1024,1024]{1,0:T(8,128)(2,1)S(1)} %get-tuple-element.154.hidden_a_ref, bf16[1024,1024]{1,0:T(8,128)(2,1)S(1)} %get-tuple-element.126.hidden_b_ref, bf16[512,2560]{1,0:T(8,128)(2,1)S(1)} %get-tuple-element.129.weights_a, ...), custom_call_target="tpu_custom_call" | custom-call | flops 67108864 | bytes 65536 | tf_op jit(solution)/shard_map/pallas_call | solution.py:634
  99.9 3.4 %collective-permute-start.32 = (bf16[1,16,4096]{2,1,0:T(8,128)(2,1)S(1)}, bf16[1,16,4096]{2,1,0:T(8,128)(2,1)S(1)}, u32[]{:S(2)}, u32[]{:S(2)}) collective-permute-start(bf16[1,16,4096]{2,1,0:T(8,128)(2,1)S(1)} %get-tuple-element.192), channel_id=1, source_target_pairs={{0,16},{2,18},{4,20},{6,22},{8,24},{10,26},{12,28},{14,30},{16,0},... | collective-permute-start | bytes 393224 | tf_op jit(solution)/shard_map/ppermute | solution.py:83
  103.6 3.2 %collective-permute-start.38 = (bf16[16,1280]{1,0:T(8,128)(2,1)S(1)}, bf16[16,1280]{1,0:T(8,128)(2,1)S(1)}, u32[]{:S(2)}, u32[]{:S(2)}) collective-permute-start(bf16[16,1280]{1,0:T(8,128)(2,1)S(1)} %get-tuple-element.198), channel_id=1, source_target_pairs={{0,24},{2,26},{4,28},{6,30},{8,16},{10,18},{12,20},{14,22},{16,8},... | collective-permute-start | bytes 122888 | tf_op jit(solution)/shard_map/ppermute | solution.py:183
  108.0 2.1 %collective-permute-done.32 = bf16[1,16,4096]{2,1,0:T(8,128)(2,1)S(1)} collective-permute-done((bf16[1,16,4096]{2,1,0:T(8,128)(2,1)S(1)}, bf16[1,16,4096]{2,1,0:T(8,128)(2,1)S(1)}, u32[]{:S(2)}, u32[]{:S(2)}) %collective-permute-start.32) | collective-permute-done | bytes 131104 | tf_op jit(solution)/shard_map/ppermute | solution.py:83
  110.1 2.1 %collective-permute-done.37.refs_7_ = bf16[16,1280]{1,0:T(8,128)(2,1)S(1)} collective-permute-done((bf16[16,1280]{1,0:T(8,128)(2,1)S(1)}, bf16[16,1280]{1,0:T(8,128)(2,1)S(1)}, u32[]{:S(2)}, u32[]{:S(2)}) %collective-permute-start.37) | collective-permute-done | bytes 40992 | tf_op jit(solution)/shard_map/ppermute | solution.py:183
  (114 shorter events, 29.1 us)
Async XLA Ops:
  0.6 13.2 %collective-permute-start = (bf16[1024,512]{1,0:T(8,128)(2,1)}, bf16[1024,512]{1,0:T(8,128)(2,1)S(1)}, u32[]{:S(2)}, u32[]{:S(2)}) collective-permute-start(bf16[1024,512]{1,0:T(8,128)(2,1)} %bitcast.80), channel_id=1, source_target_pairs={{0,1},{2,3},{4,5},{6,7},{8,9},{10,11},{12,13},{14,15},{16,17},{18,... | collective-permute-start | bytes 3145736 | tf_op jit(solution)/shard_map/ppermute | solution.py:669
  4.8 8.2 %collective-permute-start.6 = (bf16[1,16,3328]{2,1,0:T(8,128)(2,1)S(1)}, bf16[1,16,3328]{2,1,0:T(8,128)(2,1)S(1)}, u32[]{:S(2)}, u32[]{:S(2)}) collective-permute-start(bf16[1,16,3328]{2,1,0:T(8,128)(2,1)S(1)} %bitcast.67), channel_id=1, source_target_pairs={{0,16},{2,18},{4,20},{6,22},{8,24},{10,26},{12,28},{14,30},{16,0},... | collective-permute-start | bytes 319496 | tf_op jit(solution)/shard_map/ppermute | solution.py:83
  14.5 7.8 %collective-permute-start.3 = (bf16[1,16,2048]{2,1,0:T(8,128)(2,1)S(1)}, bf16[1,16,2048]{2,1,0:T(8,128)(2,1)S(1)}, u32[]{:S(2)}, u32[]{:S(2)}) collective-permute-start(bf16[1,16,2048]{2,1,0:T(8,128)(2,1)S(1)} %bitcast.69), channel_id=1, source_target_pairs={{0,6},{2,4},{4,2},{6,0},{8,14},{10,12},{12,10},{14,8},{16,22},{18,... | collective-permute-start | bytes 196616 | tf_op jit(solution)/shard_map/ppermute | solution.py:104
  22.8 13.5 %collective-permute-start.4 = (bf16[1,4,16,2048]{3,2,1,0:T(8,128)(2,1)S(1)}, bf16[1,4,16,2048]{3,2,1,0:T(8,128)(2,1)S(1)}, u32[]{:S(2)}, u32[]{:S(2)}) collective-permute-start(bf16[1,4,16,2048]{3,2,1,0:T(8,128)(2,1)S(1)} %get-tuple-element.195), channel_id=1, source_target_pairs={{0,16},{2,18},{4,20},{6,22},{8,24},{10,26},{12,28},{14,30},{16,0},... | collective-permute-start | bytes 786440 | tf_op jit(solution)/shard_map/ppermute | solution.py:83
  26.9 13.3 %collective-permute-start.15 = (bf16[16,16,768]{2,1,0:T(8,128)(2,1)S(1)}, bf16[16,16,768]{2,1,0:T(8,128)(2,1)S(1)}, u32[]{:S(2)}, u32[]{:S(2)}) collective-permute-start(bf16[16,16,768]{2,1,0:T(8,128)(2,1)S(1)} %pad_maximum_fusion.4.refs_12_), channel_id=1, source_target_pairs={{0,1},{1,0},{2,3},{3,2},{4,5},{5,4},{6,7},{7,6},{8,9},{9,8},{10,11... | collective-permute-start | bytes 1179656 | tf_op jit(solution)/shard_map/ppermute | solution.py:111
  27.0 10.2 %collective-permute-start.9 = (bf16[4,16,2560]{2,1,0:T(8,128)(2,1)S(1)}, bf16[4,16,2560]{2,1,0:T(8,128)(2,1)S(1)}, u32[]{:S(2)}, u32[]{:S(2)}) collective-permute-start(bf16[4,16,2560]{2,1,0:T(8,128)(2,1)S(1)} %slice.72.refs_6_), channel_id=1, source_target_pairs={{0,4},{2,6},{4,0},{6,2},{8,12},{10,14},{12,8},{14,10},{16,20},{18,... | collective-permute-start | bytes 983048 | tf_op jit(solution)/shard_map/ppermute | solution.py:120
  28.6 10.0 %collective-permute-start.8 = (bf16[4,16,2560]{2,1,0:T(8,128)(2,1)S(1)}, bf16[4,16,2560]{2,1,0:T(8,128)(2,1)S(1)}, u32[]{:S(2)}, u32[]{:S(2)}) collective-permute-start(bf16[4,16,2560]{2,1,0:T(8,128)(2,1)S(1)} %slice.72.refs_6_), channel_id=1, source_target_pairs={{0,2},{2,0},{4,6},{6,4},{8,10},{10,8},{12,14},{14,12},{16,18},{18,... | collective-permute-start | bytes 983048 | tf_op jit(solution)/shard_map/ppermute | solution.py:119
  36.3 13.0 %collective-permute-start.5 = (bf16[2,4,16,2048]{3,2,1,0:T(8,128)(2,1)S(1)}, bf16[2,4,16,2048]{3,2,1,0:T(8,128)(2,1)S(1)}, u32[]{:S(2)}, u32[]{:S(2)}) collective-permute-start(bf16[2,4,16,2048]{3,2,1,0:T(8,128)(2,1)S(1)} %get-tuple-element.191), channel_id=1, source_target_pairs={{0,8},{2,10},{4,12},{6,14},{8,0},{10,2},{12,4},{14,6},{16,24},{18,... | collective-permute-start | bytes 1572872 | tf_op jit(solution)/shard_map/ppermute | solution.py:83
  37.2 9.4 %collective-permute-start.10 = (bf16[2,16,2560]{2,1,0:T(8,128)(2,1)S(1)}, bf16[2,16,2560]{2,1,0:T(8,128)(2,1)S(1)}, u32[]{:S(2)}, u32[]{:S(2)}) collective-permute-start(bf16[2,16,2560]{2,1,0:T(8,128)(2,1)S(1)} %slice.96), channel_id=1, source_target_pairs={{0,2},{2,0},{4,6},{6,4},{8,10},{10,8},{12,14},{14,12},{16,18},{18,... | collective-permute-start | bytes 491528 | tf_op jit(solution)/shard_map/ppermute | solution.py:125
  38.7 7.9 %collective-permute-start.11 = (bf16[2,16,2560]{2,1,0:T(8,128)(2,1)S(1)}, bf16[2,16,2560]{2,1,0:T(8,128)(2,1)S(1)}, u32[]{:S(2)}, u32[]{:S(2)}) collective-permute-start(bf16[2,16,2560]{2,1,0:T(8,128)(2,1)S(1)} %slice.97), channel_id=1, source_target_pairs={{0,4},{2,6},{4,0},{6,2},{8,12},{10,14},{12,8},{14,10},{16,20},{18,... | collective-permute-start | bytes 491528 | tf_op jit(solution)/shard_map/ppermute | solution.py:126
  49.5 7.9 %collective-permute-start.20 = (bf16[16,16,2048]{2,1,0:T(8,128)(2,1)S(1)}, bf16[16,16,2048]{2,1,0:T(8,128)(2,1)S(1)}, u32[]{:S(2)}, u32[]{:S(2)}) collective-permute-start(bf16[16,16,2048]{2,1,0:T(8,128)(2,1)S(1)} %bitcast.64), channel_id=1, source_target_pairs={{0,1},{1,0},{2,3},{3,2},{4,5},{5,4},{6,7},{7,6},{8,9},{9,8},{10,11... | collective-permute-start | bytes 3145736 | tf_op jit(solution)/shard_map/ppermute | solution.py:111
  63.6 10.5 %collective-permute-start.22 = (bf16[16,16,2048]{2,1,0:T(8,128)(2,1)S(1)}, bf16[16,16,2048]{2,1,0:T(8,128)(2,1)S(1)}, u32[]{:S(2)}, u32[]{:S(2)}) collective-permute-start(bf16[16,16,2048]{2,1,0:T(8,128)(2,1)S(1)} %get-tuple-element.134), channel_id=1, source_target_pairs={{0,1},{1,0},{2,3},{3,2},{4,5},{5,4},{6,7},{7,6},{8,9},{9,8},{10,11... | collective-permute-start | bytes 3145736 | tf_op jit(solution)/shard_map/ppermute | solution.py:166
  64.3 12.7 %collective-permute-start.27 = (bf16[4,16,2048]{2,1,0:T(8,128)(2,1)S(1)}, bf16[4,16,2048]{2,1,0:T(8,128)(2,1)S(1)}, u32[]{:S(2)}, u32[]{:S(2)}) collective-permute-start(bf16[4,16,2048]{2,1,0:T(8,128)(2,1)S(1)} %get-tuple-element.182), channel_id=1, source_target_pairs={{0,6},{2,4},{4,2},{6,0},{8,14},{10,12},{12,10},{14,8},{16,22},{18,... | collective-permute-start | bytes 786440 | tf_op jit(solution)/shard_map/ppermute | solution.py:175
  66.7 18.6 %collective-permute-start.26 = (bf16[4,16,2048]{2,1,0:T(8,128)(2,1)S(1)}, bf16[4,16,2048]{2,1,0:T(8,128)(2,1)S(1)}, u32[]{:S(2)}, u32[]{:S(2)}) collective-permute-start(bf16[4,16,2048]{2,1,0:T(8,128)(2,1)S(1)} %get-tuple-element.183), channel_id=1, source_target_pairs={{0,4},{2,6},{4,0},{6,2},{8,12},{10,14},{12,8},{14,10},{16,20},{18,... | collective-permute-start | bytes 786440 | tf_op jit(solution)/shard_map/ppermute | solution.py:175
  67.2 18.1 %collective-permute-start.25 = (bf16[4,16,2048]{2,1,0:T(8,128)(2,1)S(1)}, bf16[4,16,2048]{2,1,0:T(8,128)(2,1)S(1)}, u32[]{:S(2)}, u32[]{:S(2)}) collective-permute-start(bf16[4,16,2048]{2,1,0:T(8,128)(2,1)S(1)} %get-tuple-element.184), channel_id=1, source_target_pairs={{0,2},{2,0},{4,6},{6,4},{8,10},{10,8},{12,14},{14,12},{16,18},{18,... | collective-permute-start | bytes 786440 | tf_op jit(solution)/shard_map/ppermute | solution.py:175
  74.6 13.6 %collective-permute-start.30 = (bf16[4,16,2048]{2,1,0:T(8,128)(2,1)S(1)}, bf16[4,16,2048]{2,1,0:T(8,128)(2,1)S(1)}, u32[]{:S(2)}, u32[]{:S(2)}) collective-permute-start(bf16[4,16,2048]{2,1,0:T(8,128)(2,1)S(1)} %get-tuple-element.178), channel_id=1, source_target_pairs={{0,6},{2,4},{4,2},{6,0},{8,14},{10,12},{12,10},{14,8},{16,22},{18,... | collective-permute-start | bytes 786440 | tf_op jit(solution)/shard_map/ppermute | solution.py:175
  77.0 13.8 %collective-permute-start.29 = (bf16[4,16,2048]{2,1,0:T(8,128)(2,1)S(1)}, bf16[4,16,2048]{2,1,0:T(8,128)(2,1)S(1)}, u32[]{:S(2)}, u32[]{:S(2)}) collective-permute-start(bf16[4,16,2048]{2,1,0:T(8,128)(2,1)S(1)} %get-tuple-element.179), channel_id=1, source_target_pairs={{0,4},{2,6},{4,0},{6,2},{8,12},{10,14},{12,8},{14,10},{16,20},{18,... | collective-permute-start | bytes 786440 | tf_op jit(solution)/shard_map/ppermute | solution.py:175
  77.5 13.4 %collective-permute-start.28 = (bf16[4,16,2048]{2,1,0:T(8,128)(2,1)S(1)}, bf16[4,16,2048]{2,1,0:T(8,128)(2,1)S(1)}, u32[]{:S(2)}, u32[]{:S(2)}) collective-permute-start(bf16[4,16,2048]{2,1,0:T(8,128)(2,1)S(1)} %get-tuple-element.180), channel_id=1, source_target_pairs={{0,2},{2,0},{4,6},{6,4},{8,10},{10,8},{12,14},{14,12},{16,18},{18,... | collective-permute-start | bytes 786440 | tf_op jit(solution)/shard_map/ppermute | solution.py:175
  85.4 7.5 %collective-permute-start.24 = (bf16[16,16,1280]{2,1,0:T(8,128)(2,1)S(1)}, bf16[16,16,1280]{2,1,0:T(8,128)(2,1)S(1)}, u32[]{:S(2)}, u32[]{:S(2)}) collective-permute-start(bf16[16,16,1280]{2,1,0:T(8,128)(2,1)S(1)} %get-tuple-element.149), channel_id=1, source_target_pairs={{0,1},{1,0},{2,3},{3,2},{4,5},{5,4},{6,7},{7,6},{8,9},{9,8},{10,11... | collective-permute-start | bytes 1966088 | tf_op jit(solution)/shard_map/ppermute | solution.py:166
  91.3 8.5 %collective-permute-start.31 = (bf16[2,16,4096]{2,1,0:T(8,128)(2,1)S(1)}, bf16[2,16,4096]{2,1,0:T(8,128)(2,1)S(1)}, u32[]{:S(2)}, u32[]{:S(2)}) collective-permute-start(bf16[2,16,4096]{2,1,0:T(8,128)(2,1)S(1)} %slice_bitcast_fusion), channel_id=1, source_target_pairs={{0,8},{2,10},{4,12},{6,14},{8,0},{10,2},{12,4},{14,6},{16,24},{18,... | collective-permute-start | bytes 786440 | tf_op jit(solution)/shard_map/ppermute | solution.py:83
  93.1 10.2 %collective-permute-start.35 = (bf16[4,16,1280]{2,1,0:T(8,128)(2,1)S(1)}, bf16[4,16,1280]{2,1,0:T(8,128)(2,1)S(1)}, u32[]{:S(2)}, u32[]{:S(2)}) collective-permute-start(bf16[4,16,1280]{2,1,0:T(8,128)(2,1)S(1)} %get-tuple-element.186), channel_id=1, source_target_pairs={{0,6},{2,4},{4,2},{6,0},{8,14},{10,12},{12,10},{14,8},{16,22},{18,... | collective-permute-start | bytes 491528 | tf_op jit(solution)/shard_map/ppermute | solution.py:175
  94.8 8.6 %collective-permute-start.34 = (bf16[4,16,1280]{2,1,0:T(8,128)(2,1)S(1)}, bf16[4,16,1280]{2,1,0:T(8,128)(2,1)S(1)}, u32[]{:S(2)}, u32[]{:S(2)}) collective-permute-start(bf16[4,16,1280]{2,1,0:T(8,128)(2,1)S(1)} %get-tuple-element.187), channel_id=1, source_target_pairs={{0,4},{2,6},{4,0},{6,2},{8,12},{10,14},{12,8},{14,10},{16,20},{18,... | collective-permute-start | bytes 491528 | tf_op jit(solution)/shard_map/ppermute | solution.py:175
  96.1 7.3 %collective-permute-start.33 = (bf16[4,16,1280]{2,1,0:T(8,128)(2,1)S(1)}, bf16[4,16,1280]{2,1,0:T(8,128)(2,1)S(1)}, u32[]{:S(2)}, u32[]{:S(2)}) collective-permute-start(bf16[4,16,1280]{2,1,0:T(8,128)(2,1)S(1)} %get-tuple-element.188), channel_id=1, source_target_pairs={{0,2},{2,0},{4,6},{6,4},{8,10},{10,8},{12,14},{14,12},{16,18},{18,... | collective-permute-start | bytes 491528 | tf_op jit(solution)/shard_map/ppermute | solution.py:175
  99.9 10.2 %collective-permute-start.32 = (bf16[1,16,4096]{2,1,0:T(8,128)(2,1)S(1)}, bf16[1,16,4096]{2,1,0:T(8,128)(2,1)S(1)}, u32[]{:S(2)}, u32[]{:S(2)}) collective-permute-start(bf16[1,16,4096]{2,1,0:T(8,128)(2,1)S(1)} %get-tuple-element.192), channel_id=1, source_target_pairs={{0,16},{2,18},{4,20},{6,22},{8,24},{10,26},{12,28},{14,30},{16,0},... | collective-permute-start | bytes 393224 | tf_op jit(solution)/shard_map/ppermute | solution.py:83
  (25 other events, 275.4 us)
